TPU v7x, 32 devices: a whole 2x2x4 slice. The times are simulated.
32 devices in a mesh: row: 8 (over z, core), chan: 4 (over y, x).
Axes of the slice: x: 2, y: 2, z: 4, core: 2. Of those that a mesh axis runs over, the one named last changes fastest.
Arguments:
- image: bfloat16 [4, 64, 64, 512], P(None, 'row', None, 'chan'), may hold values from -31 to 31
- target: bfloat16 [4, 64, 64, 512], P(None, 'row', None, 'chan'), may hold values from -6 to 6
- time_index: int32 [4], replicated, may hold values from 0 to 999
- loss_weight: float32 [4], replicated, may hold values from 0.5 to 2
- clip_embed: bfloat16 [4, 2048], replicated, may hold values from -6 to 6
- clip_tokens: bfloat16 [4, 4, 2048], replicated, may hold values from -6 to 6
- norm_gain: float32 [3, 512], P(None, 'chan'), may hold values from 0.5 to 1.5
- norm_bias: float32 [3, 512], P(None, 'chan'), may hold values from -3 to 3
- conv1_w: bfloat16 [3, 3, 512, 512], P(None, None, 'chan'), may hold values from -0.09375 to 0.09375
- conv2_w: bfloat16 [3, 3, 512, 512], P(None, None, 'chan'), may hold values from -0.09375 to 0.09375
- conv_bias: float32 [2, 512], P(None, 'chan'), may hold values from -3 to 3
- emb_w: bfloat16 [2, 512, 2048], P(None, 'chan'), may hold values from -0.125 to 0.125
- emb_b: float32 [2, 512], P(None, 'chan'), may hold values from -3 to 3
- qkv_w: bfloat16 [3, 512, 512], P(None, 'chan'), may hold values from -0.25 to 0.25
- qv_bias: float32 [2, 512], P(None, 'chan'), may hold values from -3 to 3
- ctx_w: bfloat16 [2, 512, 2048], P(None, 'chan'), may hold values from -0.125 to 0.125
- ctx_b: float32 [2, 512], P(None, 'chan'), may hold values from -3 to 3
- out_w: bfloat16 [512, 512], P('chan'), may hold values from -6 to 6
- out_b: float32 [512], P('chan'), may hold values from -3 to 3
Outputs:
- output: float32 [4, 64, 64, 512], P(None, 'row', None, 'chan')
- grad_image: float32 [4, 64, 64, 512], P(None, 'row', None, 'chan')
- grad_norm_gain: float32 [3, 512], P(None, 'chan')
- grad_norm_bias: float32 [3, 512], P(None, 'chan')
- grad_conv1_w: float32 [3, 3, 512, 512], P(None, None, 'chan')
- grad_conv2_w: float32 [3, 3, 512, 512], P(None, None, 'chan')
- grad_conv_bias: float32 [2, 512], P(None, 'chan')
- grad_emb_w: float32 [2, 512, 2048], P(None, 'chan')
- grad_emb_b: float32 [2, 512], P(None, 'chan')
- grad_qkv_w: float32 [3, 512, 512], P(None, 'chan')
- grad_qv_bias: float32 [2, 512], P(None, 'chan')
- grad_ctx_w: float32 [2, 512, 2048], P(None, 'chan')
- grad_ctx_b: float32 [2, 512], P(None, 'chan')
- grad_out_w: float32 [512, 512], P('chan')
- grad_out_b: float32 [512], P('chan')
All inputs are finite; a program needn't handle non-finite values.
Results may differ from a plain program's by a relative error of at most 0.018.
Values may be sent and summed in bfloat16 or wider, within the bound.
A program may use at most 192 MiB of HBM per device.

v0:
```python
import math

import jax
import jax.numpy as jnp
from jax import lax
from jax.sharding import PartitionSpec as P

C = 512
GROUPS = 32
HEAD = 64
EMB = 2048
CTXW = 2048
CTX = 4
H = 64
W = 64
MB_IMG = 2


HIGH = lax.Precision.HIGHEST
EPSILON = 1e-05


def with_halo(cells, sides, width):
    for axis, dim in sides:
        count = lax.axis_size(axis)
        ends = count - 1
        head = lax.slice_in_dim(cells, 0, width, axis=dim)
        tail = lax.slice_in_dim(cells, cells.shape[dim] - width, cells.shape[dim], axis=dim)
        cells = jnp.concatenate(
            [
                lax.ppermute(tail, axis, [(i, (i + 1) % count) for i in range(ends)]),
                cells,
                lax.ppermute(head, axis, [((i + 1) % count, i) for i in range(ends)]),
            ],
            axis=dim,
        )
    return cells


def swish(source):
    return source * jax.nn.sigmoid(source)


def swish_slope(source):
    sigma = jax.nn.sigmoid(source)
    return sigma * (1.0 + source * (1.0 - sigma))


def time_features(time_index, width_all):
    half_width = width_all // 2
    frequency = jnp.exp(-math.log(10000.0) * jnp.arange(half_width, dtype=jnp.float32) / half_width)
    angles = time_index.astype(jnp.float32)[:, None] * frequency[None, :]
    return jnp.concatenate([jnp.cos(angles), jnp.sin(angles)], axis=1)


def rows_around(source):
    return with_halo(source, (("row", 1),), 1)


def all_channels(source):
    return lax.all_gather(source, "chan", axis=3, tiled=True)


def channel_total(source):
    return lax.psum_scatter(
        source.astype(jnp.bfloat16), "chan", scatter_dimension=3, tiled=True
    ).astype(jnp.float32)


def norm_forward(source, group_width, members):
    layout = source.shape
    grouped = source.reshape(layout[0], layout[1], layout[2], layout[3] // group_width, group_width)
    first_sum = jnp.sum(grouped, axis=(1, 2, 4))
    square_sum = jnp.sum(grouped * grouped, axis=(1, 2, 4))
    first_sum, square_sum = lax.psum((first_sum, square_sum), "row")
    center = first_sum / members
    spread = square_sum / members - center * center
    inverse_std = lax.rsqrt(spread + EPSILON)
    scaled = (grouped - center[:, None, None, :, None]) * inverse_std[:, None, None, :, None]
    return (scaled.reshape(layout), inverse_std)


def norm_backward(upstream, scaled, inverse_std, gain, group_width, members):
    layout = upstream.shape
    grouped_grad = (upstream * gain).reshape(
        layout[0], layout[1], layout[2], layout[3] // group_width, group_width
    )
    grouped_norm = scaled.reshape(grouped_grad.shape)
    grad_sum = jnp.sum(grouped_grad, axis=(1, 2, 4))
    cross_sum = jnp.sum(grouped_grad * grouped_norm, axis=(1, 2, 4))
    grad_sum, cross_sum = lax.psum((grad_sum, cross_sum), "row")
    result = inverse_std[:, None, None, :, None] * (
        grouped_grad
        - grad_sum[:, None, None, :, None] / members
        - grouped_norm * (cross_sum[:, None, None, :, None] / members)
    )
    gain_grad = jnp.sum(upstream * scaled, axis=(0, 1, 2))
    bias_grad = jnp.sum(upstream, axis=(0, 1, 2))
    return (result.reshape(layout), gain_grad, bias_grad)


def conv_apply(padded, weight):
    height = padded.shape[1] - 2
    width = padded.shape[2]
    widened = jnp.pad(padded, ((0, 0), (0, 0), (1, 1), (0, 0)))
    result = None
    for row_step in range(3):
        for col_step in range(3):
            partial_term = jnp.einsum(
                "nhwc,dc->nhwd",
                widened[:, row_step : row_step + height, col_step : col_step + width],
                weight[row_step, col_step],
                preferred_element_type=jnp.float32,
            )
            result = partial_term if result is None else result + partial_term
    return result


def conv_weight_grad(padded, upstream_low):
    height = upstream_low.shape[1]
    width = upstream_low.shape[2]
    widened = jnp.pad(padded, ((0, 0), (0, 0), (1, 1), (0, 0)))
    stacked = []
    for row_step in range(3):
        row_terms = []
        for col_step in range(3):
            row_terms.append(
                jnp.einsum(
                    "nhwc,nhwd->dc",
                    widened[:, row_step : row_step + height, col_step : col_step + width],
                    upstream_low,
                    preferred_element_type=jnp.float32,
                )
            )
        stacked.append(jnp.stack(row_terms))
    return jnp.stack(stacked)


def conv_input_grad(upstream_low, weight):
    height = upstream_low.shape[1]
    width = upstream_low.shape[2]
    widened = jnp.pad(rows_around(upstream_low), ((0, 0), (0, 0), (1, 1), (0, 0)))
    result = None
    for row_step in range(3):
        for col_step in range(3):
            partial_term = jnp.einsum(
                "nhwd,dc->nhwc",
                widened[
                    :, 2 - row_step : 2 - row_step + height, 2 - col_step : 2 - col_step + width
                ],
                weight[row_step, col_step],
                preferred_element_type=jnp.float32,
            )
            result = partial_term if result is None else result + partial_term
    return channel_total(result)


def body(
    image,
    target,
    time_index,
    loss_weight,
    clip_embed,
    clip_tokens,
    norm_gain,
    norm_bias,
    conv1_w,
    conv2_w,
    conv_bias,
    emb_w,
    emb_b,
    qkv_w,
    qv_bias,
    ctx_w,
    ctx_b,
    out_w,
    out_b,
):
    local_chan = conv1_w.shape[2]
    group_width = C // GROUPS
    members = H * W * group_width
    head_count = local_chan // HEAD
    scaling = HEAD ** (-0.5)
    batches = image.shape[0] // MB_IMG
    band_rows = image.shape[1]
    image_cols = image.shape[2]

    def heads_of(source):
        return source.reshape(source.shape[0], -1, head_count, HEAD)

    def one_batch(carry, items):
        picture, target_in, steps_in, weight_in, embed_in, tokens_in = items
        feat_low = swish(time_features(steps_in, EMB) + embed_in.astype(jnp.float32)).astype(
            jnp.bfloat16
        )
        cond = (
            jnp.einsum("ne,jde->njd", feat_low, emb_w, preferred_element_type=jnp.float32) + emb_b
        )
        scale_term = cond[:, 0][:, None, None, :]
        shift_term = cond[:, 1][:, None, None, :]
        picture_f = picture.astype(jnp.float32)
        scaled_one, inverse_one = norm_forward(picture_f, group_width, members)
        pre_one = scaled_one * norm_gain[0] + norm_bias[0]
        padded_one = all_channels(rows_around(swish(pre_one).astype(jnp.bfloat16)))
        hidden = conv_apply(padded_one, conv1_w) + conv_bias[0]
        scaled_two, inverse_two = norm_forward(hidden, group_width, members)
        normal_two = scaled_two * norm_gain[1] + norm_bias[1]
        modded = normal_two * (1.0 + scale_term) + shift_term
        padded_two = all_channels(rows_around(swish(modded).astype(jnp.bfloat16)))
        resid = picture_f + conv_apply(padded_two, conv2_w) + conv_bias[1]
        scaled_three, inverse_three = norm_forward(resid, group_width, members)
        normed_full = all_channels(
            (scaled_three * norm_gain[2] + norm_bias[2]).astype(jnp.bfloat16)
        )
        projected = jnp.einsum(
            "nhwc,tdc->nhwtd", normed_full, qkv_w, preferred_element_type=jnp.float32
        )
        query_own = heads_of((projected[..., 0, :] + qv_bias[0]).astype(jnp.bfloat16))
        key_own = heads_of(projected[..., 1, :].astype(jnp.bfloat16))
        value_own = heads_of((projected[..., 2, :] + qv_bias[1]).astype(jnp.bfloat16))
        context = (
            jnp.einsum("nte,jde->ntjd", tokens_in, ctx_w, preferred_element_type=jnp.float32)
            + ctx_b
        )
        ctx_key = heads_of(context[:, :, 0].astype(jnp.bfloat16))
        ctx_value = heads_of(context[:, :, 1].astype(jnp.bfloat16))
        key_rows, value_rows = (
            lax.all_gather(key_own, "row", axis=1, tiled=True),
            lax.all_gather(value_own, "row", axis=1, tiled=True),
        )
        score_image = (
            jnp.einsum("nqhd,nkhd->nhqk", query_own, key_rows, preferred_element_type=jnp.float32)
            * scaling
        )
        score_context = (
            jnp.einsum("nqhd,nkhd->nhqk", query_own, ctx_key, preferred_element_type=jnp.float32)
            * scaling
        )
        top_score = jnp.maximum(jnp.max(score_image, axis=3), jnp.max(score_context, axis=3))
        expo_image = jnp.exp(score_image - top_score[..., None])
        expo_context = jnp.exp(score_context - top_score[..., None])
        denom = jnp.sum(expo_image, axis=3) + jnp.sum(expo_context, axis=3)
        prob_image = expo_image / denom[..., None]
        prob_context = expo_context / denom[..., None]
        attended = jnp.einsum(
            "nhqk,nkhd->nqhd",
            prob_image.astype(jnp.bfloat16),
            value_rows,
            preferred_element_type=jnp.float32,
        ) + jnp.einsum(
            "nhqk,nkhd->nqhd",
            prob_context.astype(jnp.bfloat16),
            ctx_value,
            preferred_element_type=jnp.float32,
        )
        attn_full = all_channels(attended.astype(jnp.bfloat16).reshape(picture.shape))
        result = (
            resid
            + jnp.einsum("nhwc,dc->nhwd", attn_full, out_w, preferred_element_type=jnp.float32)
            + out_b
        )
        cotangent = weight_in[:, None, None, None] * (result - target_in.astype(jnp.float32))
        grad_proj = cotangent.astype(jnp.bfloat16)
        grad_outw = jnp.einsum(
            "nhwc,nhwd->dc", attn_full, grad_proj, preferred_element_type=jnp.float32
        )
        grad_outb = jnp.sum(grad_proj.astype(jnp.float32), axis=(0, 1, 2))
        grad_attn = heads_of(
            channel_total(
                jnp.einsum("nhwd,dc->nhwc", grad_proj, out_w, preferred_element_type=jnp.float32)
            ).astype(jnp.bfloat16)
        )
        dprob_image = jnp.einsum(
            "nqhd,nkhd->nhqk", grad_attn, value_rows, preferred_element_type=jnp.float32
        )
        dprob_context = jnp.einsum(
            "nqhd,nkhd->nhqk", grad_attn, ctx_value, preferred_element_type=jnp.float32
        )
        delta = jnp.sum(prob_image * dprob_image, axis=3) + jnp.sum(
            prob_context * dprob_context, axis=3
        )
        dscore_image = (prob_image * (dprob_image - delta[..., None])).astype(jnp.bfloat16)
        dscore_context = (prob_context * (dprob_context - delta[..., None])).astype(jnp.bfloat16)
        grad_query = (
            jnp.einsum(
                "nhqk,nkhd->nqhd", dscore_image, key_rows, preferred_element_type=jnp.float32
            )
            + jnp.einsum(
                "nhqk,nkhd->nqhd", dscore_context, ctx_key, preferred_element_type=jnp.float32
            )
        ) * scaling
        grad_ctx_key = (
            jnp.einsum(
                "nhqk,nqhd->nkhd", dscore_context, query_own, preferred_element_type=jnp.float32
            )
            * scaling
        )
        grad_ctx_value = jnp.einsum(
            "nhqk,nqhd->nkhd",
            prob_context.astype(jnp.bfloat16),
            grad_attn,
            preferred_element_type=jnp.float32,
        )
        key_terms = (
            jnp.einsum(
                "nhqk,nqhd->nkhd", dscore_image, query_own, preferred_element_type=jnp.float32
            )
            * scaling
        )
        value_terms = jnp.einsum(
            "nhqk,nqhd->nkhd",
            prob_image.astype(jnp.bfloat16),
            grad_attn,
            preferred_element_type=jnp.float32,
        )
        grad_key, grad_value = (
            lax.psum_scatter(
                key_terms.astype(jnp.bfloat16), "row", scatter_dimension=1, tiled=True
            ).astype(jnp.float32),
            lax.psum_scatter(
                value_terms.astype(jnp.bfloat16), "row", scatter_dimension=1, tiled=True
            ).astype(jnp.float32),
        )
        grad_stack = (
            jnp.stack([grad_query, grad_key, grad_value], axis=2)
            .reshape(picture.shape[0], band_rows, image_cols, 3, local_chan)
            .astype(jnp.bfloat16)
        )
        grad_qkvw = jnp.einsum(
            "nhwc,nhwtd->tdc", normed_full, grad_stack, preferred_element_type=jnp.float32
        )
        stack_sums = jnp.sum(grad_stack.astype(jnp.float32), axis=(0, 1, 2))
        grad_qvb = jnp.stack([stack_sums[0], stack_sums[2]])
        grad_context = jnp.stack(
            [
                grad_ctx_key.reshape(picture.shape[0], CTX, local_chan),
                grad_ctx_value.reshape(picture.shape[0], CTX, local_chan),
            ],
            axis=2,
        )
        grad_ctxw = jnp.einsum(
            "nte,ntjd->jde", tokens_in.astype(jnp.float32), grad_context, precision=HIGH
        )
        grad_ctxb = jnp.sum(grad_context, axis=(0, 1))
        grad_normed = channel_total(
            jnp.einsum("nhwtd,tdc->nhwc", grad_stack, qkv_w, preferred_element_type=jnp.float32)
        )
        grad_resid, gain_three, bias_three = norm_backward(
            grad_normed, scaled_three, inverse_three, norm_gain[2], group_width, members
        )
        grad_resid = cotangent + grad_resid
        grad_conv_two = grad_resid.astype(jnp.bfloat16)
        grad_w_two = conv_weight_grad(padded_two, grad_conv_two)
        grad_b_two = jnp.sum(grad_conv_two.astype(jnp.float32), axis=(0, 1, 2))
        grad_modded = conv_input_grad(grad_conv_two, conv2_w) * swish_slope(modded)
        grad_cond = jnp.stack(
            [jnp.sum(grad_modded * normal_two, axis=(1, 2)), jnp.sum(grad_modded, axis=(1, 2))],
            axis=1,
        )
        grad_embw = jnp.einsum(
            "ne,njd->jde", feat_low.astype(jnp.float32), grad_cond, precision=HIGH
        )
        grad_embb = jnp.sum(grad_cond, axis=0)
        grad_hidden, gain_two, bias_two = norm_backward(
            grad_modded * (1.0 + scale_term),
            scaled_two,
            inverse_two,
            norm_gain[1],
            group_width,
            members,
        )
        grad_conv_one = grad_hidden.astype(jnp.bfloat16)
        grad_w_one = conv_weight_grad(padded_one, grad_conv_one)
        grad_b_one = jnp.sum(grad_conv_one.astype(jnp.float32), axis=(0, 1, 2))
        grad_pre_one = conv_input_grad(grad_conv_one, conv1_w) * swish_slope(pre_one)
        grad_input, gain_one, bias_one = norm_backward(
            grad_pre_one, scaled_one, inverse_one, norm_gain[0], group_width, members
        )
        grad_picture = grad_resid + grad_input
        grad_gains = jnp.stack([gain_one, gain_two, gain_three])
        grad_biases = jnp.stack([bias_one, bias_two, bias_three])
        grad_convb = jnp.stack([grad_b_one, grad_b_two])
        batch_grads = (
            grad_gains,
            grad_biases,
            grad_w_one,
            grad_w_two,
            grad_convb,
            grad_embw,
            grad_embb,
            grad_qkvw,
            grad_qvb,
            grad_ctxw,
            grad_ctxb,
            grad_outw,
            grad_outb,
        )
        updated = tuple((running + update for running, update in zip(carry, batch_grads)))
        return (updated, (result, grad_picture))

    start = (
        jnp.zeros(norm_gain.shape, jnp.float32),
        jnp.zeros(norm_bias.shape, jnp.float32),
        jnp.zeros(conv1_w.shape, jnp.float32),
        jnp.zeros(conv2_w.shape, jnp.float32),
        jnp.zeros(conv_bias.shape, jnp.float32),
        jnp.zeros(emb_w.shape, jnp.float32),
        jnp.zeros(emb_b.shape, jnp.float32),
        jnp.zeros(qkv_w.shape, jnp.float32),
        jnp.zeros(qv_bias.shape, jnp.float32),
        jnp.zeros(ctx_w.shape, jnp.float32),
        jnp.zeros(ctx_b.shape, jnp.float32),
        jnp.zeros(out_w.shape, jnp.float32),
        jnp.zeros(out_b.shape, jnp.float32),
    )
    items = (
        image.reshape(batches, MB_IMG, band_rows, image_cols, local_chan),
        target.reshape(batches, MB_IMG, band_rows, image_cols, local_chan),
        time_index.reshape(batches, MB_IMG),
        loss_weight.reshape(batches, MB_IMG),
        clip_embed.reshape(batches, MB_IMG, EMB),
        clip_tokens.reshape(batches, MB_IMG, CTX, CTXW),
    )
    totals, (results, picture_grads) = lax.scan(one_batch, start, items)
    (
        sum_gain,
        sum_bias,
        sum_conv_one,
        sum_conv_two,
        sum_conv_bias,
        sum_emb_w,
        sum_emb_b,
        sum_qkv_w,
        sum_qv_bias,
        sum_ctx_w,
        sum_ctx_b,
        sum_out_w,
        sum_out_b,
    ) = totals
    (
        sum_gain,
        sum_bias,
        sum_conv_one,
        sum_conv_two,
        sum_conv_bias,
        sum_emb_w,
        sum_emb_b,
        sum_qkv_w,
        sum_qv_bias,
        sum_ctx_w,
        sum_ctx_b,
        sum_out_w,
        sum_out_b,
    ) = (
        lax.psum(sum_gain.astype(jnp.bfloat16), "row").astype(jnp.float32),
        lax.psum(sum_bias.astype(jnp.bfloat16), "row").astype(jnp.float32),
        lax.psum(sum_conv_one.astype(jnp.bfloat16), "row").astype(jnp.float32),
        lax.psum(sum_conv_two.astype(jnp.bfloat16), "row").astype(jnp.float32),
        lax.psum(sum_conv_bias.astype(jnp.bfloat16), "row").astype(jnp.float32),
        lax.psum(sum_emb_w.astype(jnp.bfloat16), "row").astype(jnp.float32),
        lax.psum(sum_emb_b.astype(jnp.bfloat16), "row").astype(jnp.float32),
        lax.psum(sum_qkv_w.astype(jnp.bfloat16), "row").astype(jnp.float32),
        lax.psum(sum_qv_bias.astype(jnp.bfloat16), "row").astype(jnp.float32),
        lax.psum(sum_ctx_w.astype(jnp.bfloat16), "row").astype(jnp.float32),
        lax.psum(sum_ctx_b.astype(jnp.bfloat16), "row").astype(jnp.float32),
        lax.psum(sum_out_w.astype(jnp.bfloat16), "row").astype(jnp.float32),
        lax.psum(sum_out_b.astype(jnp.bfloat16), "row").astype(jnp.float32),
    )
    return (
        results.reshape(image.shape),
        picture_grads.reshape(image.shape),
        sum_gain,
        sum_bias,
        sum_conv_one,
        sum_conv_two,
        sum_conv_bias,
        sum_emb_w,
        sum_emb_b,
        sum_qkv_w,
        sum_qv_bias,
        sum_ctx_w,
        sum_ctx_b,
        sum_out_w,
        sum_out_b,
    )


def solution(mesh):
    return jax.shard_map(
        body,
        mesh=mesh,
        in_specs=(
            P(None, "row", None, "chan"),
            P(None, "row", None, "chan"),
            P(),
            P(),
            P(),
            P(),
            P(None, "chan"),
            P(None, "chan"),
            P(None, None, "chan", None),
            P(None, None, "chan", None),
            P(None, "chan"),
            P(None, "chan", None),
            P(None, "chan"),
            P(None, "chan", None),
            P(None, "chan"),
            P(None, "chan", None),
            P(None, "chan"),
            P("chan", None),
            P("chan"),
        ),
        out_specs=(
            P(None, "row", None, "chan"),
            P(None, "row", None, "chan"),
            P(None, "chan"),
            P(None, "chan"),
            P(None, None, "chan", None),
            P(None, None, "chan", None),
            P(None, "chan"),
            P(None, "chan", None),
            P(None, "chan"),
            P(None, "chan", None),
            P(None, "chan"),
            P(None, "chan", None),
            P(None, "chan"),
            P("chan", None),
            P("chan"),
        ),
        check_vma=False,
    )
```

profile of v0, /device:TPU:7, one launch (start us, length us, event | category | flops | bytes accessed | tf_op | source)
XLA Modules:
  0.0 1374.9 jit_solution(2033101402865231942)
XLA Ops:
  11.5 1221.2 %while.41 = (s32[]{:T(128)}, f32[3,128]{1,0:T(4,128)}, f32[3,128]{1,0:T(4,128)}, f32[3,3,128,512]{3,2,1,0:T(8,128)}, f32[3,3,128,512]{3,2,1,0:T(8,128)}, /*index...) while((s32[]{:T(128)}, f32[3,128]{1,0:T(4,128)}, ...), condition=%wide.region_63.64_spmd.clone, body=%wide.region_0.63_spmd.clone.sunk | while | flops 15635671040 | bytes 873531456 | solution.py:424
  43.0 23.4 %all-gather.7.cloned.1.call-done = bf16[2,10,64,512]{3,2,1,0:T(8,128)(2,1)} async-done(((bf16[2,10,64,128]{3,2,1,0:T(8,128)(2,1)}), bf16[2,10,64,512]{3,2,1,0:T(8,128)(2,1)}) %all-gather.7.cloned.1.call-update) | async-done | bytes 1310736 | tf_op jit(solution)/shard_map/while/body/eval_jaxpr/all_gather | solution.py:61
  96.0 27.3 %all-gather.9.cloned.1.call-done = bf16[2,10,64,512]{3,2,1,0:T(8,128)(2,1)} async-done(((bf16[2,10,64,128]{3,2,1,0:T(8,128)(2,1)}), bf16[2,10,64,512]{3,2,1,0:T(8,128)(2,1)}) %all-gather.9.cloned.1.call-update) | async-done | bytes 1310736 | tf_op jit(solution)/shard_map/while/body/eval_jaxpr/all_gather | solution.py:61
  144.1 26.6 %all-gather.11.cloned.1.call-done = bf16[2,8,64,512]{3,2,1,0:T(8,128)(2,1)} async-done(((bf16[2,8,64,128]{3,2,1,0:T(8,128)(2,1)}), bf16[2,8,64,512]{3,2,1,0:T(8,128)(2,1)}) %all-gather.11.cloned.1.call-update) | async-done | bytes 1048592 | tf_op jit(solution)/shard_map/while/body/eval_jaxpr/all_gather | solution.py:61
  179.9 24.6 %all-gather.15.cloned.1.call-done = bf16[2,4096,2,64]{1,3,2,0:T(8,128)(2,1)} async-done(((bf16[2,512,2,64]{1,3,2,0:T(8,128)(2,1)}), bf16[2,4096,2,64]{1,3,2,0:T(8,128)(2,1)}) %all-gather.15.cloned.1.call-update) | async-done | bytes 2097168 | tf_op jit(solution)/shard_map/while/body/eval_jaxpr/all_gather | solution.py:228
  250.5 24.7 %all-gather.17.cloned.1.call-done = bf16[2,8,64,512]{3,2,1,0:T(8,128)(2,1)} async-done(((bf16[2,8,64,128]{3,2,1,0:T(8,128)(2,1)}), bf16[2,8,64,512]{3,2,1,0:T(8,128)(2,1)}) %all-gather.17.cloned.1.call-update) | async-done | bytes 1048592 | tf_op jit(solution)/shard_map/while/body/eval_jaxpr/all_gather | solution.py:61
  284.9 27.2 %reduce-scatter.23.cloned.1.call-done = bf16[128,1024]{1,0:T(8,128)(2,1)} async-done(((bf16[512,1024]{1,0:T(8,128)(2,1)}), bf16[128,1024]{1,0:T(8,128)(2,1)}) %reduce-scatter.23.cloned.1.call-update) | async-done | bytes 262160 | tf_op jit(solution)/shard_map/while
  329.5 24.6 %multiply_reduce_fusion.16 = (f32[2,2,512]{2,1,0:T(2,128)S(1)}, f32[2,2,512,4096]{3,2,1,0:T(8,128)}) fusion(f32[2,2,512]{2,1,0:T(2,128)S(1)} %add.1104, f32[2,2,512]{2,1,0:T(2,128)S(1)} %max.12, f32[2,2,512,4096]{3,2,1,0:T(8,128)} %get-tuple-element.1140, bf16[2,4096,2,64]{1,3,2,0:T(8,128)(2,1)} %all-gather.13.cloned.1.call-done, ...), kind=kOutput, calls=%fused_computation.1.clone.1 | convolution fusion | flops 1115682816 | bytes 69492736 | tf_op jit(solution)/shard_map/while/body/eval_jaxpr/nqhd,nkhd->nhqk/dot_general | solution.py:273
  354.1 28.1 %multiply_convert_fusion.9 = bf16[2,2,512,4096]{3,2,1,0:T(8,128)(2,1)} fusion(f32[2,2,512,4096]{3,2,1,0:T(8,128)} %get-tuple-element.1147, f32[2,2,512]{2,1,0:T(2,128)S(1)} %add.1105, f32[2,2,512]{2,1,0:T(2,128)S(1)} %add.1104, f32[2,2,512]{2,1,0:T(2,128)S(1)} %max.12, f32[2,2,512,4096]{3,2,1,0:T(8,128)} %get-tuple-element.1140), kind=kLoop, calls=%fused_computation.clone.1 | loop fusion | flops 50331648 | bytes 83910656 | tf_op jit(solution)/shard_map/while/body/eval_jaxpr/convert_element_type | solution.py:282
  447.0 18.5 %reduce-scatter.29.cloned.1.call-done = bf16[128,1024]{1,0:T(8,128)(2,1)} async-done(((bf16[512,1024]{1,0:T(8,128)(2,1)}), bf16[128,1024]{1,0:T(8,128)(2,1)}) %reduce-scatter.29.cloned.1.call-update) | async-done | bytes 262160 | tf_op jit(solution)/shard_map/while
  511.3 16.7 %reduce-scatter.31.cloned.1.call-done = bf16[128,1024]{1,0:T(8,128)(2,1)} async-done(((bf16[512,1024]{1,0:T(8,128)(2,1)}), bf16[128,1024]{1,0:T(8,128)(2,1)}) %reduce-scatter.31.cloned.1.call-update) | async-done | bytes 262160 | tf_op jit(solution)/shard_map/while
  623.6 16.4 %all-reduce.18 = (f32[2,8]{1,0:T(2,128)S(1)}, f32[2,8]{1,0:T(2,128)S(1)}) all-reduce(f32[2,8]{1,0:T(2,128)S(1)} %reduce_sum.587, f32[2,8]{1,0:T(2,128)S(1)} %reduce_sum.589), channel_id=1, replica_groups=mesh['row'=8,'chan'=4] {'row'}, use_global_device_ids=true, to_apply=%region_6.6 | all-reduce | flops 32 | bytes 256 | tf_op jit(solution)/shard_map/while/body/eval_jaxpr/psum | solution.py:75
  652.8 23.6 %all-gather.7.cloned.1.call-done = bf16[2,10,64,512]{3,2,1,0:T(8,128)(2,1)} async-done(((bf16[2,10,64,128]{3,2,1,0:T(8,128)(2,1)}), bf16[2,10,64,512]{3,2,1,0:T(8,128)(2,1)}) %all-gather.7.cloned.1.call-update) | async-done | bytes 1310736 | tf_op jit(solution)/shard_map/while/body/eval_jaxpr/all_gather | solution.py:61
  706.0 27.3 %all-gather.9.cloned.1.call-done = bf16[2,10,64,512]{3,2,1,0:T(8,128)(2,1)} async-done(((bf16[2,10,64,128]{3,2,1,0:T(8,128)(2,1)}), bf16[2,10,64,512]{3,2,1,0:T(8,128)(2,1)}) %all-gather.9.cloned.1.call-update) | async-done | bytes 1310736 | tf_op jit(solution)/shard_map/while/body/eval_jaxpr/all_gather | solution.py:61
  754.0 26.6 %all-gather.11.cloned.1.call-done = bf16[2,8,64,512]{3,2,1,0:T(8,128)(2,1)} async-done(((bf16[2,8,64,128]{3,2,1,0:T(8,128)(2,1)}), bf16[2,8,64,512]{3,2,1,0:T(8,128)(2,1)}) %all-gather.11.cloned.1.call-update) | async-done | bytes 1048592 | tf_op jit(solution)/shard_map/while/body/eval_jaxpr/all_gather | solution.py:61
  789.7 24.7 %all-gather.15.cloned.1.call-done = bf16[2,4096,2,64]{1,3,2,0:T(8,128)(2,1)} async-done(((bf16[2,512,2,64]{1,3,2,0:T(8,128)(2,1)}), bf16[2,4096,2,64]{1,3,2,0:T(8,128)(2,1)}) %all-gather.15.cloned.1.call-update) | async-done | bytes 2097168 | tf_op jit(solution)/shard_map/while/body/eval_jaxpr/all_gather | solution.py:228
  860.4 24.8 %all-gather.17.cloned.1.call-done = bf16[2,8,64,512]{3,2,1,0:T(8,128)(2,1)} async-done(((bf16[2,8,64,128]{3,2,1,0:T(8,128)(2,1)}), bf16[2,8,64,512]{3,2,1,0:T(8,128)(2,1)}) %all-gather.17.cloned.1.call-update) | async-done | bytes 1048592 | tf_op jit(solution)/shard_map/while/body/eval_jaxpr/all_gather | solution.py:61
  894.7 27.4 %reduce-scatter.23.cloned.1.call-done = bf16[128,1024]{1,0:T(8,128)(2,1)} async-done(((bf16[512,1024]{1,0:T(8,128)(2,1)}), bf16[128,1024]{1,0:T(8,128)(2,1)}) %reduce-scatter.23.cloned.1.call-update) | async-done | bytes 262160 | tf_op jit(solution)/shard_map/while
  939.4 24.6 %multiply_reduce_fusion.16 = (f32[2,2,512]{2,1,0:T(2,128)S(1)}, f32[2,2,512,4096]{3,2,1,0:T(8,128)}) fusion(f32[2,2,512]{2,1,0:T(2,128)S(1)} %add.1104, f32[2,2,512]{2,1,0:T(2,128)S(1)} %max.12, f32[2,2,512,4096]{3,2,1,0:T(8,128)} %get-tuple-element.1140, bf16[2,4096,2,64]{1,3,2,0:T(8,128)(2,1)} %all-gather.13.cloned.1.call-done, ...), kind=kOutput, calls=%fused_computation.1.clone.1 | convolution fusion | flops 1115682816 | bytes 69492736 | tf_op jit(solution)/shard_map/while/body/eval_jaxpr/nqhd,nkhd->nhqk/dot_general | solution.py:273
  964.1 28.1 %multiply_convert_fusion.9 = bf16[2,2,512,4096]{3,2,1,0:T(8,128)(2,1)} fusion(f32[2,2,512,4096]{3,2,1,0:T(8,128)} %get-tuple-element.1147, f32[2,2,512]{2,1,0:T(2,128)S(1)} %add.1105, f32[2,2,512]{2,1,0:T(2,128)S(1)} %add.1104, f32[2,2,512]{2,1,0:T(2,128)S(1)} %max.12, f32[2,2,512,4096]{3,2,1,0:T(8,128)} %get-tuple-element.1140), kind=kLoop, calls=%fused_computation.clone.1 | loop fusion | flops 50331648 | bytes 83910656 | tf_op jit(solution)/shard_map/while/body/eval_jaxpr/convert_element_type | solution.py:282
  1060.0 15.6 %reduce-scatter.29.cloned.1.call-done = bf16[128,1024]{1,0:T(8,128)(2,1)} async-done(((bf16[512,1024]{1,0:T(8,128)(2,1)}), bf16[128,1024]{1,0:T(8,128)(2,1)}) %reduce-scatter.29.cloned.1.call-update) | async-done | bytes 262160 | tf_op jit(solution)/shard_map/while
  1121.3 16.7 %reduce-scatter.31.cloned.1.call-done = bf16[128,1024]{1,0:T(8,128)(2,1)} async-done(((bf16[512,1024]{1,0:T(8,128)(2,1)}), bf16[128,1024]{1,0:T(8,128)(2,1)}) %reduce-scatter.31.cloned.1.call-update) | async-done | bytes 262160 | tf_op jit(solution)/shard_map/while
  1244.3 17.0 %all-reduce.10 = (bf16[3,128]{1,0:T(4,128)(2,1)S(1)}, bf16[3,128]{1,0:T(4,128)(2,1)S(1)}, bf16[2,128]{1,0:T(2,128)(2,1)S(1)}, bf16[2,128]{1,0:T(2,128)(2,1)S(1)}...) all-reduce(bf16[3,128]{1,0:T(4,128)(2,1)S(1)} %convert_element_type, ...), channel_id=1, replica_groups=mesh['row'=8,'chan'=4] {'row'}, use_global_device_ids=true, to_apply=%region_64.65 | all-reduce | flops 1920 | bytes 7680 | tf_op jit(solution)/shard_map/psum | solution.py:455
  1265.2 92.4 %all-reduce.26.cloned.1.call-done = (bf16[3,3,128,512]{3,2,1,0:T(8,128)(2,1)}, bf16[3,3,128,512]{3,2,1,0:T(8,128)(2,1)}, bf16[2,128,2048]{2,1,0:T(8,128)(2,1)}, ...) async-done(((bf16[3,3,128,512]{3,2,1,0:T(8,128)(2,1)}, bf16[3,3,128,512]{3,2,1,0:T(8,128)(2,1)}, ...) | async-done | bytes 4980752 | tf_op jit(solution)/shard_map/psum | solution.py:457
  (1107 shorter events, 745.5 us)
Async XLA Ops:
  39.1 84.2 %all-gather.9.cloned.1.call-start = ((), (), s32[]{:S(2)}) async-start(), calls=%async_computation.8 | async-start | bytes 1638400 | tf_op jit(solution)/shard_map/while/body/eval_jaxpr/all_gather | solution.py:61
  96.0 74.7 %all-gather.11.cloned.1.call-start = ((), (), s32[]{:S(2)}) async-start(), calls=%async_computation.9 | async-start | bytes 1310720 | tf_op jit(solution)/shard_map/while/body/eval_jaxpr/all_gather | solution.py:61
  144.0 60.5 %all-gather.15.cloned.1.call-start = ((), (), s32[]{:S(2)}) async-start(), calls=%async_computation.11 | async-start | bytes 2359296 | tf_op jit(solution)/shard_map/while/body/eval_jaxpr/all_gather | solution.py:228
  174.0 60.7 %all-gather.13.cloned.1.call-start = ((), (), s32[]{:S(2)}) async-start(), calls=%async_computation.10 | async-start | bytes 2359296 | tf_op jit(solution)/shard_map/while/body/eval_jaxpr/all_gather | solution.py:229
  179.6 95.6 %all-gather.17.cloned.1.call-start = ((), (), s32[]{:S(2)}) async-start(), calls=%async_computation.12 | async-start | bytes 1310720 | tf_op jit(solution)/shard_map/while/body/eval_jaxpr/all_gather | solution.py:61
  250.4 61.7 %reduce-scatter.23.cloned.1.call-start = ((), (), s32[]{:S(2)}) async-start(), calls=%async_computation.13 | async-start | bytes 1310720 | tf_op jit(solution)/shard_map/while
  284.3 126.3 %reduce-scatter.25.cloned.1.call-start = ((), (), s32[]{:S(2)}) async-start(), calls=%async_computation.14 | async-start | bytes 2359296 | tf_op jit(solution)/shard_map/while/body/eval_jaxpr/reduce_scatter | solution.py:320
  329.4 97.0 %reduce-scatter.27.cloned.1.call-start = ((), (), s32[]{:S(2)}) async-start(), calls=%async_computation.15 | async-start | bytes 2359296 | tf_op jit(solution)/shard_map/while/body/eval_jaxpr/reduce_scatter | solution.py:317
  392.4 73.2 %reduce-scatter.29.cloned.1.call-start = ((), (), s32[]{:S(2)}) async-start(), calls=%async_computation.16 | async-start | bytes 1310720 | tf_op jit(solution)/shard_map/while
  437.1 90.9 %reduce-scatter.31.cloned.1.call-start = ((), (), s32[]{:S(2)}) async-start(), calls=%async_computation.17 | async-start | bytes 1310720 | tf_op jit(solution)/shard_map/while
  503.3 93.4 %reduce-scatter.33.cloned.1.call-start = ((), (), s32[]{:S(2)}) async-start(), calls=%async_computation.18 | async-start | bytes 1310720 | tf_op jit(solution)/shard_map/while
  620.6 55.8 %all-gather.7.cloned.1.call-start = ((), (), s32[]{:S(2)}) async-start(), calls=%async_computation.7 | async-start | bytes 1638400 | tf_op jit(solution)/shard_map/while/body/eval_jaxpr/all_gather | solution.py:61
  648.9 84.4 %all-gather.9.cloned.1.call-start = ((), (), s32[]{:S(2)}) async-start(), calls=%async_computation.8 | async-start | bytes 1638400 | tf_op jit(solution)/shard_map/while/body/eval_jaxpr/all_gather | solution.py:61
  705.9 74.7 %all-gather.11.cloned.1.call-start = ((), (), s32[]{:S(2)}) async-start(), calls=%async_computation.9 | async-start | bytes 1310720 | tf_op jit(solution)/shard_map/while/body/eval_jaxpr/all_gather | solution.py:61
  754.0 60.5 %all-gather.15.cloned.1.call-start = ((), (), s32[]{:S(2)}) async-start(), calls=%async_computation.11 | async-start | bytes 2359296 | tf_op jit(solution)/shard_map/while/body/eval_jaxpr/all_gather | solution.py:228
  784.0 60.7 %all-gather.13.cloned.1.call-start = ((), (), s32[]{:S(2)}) async-start(), calls=%async_computation.10 | async-start | bytes 2359296 | tf_op jit(solution)/shard_map/while/body/eval_jaxpr/all_gather | solution.py:229
  789.4 95.8 %all-gather.17.cloned.1.call-start = ((), (), s32[]{:S(2)}) async-start(), calls=%async_computation.12 | async-start | bytes 1310720 | tf_op jit(solution)/shard_map/while/body/eval_jaxpr/all_gather | solution.py:61
  860.3 61.8 %reduce-scatter.23.cloned.1.call-start = ((), (), s32[]{:S(2)}) async-start(), calls=%async_computation.13 | async-start | bytes 1310720 | tf_op jit(solution)/shard_map/while
  894.2 126.3 %reduce-scatter.25.cloned.1.call-start = ((), (), s32[]{:S(2)}) async-start(), calls=%async_computation.14 | async-start | bytes 2359296 | tf_op jit(solution)/shard_map/while/body/eval_jaxpr/reduce_scatter | solution.py:320
  939.4 97.1 %reduce-scatter.27.cloned.1.call-start = ((), (), s32[]{:S(2)}) async-start(), calls=%async_computation.15 | async-start | bytes 2359296 | tf_op jit(solution)/shard_map/while/body/eval_jaxpr/reduce_scatter | solution.py:317
  1002.3 73.2 %reduce-scatter.29.cloned.1.call-start = ((), (), s32[]{:S(2)}) async-start(), calls=%async_computation.16 | async-start | bytes 1310720 | tf_op jit(solution)/shard_map/while
  1047.2 90.9 %reduce-scatter.31.cloned.1.call-start = ((), (), s32[]{:S(2)}) async-start(), calls=%async_computation.17 | async-start | bytes 1310720 | tf_op jit(solution)/shard_map/while
  1113.3 93.4 %reduce-scatter.33.cloned.1.call-start = ((), (), s32[]{:S(2)}) async-start(), calls=%async_computation.18 | async-start | bytes 1310720 | tf_op jit(solution)/shard_map/while
  1232.7 124.9 %all-reduce.26.cloned.1.call-start = ((), (), s32[]{:S(2)}) async-start(), calls=%async_computation.6 | async-start | bytes 9961472 | tf_op jit(solution)/shard_map/psum | solution.py:457
  (270 other events, 4508.6 us)
Sparse Core Ops, SparseCore 0:
  39.2 27.1 all-gather.6
  96.1 27.1 all-gather.8
  144.2 26.4 all-gather.10
  174.2 30.3 all-gather.14
  206.0 28.6 all-gather.12
  250.5 24.6 all-gather.16
  284.4 27.7 reduce-scatter.22
  329.5 33.8 reduce-scatter.24
  392.5 33.8 reduce-scatter.26
  437.2 28.2 reduce-scatter.28
  503.4 24.5 reduce-scatter.30
  572.2 24.4 reduce-scatter.32
  649.0 27.3 all-gather.6
  706.1 27.1 all-gather.8
  754.1 26.4 all-gather.10
  784.1 30.2 all-gather.14
  815.9 28.7 all-gather.12
  860.4 24.6 all-gather.16
  894.3 27.7 reduce-scatter.22
  939.5 33.8 reduce-scatter.24
  1002.5 33.9 reduce-scatter.26
  1047.3 28.2 reduce-scatter.28
  1113.5 24.5 reduce-scatter.30
  1182.3 24.4 reduce-scatter.32
Sparse Core Ops, SparseCore 1:
  1243.6 113.9 all-reduce.25
where the time goes:
time: 1380 us; the launch traced here: 1370 us
  waiting for transfers between devices  532 us (39%)
  matrix products  287 us (21%)
  blocking collectives  183 us (13%)
  other arithmetic  160 us (12%)
  local copies, waits for them, and re-layouts  133 us (10%)
  starting transfers between devices  58.2 us (4%)
  between operations  15.9 us (1%)
    all_gather x8, waiting for transfers between devices, all_channels(): return lax.all_gather(source, 'chan', axis=3, tiled=True)  204 us
    while x32, waiting for transfers between devices  150 us
    psum x1, waiting for transfers between devices, body(): lax.psum(sum_conv_one.astype(jnp.bfloat16), 'row').astype(jnp.float32)  92.4 us
    psum x6, blocking collectives, norm_forward(): first_sum, square_sum = lax.psum((first_sum, square_sum), 'row')  84.6 us
    psum x6, blocking collectives, norm_backward(): grad_sum, cross_sum = lax.psum((grad_sum, cross_sum), 'row')  81.7 us
    while x508, local copies, waits for them, and re-layouts  79.6 us
    convert_element_type x2, other arithmetic, one_batch(): (prob_image * (dprob_image - delta[..., None])).astype(jnp.bfloat16)  56.2 us
    all_gather x2, waiting for transfers between devices, one_batch(): lax.all_gather(key_own, 'row', axis=1, tiled=True)  49.3 us
  transfers between devices with their start and end apart: 41, of which 29 were waited for; matrix products, arithmetic and copies ran while one was open for 22% of the time, Pallas kernels for 0%

commit v1 on v0

--- a/solution.py
+++ b/solution.py
@@ -3,6 +3,8 @@
 import jax
 import jax.numpy as jnp
 from jax import lax
+from jax.experimental import pallas as pl
+from jax.experimental.pallas import tpu as pltpu
 from jax.sharding import PartitionSpec as P
 
 C = 512
@@ -155,7 +157,7 @@
     return channel_total(result)
 
 
-def body(
+def general_body(
     image,
     target,
     time_index,
@@ -485,47 +487,1160 @@
     )
 
 
+BF = jnp.bfloat16
+F32 = jnp.float32
+MESH_ID = pl.DeviceIdType.MESH
+NN = (((1,), (0,)), ((), ()))
+NT = (((1,), (1,)), ((), ()))
+ANY = pl.BlockSpec(memory_space=pl.ANY)
+VMEM = pl.BlockSpec(memory_space=pltpu.VMEM)
+PIX = 512
+PAD = 640
+CHUNKS = 8
+VMEM_LIMIT = 60 * 2**20
+DMA = pltpu.SemaphoreType.DMA
+
+
+def mm(left, right, dims=NN):
+    return lax.dot_general(left, right, dims, preferred_element_type=F32)
+
+
+class Place:
+    def __init__(self):
+        self.r = lax.axis_index("row")
+        self.c = lax.axis_index("chan")
+        self.z = lax.div(self.r, 2)
+        self.k = lax.rem(self.r, 2)
+        self.d = 2 * self.c + self.k
+        self.pair = lax.rem(self.c - self.z + 4, 4)
+        self.band = 2 * self.pair + self.k
+
+    def head_device(self, head):
+        return (2 * self.z + lax.rem(head, 2), lax.div(head, 2))
+
+    def band_device(self, band):
+        return (2 * self.z + lax.rem(band, 2), lax.rem(lax.div(band, 2) + self.z, 4))
+
+
+def send(src, dst, send_sem, recv_sem, device):
+    copy = pltpu.make_async_remote_copy(
+        src_ref=src,
+        dst_ref=dst,
+        send_sem=send_sem,
+        recv_sem=recv_sem,
+        device_id=device,
+        device_id_type=MESH_ID,
+    )
+    copy.start()
+    return copy
+
+
+def local(src, dst, sem):
+    copy = pltpu.make_async_copy(src, dst, sem)
+    copy.start()
+    return copy
+
+
+def greet_plane(me, barrier):
+    for step in range(1, 8):
+        pl.semaphore_signal(
+            barrier,
+            inc=1,
+            device_id=me.head_device(lax.rem(me.d + step, 8)),
+            device_id_type=MESH_ID,
+        )
+
+
+def group_matrix(ref):
+    rows = lax.broadcasted_iota(jnp.int32, (C, C), 0)
+    cols = lax.broadcasted_iota(jnp.int32, (C, C), 1)
+    ref[...] = jnp.where(lax.div(rows, 16) == lax.div(cols, 16), 1.0, 0.0).astype(BF)
+
+
+def group_total(rows, groups_ref):
+    top = rows.astype(BF)
+    rest = rows - top.astype(F32)
+    mid = rest.astype(BF)
+    low = (rest - mid.astype(F32)).astype(BF)
+    stacked = jnp.concatenate([top, mid, low, jnp.zeros_like(low)], axis=0)
+    sums = mm(stacked, groups_ref[...])
+    return sums[0:8] + sums[8:16] + sums[16:24]
+
+
+def plane_exchange(me, slots, ssem, rsem):
+    copies = []
+    for step in range(1, 8):
+        copies.append(
+            send(
+                slots.at[me.d],
+                slots.at[me.d],
+                ssem.at[step],
+                rsem.at[step],
+                me.head_device(lax.rem(me.d + step, 8)),
+            )
+        )
+    return copies
+
+
+def slots_total(slots):
+    total = slots[0]
+    for slot in range(1, 8):
+        total = total + slots[slot]
+    return total
+
+
+def fold(value):
+    return value.reshape(value.shape[0] // 8, 8, value.shape[1]).sum(axis=0)
+
+
+def as_row(value):
+    return jnp.sum(value, axis=0, keepdims=True)
+
+
+def store_rows(slots, index, rows):
+    filled = rows + [jnp.zeros((1, C), F32)] * (8 - len(rows))
+    slots[index] = jnp.concatenate(filled, axis=0)
+
+
+def chunk_of(i):
+    return pl.ds(pl.multiple_of(i * 64, 64), 64)
+
+
+def put_shifted(dst, start, value):
+    col = lax.broadcasted_iota(jnp.int32, (64, C), 0)
+    where = pl.ds(pl.multiple_of(start, 64), 64)
+    dst[1, where, :] = value.astype(BF)
+    dst[0, where, :] = jnp.where(col == 0, 0.0, pltpu.roll(value, 1, 0)).astype(BF)
+    dst[2, where, :] = jnp.where(col == 63, 0.0, pltpu.roll(value, 63, 0)).astype(BF)
+
+
+def halo_send(me, cat, halo, ssem, rsem):
+    @pl.when(me.band > 0)
+    def _():
+        send(cat.at[1, pl.ds(64, 64), :], halo.at[1], ssem.at[0], rsem.at[1],
+             me.band_device(me.band - 1))
+
+    @pl.when(me.band < 7)
+    def _():
+        send(cat.at[1, pl.ds(512, 64), :], halo.at[0], ssem.at[1], rsem.at[0],
+             me.band_device(me.band + 1))
+
+
+def halo_wait(me, cat, halo, ssem, rsem):
+    def pair(slot, ahead):
+        return pltpu.make_async_remote_copy(
+            src_ref=cat.at[1, pl.ds(64, 64), :], dst_ref=halo.at[slot],
+            send_sem=ssem.at[slot], recv_sem=rsem.at[slot],
+            device_id=me.band_device(ahead), device_id_type=MESH_ID)
+
+    zero = jnp.zeros((64, C), F32)
+
+    @pl.when(me.band > 0)
+    def _():
+        both = pair(0, me.band - 1)
+        both.wait_send()
+        both.wait_recv()
+        put_shifted(cat, 0, halo[0].astype(F32))
+
+    @pl.when(me.band == 0)
+    def _():
+        put_shifted(cat, 0, zero)
+
+    @pl.when(me.band < 7)
+    def _():
+        both = pair(1, me.band + 1)
+        both.wait_send()
+        both.wait_recv()
+        put_shifted(cat, 576, halo[1].astype(F32))
+
+    @pl.when(me.band == 7)
+    def _():
+        put_shifted(cat, 576, zero)
+
+
+def conv_taps(acc, cat, weight, order, flip, dims):
+    @pl.loop(0, 3 * len(order))
+    def _(i):
+        step = lax.div(i, 3)
+        col = lax.rem(i, 3)
+        row = order[0] if len(order) == 1 else order[0] + step * (order[1] - order[0])
+        tap = (2 - row) * 3 + (2 - col) if flip else row * 3 + col
+        start = pl.multiple_of(row * 64, 64)
+        acc[...] += mm(cat[col, pl.ds(start, PIX), :], weight[tap], dims)
+
+
+def image_targets(me):
+    return [(n, (2 * n + me.k, lax.rem(me.z + n, 4))) for n in range(4)]
+
+
+def front_kernel(
+    img, tgt, vec, w1, w2, wq, wo,
+    x_o, t_o, vec_o, st_o, a1_o, hid_o, a2_o, res_o, nrm_o, w1_o, w2_o, wq_o, wo_o, qkv_o,
+    x_v, t_v, vec_v, st_v, a1_v, hid_v, a2_v, res_v, nrm_v, w1_v, w2_v, wq_v, wo_v, qkv_v,
+    msg, groups, slots, halo,
+    vs, vr, ims, imr, tgs, tgr, ws, wr, fs, fr, wl, sts, str_, hs, hr, qs, qr, lsem, osem,
+):
+    me = Place()
+    barrier = pltpu.get_barrier_semaphore()
+    greet_plane(me, barrier)
+    own_block = jnp.logical_and(me.c == lax.rem(2 * me.z, 4), True)
+    for chan in range(4):
+        itself = jnp.logical_and(me.pair == me.z, me.c == chan)
+
+        @pl.when(jnp.logical_not(itself))
+        def _():
+            pl.semaphore_signal(
+                barrier, inc=1, device_id=(2 * me.pair + me.k, chan), device_id_type=MESH_ID
+            )
+
+    pl.semaphore_wait(barrier, 7 + 4 - jnp.where(own_block, 1, 0))
+    own_cols = pl.ds(pl.multiple_of(me.c * 128, 128), 128)
+    half = pl.ds(pl.multiple_of(me.c * 128 + me.k * 64, 64), 64)
+    my_half = pl.ds(pl.multiple_of(me.k * 64, 64), 64)
+
+    vec_v[:, own_cols] = vec[...]
+    vec_copies = [
+        send(vec, vec_v.at[:, own_cols], vs.at[t], vr.at[t], (me.r, lax.rem(me.c + t, 4)))
+        for t in range(1, 4)
+    ]
+
+    def image_send(src, dst, ssem, rsem):
+        for n, device in image_targets(me):
+            itself = jnp.logical_and(own_block, me.z == n)
+
+            @pl.when(jnp.logical_not(itself))
+            def _():
+                send(src.at[n], dst.at[:, own_cols], ssem.at[n], rsem.at[me.c], device)
+
+            @pl.when(itself)
+            def _():
+                local(src.at[n], dst.at[:, own_cols], rsem.at[me.c])
+
+    def image_wait(src, dst, ssem, rsem):
+        for chan in range(4):
+            pltpu.make_async_copy(
+                src.at[0], dst.at[:, pl.ds(chan * 128, 128)], rsem.at[chan]
+            ).wait()
+
+    def image_drain(src, dst, ssem, rsem):
+        for n, device in image_targets(me):
+            itself = jnp.logical_and(own_block, me.z == n)
+
+            @pl.when(jnp.logical_not(itself))
+            def _():
+                pltpu.make_async_remote_copy(
+                    src_ref=src.at[n], dst_ref=dst.at[:, own_cols], send_sem=ssem.at[n],
+                    recv_sem=rsem.at[me.c], device_id=device, device_id_type=MESH_ID,
+                ).wait_send()
+
+    def weight_send(index, src, dst):
+        local(src, dst.at[:, own_cols, :], wl.at[index])
+        return [
+            send(src.at[:, my_half, :], dst.at[:, half, :], ws.at[index, t], wr.at[index, t],
+                 (me.r, lax.rem(me.c + t, 4)))
+            for t in range(1, 4)
+        ]
+
+    def weight_forward(index, dst, copies):
+        out = []
+        for t in range(1, 4):
+            copies[t - 1].wait_recv()
+            origin = lax.rem(me.c - t + 4, 4)
+            rows = pl.ds(pl.multiple_of(origin * 128 + me.k * 64, 64), 64)
+            out.append(
+                send(dst.at[:, rows, :], dst.at[:, rows, :], fs.at[index, t], fr.at[index, t],
+                     (me.r + 1 - 2 * me.k, me.c))
+            )
+        return out
+
+    def weight_wait(index, src, dst, copies, forwards):
+        for copy in copies:
+            copy.wait_send()
+        for copy in forwards:
+            copy.wait()
+        pltpu.make_async_copy(src, dst.at[:, own_cols, :], wl.at[index]).wait()
+
+    image_send(img, x_v, ims, imr)
+    w1_copies = weight_send(0, w1, w1_v)
+    group_matrix(groups)
+    col_zero = jnp.zeros((8, C), F32)
+    for copy in vec_copies:
+        copy.wait()
+    image_wait(img, x_v, ims, imr)
+    outs = []
+
+    def save(index, src, dst):
+        outs.append(local(src, dst, osem.at[index]))
+
+    save(0, x_v, x_o)
+    save(2, vec_v, vec_o)
+
+    def statistics(number, ref):
+        def add(i, carry):
+            value = ref[chunk_of(i), :].astype(F32)
+            return (carry[0] + fold(value), carry[1] + fold(value * value))
+
+        first, square = lax.fori_loop(0, CHUNKS, add, (col_zero, col_zero))
+        store_rows(slots.at[number], me.d, [as_row(first), as_row(square)])
+        return plane_exchange(me, slots.at[number], sts.at[number], str_.at[number])
+
+    def finish_statistics(number, copies):
+        for copy in copies:
+            copy.wait()
+        means = group_total(slots_total(slots.at[number]), groups) * (1.0 / (H * W * 16))
+        center = means[0:1]
+        inverse = lax.rsqrt(means[1:2] - center * center + EPSILON)
+        st_v[2 * number : 2 * number + 1, :] = center
+        st_v[2 * number + 1 : 2 * number + 2, :] = inverse
+        return center, inverse
+
+    copies = statistics(0, x_v)
+    w2_copies = weight_send(1, w2, w2_v)
+    center, inverse = finish_statistics(0, copies)
+    gain, bias = vec_v[0:1, :], vec_v[3:4, :]
+
+    @pl.loop(0, CHUNKS)
+    def _(i):
+        value = (x_v[chunk_of(i), :].astype(F32) - center) * inverse
+        put_shifted(a1_v, 64 + i * 64, swish(value * gain + bias))
+
+    halo_send(me, a1_v, halo.at[0], hs.at[0], hr.at[0])
+    hid_v[...] = jnp.broadcast_to(vec_v[6:7, :], (PIX, C))
+    w1_forward = weight_forward(0, w1_v, w1_copies)
+    weight_wait(0, w1, w1_v, w1_copies, w1_forward)
+    save(9, w1_v, w1_o)
+    wq_copies = weight_send(2, wq, wq_v)
+    conv_taps(hid_v, a1_v, w1_v, (1,), False, NT)
+    halo_wait(me, a1_v, halo.at[0], hs.at[0], hr.at[0])
+    save(4, a1_v, a1_o)
+    conv_taps(hid_v, a1_v, w1_v, (0, 2), False, NT)
+    save(5, hid_v, hid_o)
+    copies = statistics(1, hid_v)
+    wo_copies = weight_send(3, wo, wo_v)
+    image_send(tgt, t_v, tgs, tgr)
+    center, inverse = finish_statistics(1, copies)
+    gain, bias = vec_v[1:2, :], vec_v[4:5, :]
+    scale, shift = 1.0 + vec_v[11:12, :], vec_v[12:13, :]
+
+    @pl.loop(0, CHUNKS)
+    def _(i):
+        value = (hid_v[chunk_of(i), :] - center) * inverse
+        put_shifted(a2_v, 64 + i * 64, swish((value * gain + bias) * scale + shift))
+
+    halo_send(me, a2_v, halo.at[1], hs.at[1], hr.at[1])
+    res_v[...] = x_v[...].astype(F32) + vec_v[7:8, :]
+    w2_forward = weight_forward(1, w2_v, w2_copies)
+    weight_wait(1, w2, w2_v, w2_copies, w2_forward)
+    save(10, w2_v, w2_o)
+    conv_taps(res_v, a2_v, w2_v, (1,), False, NT)
+    halo_wait(me, a2_v, halo.at[1], hs.at[1], hr.at[1])
+    save(6, a2_v, a2_o)
+    conv_taps(res_v, a2_v, w2_v, (0, 2), False, NT)
+    save(7, res_v, res_o)
+    copies = statistics(2, res_v)
+    wq_forward = weight_forward(2, wq_v, wq_copies)
+    wo_forward = weight_forward(3, wo_v, wo_copies)
+    weight_wait(2, wq, wq_v, wq_copies, wq_forward)
+    save(11, wq_v, wq_o)
+    center, inverse = finish_statistics(2, copies)
+    gain, bias = vec_v[2:3, :], vec_v[5:6, :]
+    normed = ((res_v[...] - center) * inverse * gain + bias)
+    nrm_v[...] = normed.astype(BF)
+    save(8, nrm_v, nrm_o)
+    save(3, st_v, st_o)
+    turned = jnp.transpose(normed).astype(BF)
+    for j, row in ((0, 8), (1, None), (2, 9)):
+        value = mm(wq_v[j], turned)
+        if row is not None:
+            wide = jnp.transpose(jnp.broadcast_to(vec_v[row : row + 1, :], (128, C)))
+            value = value + jnp.concatenate([wide] * 4, axis=1)
+        msg[j] = value.astype(BF)
+
+    band_cols = pl.ds(pl.multiple_of(me.band * PIX, PIX), PIX)
+
+    def head_rows(head):
+        return pl.ds(pl.multiple_of(head * HEAD, HEAD), HEAD)
+
+    own = local(msg.at[:, head_rows(me.d), :], qkv_v.at[:, :, band_cols], lsem.at[0])
+    copies = []
+    for step in range(1, 8):
+        head = lax.rem(me.d + step, 8)
+        copies.append(
+            send(msg.at[:, head_rows(head), :], qkv_v.at[:, :, band_cols], qs.at[step],
+                 qr.at[step], me.head_device(head))
+        )
+    weight_wait(3, wo, wo_v, wo_copies, wo_forward)
+    save(12, wo_v, wo_o)
+    image_wait(tgt, t_v, tgs, tgr)
+    save(1, t_v, t_o)
+    image_drain(img, x_v, ims, imr)
+    image_drain(tgt, t_v, tgs, tgr)
+    own.wait()
+    for copy in copies:
+        copy.wait()
+    save(13, qkv_v, qkv_o)
+    for copy in outs:
+        copy.wait()
+
+
+def front(img, tgt, vec, w1, w2, wq, wo):
+    saved = [
+        ((PIX, C), BF), ((PIX, C), BF), ((16, C), F32), ((8, C), F32), ((3, PAD, C), BF),
+        ((PIX, C), F32), ((3, PAD, C), BF), ((PIX, C), F32), ((PIX, C), BF), ((9, C, C), BF),
+        ((9, C, C), BF), ((3, C, C), BF), ((1, C, C), BF), ((3, HEAD, H * W), BF),
+    ]
+    return pl.pallas_call(
+        front_kernel,
+        name="front",
+        out_shape=[jax.ShapeDtypeStruct(*one) for one in saved],
+        in_specs=[ANY, ANY, VMEM, ANY, ANY, ANY, ANY],
+        out_specs=[ANY] * len(saved),
+        scratch_shapes=[pltpu.VMEM(*one) for one in saved]
+        + [
+            pltpu.VMEM((3, C, C), BF), pltpu.VMEM((C, C), BF), pltpu.VMEM((3, 8, 8, C), F32),
+            pltpu.VMEM((2, 2, 64, C), BF),
+            DMA((4,)), DMA((4,)), DMA((4,)), DMA((4,)), DMA((4,)), DMA((4,)),
+            DMA((4, 4)), DMA((4, 4)), DMA((4, 4)), DMA((4, 4)), DMA((4,)),
+            DMA((3, 8)), DMA((3, 8)), DMA((2, 2)), DMA((2, 2)), DMA((8,)), DMA((8,)),
+            DMA((1,)), DMA((14,)),
+        ],
+        compiler_params=pltpu.CompilerParams(
+            collective_id=1, has_side_effects=True, vmem_limit_bytes=VMEM_LIMIT
+        ),
+    )(img, tgt, vec, w1, w2, wq, wo)
+
+
+LOG2E = 1.4426950408889634
+QBLOCK = 256
+VROWS = 80
+
+
+def attend_kernel(qkv, ctx, p_o, pc_o, o_o, ot_o, linv_o, keys, ckeys, qs, vext, cvext):
+    pixels = H * W
+    i = pl.program_id(0)
+
+    @pl.when(i == 0)
+    def _():
+        both = jnp.concatenate([qkv[1], qkv[1]], axis=0).astype(F32)
+        keys[...] = jnp.transpose(both).astype(BF)
+        cboth = jnp.concatenate([ctx[0], ctx[0]], axis=0).astype(F32)
+        ckeys[...] = jnp.transpose(cboth)[0:16].astype(BF)
+        scaled = qkv[0].astype(F32) * (HEAD ** (-0.5) * LOG2E)
+        top = scaled.astype(BF)
+        qs[0:HEAD, :] = top
+        qs[HEAD:, :] = (scaled - top.astype(F32)).astype(BF)
+        row = lax.broadcasted_iota(jnp.int32, (16, pixels), 0)
+        vext[0:HEAD, :] = qkv[2]
+        vext[HEAD:, :] = jnp.where(row == 0, 1.0, 0.0).astype(BF)
+        cvext[0:HEAD, :] = ctx[1]
+        cvext[HEAD:, :] = jnp.where(row[:, 0:128] == 0, 1.0, 0.0).astype(BF)
+
+    cols = pl.ds(pl.multiple_of(i * QBLOCK, QBLOCK), QBLOCK)
+    query = qs[:, cols]
+    score = mm(keys[...], query)
+    cscore = mm(ckeys[...], query)
+    token = lax.broadcasted_iota(jnp.int32, (16, QBLOCK), 0)
+    cscore = jnp.where(token < CTX, cscore, -1e30)
+    top = jnp.maximum(
+        jnp.max(score, axis=0, keepdims=True), jnp.max(cscore, axis=0, keepdims=True)
+    )
+    p_o[...] = jnp.exp2(score - top).astype(BF)
+    pc = jnp.exp2(cscore - top).astype(BF)
+    pc_o[...] = pc
+    out = mm(vext[...], p_o[...]) + mm(cvext[:, 0:16], pc)
+    linv = 1.0 / out[HEAD : HEAD + 1]
+    out = out[0:HEAD] * linv
+    o_o[...] = out
+    ot_o[...] = out.astype(BF)
+    linv_o[...] = jnp.broadcast_to(linv, (8, QBLOCK))
+
+
+def attend(qkv, ctx):
+    pixels = H * W
+    whole = lambda *shape: pl.BlockSpec(shape, lambda i: (0,) * len(shape))
+    cols = lambda rows: pl.BlockSpec((rows, QBLOCK), lambda i: (0, i))
+    return pl.pallas_call(
+        attend_kernel,
+        name="attend",
+        grid=(pixels // QBLOCK,),
+        out_shape=[
+            jax.ShapeDtypeStruct((pixels, pixels), BF),
+            jax.ShapeDtypeStruct((16, pixels), BF),
+            jax.ShapeDtypeStruct((HEAD, pixels), F32),
+            jax.ShapeDtypeStruct((HEAD, pixels), BF),
+            jax.ShapeDtypeStruct((8, pixels), F32),
+        ],
+        in_specs=[whole(3, HEAD, pixels), whole(2, HEAD, 128)],
+        out_specs=[cols(pixels), cols(16), cols(HEAD), cols(HEAD), cols(8)],
+        scratch_shapes=[
+            pltpu.VMEM((pixels, 128), BF), pltpu.VMEM((16, 128), BF),
+            pltpu.VMEM((128, pixels), BF), pltpu.VMEM((VROWS, pixels), BF),
+            pltpu.VMEM((VROWS, 128), BF),
+        ],
+        compiler_params=pltpu.CompilerParams(vmem_limit_bytes=VMEM_LIMIT),
+    )(qkv, ctx)
+
+
+def band_back_send(me, src, dst, ssem, rsem):
+    for chan in range(4):
+        cols = pl.ds(chan * 128, 128)
+        itself = jnp.logical_and(me.band == me.r, me.c == chan)
+
+        @pl.when(jnp.logical_not(itself))
+        def _():
+            send(src.at[:, cols], dst.at[me.z], ssem.at[chan], rsem.at[me.z], (me.band, chan))
+
+        @pl.when(itself)
+        def _():
+            local(src.at[:, cols], dst.at[me.z], rsem.at[me.z])
+
+
+def band_back_wait(me, src, dst, ssem, rsem):
+    for n in range(4):
+        pltpu.make_async_copy(src.at[:, pl.ds(0, 128)], dst.at[n], rsem.at[n]).wait()
+    for chan in range(4):
+        itself = jnp.logical_and(me.band == me.r, me.c == chan)
+
+        @pl.when(jnp.logical_not(itself))
+        def _():
+            pltpu.make_async_remote_copy(
+                src_ref=src.at[:, pl.ds(chan * 128, 128)], dst_ref=dst.at[me.z],
+                send_sem=ssem.at[chan], recv_sem=rsem.at[me.z], device_id=(me.band, chan),
+                device_id_type=MESH_ID,
+            ).wait_send()
+
+
+def greet_back(me, barrier):
+    own_block = me.c == lax.rem(2 * me.z, 4)
+    for n in range(4):
+        itself = jnp.logical_and(own_block, me.z == n)
+
+        @pl.when(jnp.logical_not(itself))
+        def _():
+            pl.semaphore_signal(
+                barrier, inc=1, device_id=(2 * n + me.k, lax.rem(me.z + n, 4)),
+                device_id_type=MESH_ID,
+            )
+
+    return 4 - jnp.where(own_block, 1, 0)
+
+
+def middle_kernel(
+    ot, res, tgt, wo, vec,
+    out_o, cot_o, gwo_o, gob_o, dot_o,
+    attn_t, res_v, tgt_v, wo_v, out_b, back, cot_v, dat, dot_v,
+    as_, ar, bs, br, ds_, dr, lsem, osem,
+):
+    me = Place()
+    barrier = pltpu.get_barrier_semaphore()
+    greet_plane(me, barrier)
+    others = greet_back(me, barrier)
+    loads = [local(a, b, lsem.at[j]) for j, (a, b) in enumerate(
+        ((res, res_v), (tgt, tgt_v), (wo.at[0], wo_v)))]
+    pl.semaphore_wait(barrier, 7 + others)
+    mine = pl.ds(pl.multiple_of(me.d * HEAD, HEAD), HEAD)
+
+    def band_cols(band):
+        return pl.ds(pl.multiple_of(band * PIX, PIX), PIX)
+
+    own = local(ot.at[:, band_cols(me.band)], attn_t.at[mine, :], lsem.at[3])
+    copies = []
+    for step in range(1, 8):
+        band = lax.rem(me.band + step, 8)
+        copies.append(
+            send(ot.at[:, band_cols(band)], attn_t.at[mine, :], as_.at[step], ar.at[me.d],
+                 me.band_device(band))
+        )
+    for load in loads:
+        load.wait()
+    own.wait()
+    for copy in copies:
+        copy.wait_send()
+    for step in range(1, 8):
+        head = lax.rem(me.d + step, 8)
+        pltpu.make_async_copy(
+            ot.at[:, band_cols(0)],
+            attn_t.at[pl.ds(pl.multiple_of(head * HEAD, HEAD), HEAD), :],
+            ar.at[head],
+        ).wait()
+    attn = jnp.transpose(attn_t[...].astype(F32)).astype(BF)
+    result = res_v[...] + mm(attn, wo_v[...], NT) + vec[10:11, :]
+    out_b[...] = result.astype(BF)
+    band_back_send(me, out_b, back, bs, br)
+    cot = vec[13:14, :] * (result - tgt_v[...].astype(F32))
+    cot_v[...] = cot
+    saves = [local(cot_v, cot_o, osem.at[0])]
+    low = cot.astype(BF)
+    dat[...] = jnp.transpose(mm(low, wo_v[...])).astype(BF)
+    own = local(dat.at[mine, :], dot_v.at[:, band_cols(me.band)], lsem.at[4])
+    copies = []
+    for step in range(1, 8):
+        head = lax.rem(me.d + step, 8)
+        rows = pl.ds(pl.multiple_of(head * HEAD, HEAD), HEAD)
+        copies.append(
+            send(dat.at[rows, :], dot_v.at[:, band_cols(me.band)], ds_.at[step], dr.at[step],
+                 me.head_device(head))
+        )
+    lowf = low.astype(F32)
+    gwo_o[...] = mm(jnp.transpose(lowf).astype(BF), attn).astype(BF)
+    gob_o[...] = jnp.broadcast_to(as_row(lowf), (8, C))
+    band_back_wait(me, out_b, back, bs, br)
+    out_o[...] = back[...].astype(F32)
+    own.wait()
+    for copy in copies:
+        copy.wait()
+    saves.append(local(dot_v, dot_o, osem.at[1]))
+    for copy in saves:
+        copy.wait()
+
+
+def middle(ot, res, tgt, wo, vec):
+    return pl.pallas_call(
+        middle_kernel,
+        name="middle",
+        out_shape=[
+            jax.ShapeDtypeStruct((4, PIX, 128), F32),
+            jax.ShapeDtypeStruct((PIX, C), F32),
+            jax.ShapeDtypeStruct((C, C), BF),
+            jax.ShapeDtypeStruct((8, C), F32),
+            jax.ShapeDtypeStruct((HEAD, H * W), BF),
+        ],
+        in_specs=[ANY, ANY, ANY, ANY, VMEM],
+        out_specs=[VMEM, ANY, VMEM, VMEM, ANY],
+        scratch_shapes=[
+            pltpu.VMEM((C, PIX), BF), pltpu.VMEM((PIX, C), F32), pltpu.VMEM((PIX, C), BF),
+            pltpu.VMEM((C, C), BF), pltpu.VMEM((PIX, C), BF), pltpu.VMEM((4, PIX, 128), BF),
+            pltpu.VMEM((PIX, C), F32), pltpu.VMEM((C, PIX), BF), pltpu.VMEM((HEAD, H * W), BF),
+            DMA((8,)), DMA((8,)), DMA((4,)), DMA((4,)), DMA((8,)), DMA((8,)), DMA((5,)),
+            DMA((2,)),
+        ],
+        compiler_params=pltpu.CompilerParams(
+            collective_id=2, has_side_effects=True, vmem_limit_bytes=VMEM_LIMIT
+        ),
+    )(ot, res, tgt, wo, vec)
+
+
+KBLOCK = 256
+
+
+def attend_back_kernel(
+    qkv, ctx, p, pc, o, linv, dot_, dqkv_o, dctx_o, vext, cvext, dos, dor, qrow, dq
+):
+    pixels = H * W
+    i = pl.program_id(0)
+    scaling = HEAD ** (-0.5)
+
+    def score_grads(values, probs):
+        return (probs.astype(F32) * mm(values, dos[...])).astype(BF)
+
+    @pl.when(i == 0)
+    def _():
+        row = lax.broadcasted_iota(jnp.int32, (HEAD, pixels), 0)
+        ones = jnp.where(row < 3, 1.0, 0.0)
+        vext[...] = jnp.transpose(
+            jnp.concatenate([qkv[2].astype(F32), ones], axis=0)
+        ).astype(BF)
+        cvext[...] = jnp.transpose(
+            jnp.concatenate([ctx[1].astype(F32), ones[:, 0:128]], axis=0)
+        )[0:16].astype(BF)
+        grad = (dot_[...].astype(F32) * linv[0:1, :]).astype(BF)
+        gradf = grad.astype(F32)
+        delta = -jnp.sum(gradf * o[...], axis=0, keepdims=True)
+        top = delta.astype(BF).astype(F32)
+        mid = (delta - top).astype(BF).astype(F32)
+        low = delta - top - mid
+        dos[0:HEAD, :] = grad
+        dos[HEAD:, :] = jnp.where(
+            row == 0, top, jnp.where(row == 1, mid, jnp.where(row == 2, low, 0.0))
+        ).astype(BF)
+        dor[...] = jnp.transpose(jnp.concatenate([gradf, jnp.zeros_like(gradf)], axis=0)).astype(BF)
+        qf = qkv[0].astype(F32) * scaling
+        qrow[...] = jnp.transpose(jnp.concatenate([qf, jnp.zeros_like(qf)], axis=0)).astype(BF)
+        probs = pc[...]
+        dsc = score_grads(cvext[...], probs)
+        dctx_o[0] = mm(dsc, qrow[...])
+        dctx_o[1] = mm(probs, dor[...])
+        dq[...] = mm(ctx[0][:, 0:16], dsc)
+
+    cols = pl.ds(pl.multiple_of(i * KBLOCK, KBLOCK), KBLOCK)
+    probs = p[...]
+    ds = score_grads(vext[cols, :], probs)
+    dqkv_o[2, :, cols] = jnp.transpose(mm(probs, dor[...]))[0:HEAD].astype(BF)
+    dqkv_o[1, :, cols] = jnp.transpose(mm(ds, qrow[...]))[0:HEAD].astype(BF)
+    dq[...] += mm(qkv[1, :, cols], ds)
+
+    @pl.when(i == pixels // KBLOCK - 1)
+    def _():
+        dqkv_o[0] = (dq[...] * scaling).astype(BF)
+
+
+def attend_back(qkv, ctx, p, pc, o, linv, dot_):
+    pixels = H * W
+    whole = lambda *shape: pl.BlockSpec(shape, lambda i: (0,) * len(shape))
+    return pl.pallas_call(
+        attend_back_kernel,
+        name="attend_back",
+        grid=(pixels // KBLOCK,),
+        out_shape=[
+            jax.ShapeDtypeStruct((3, HEAD, pixels), BF),
+            jax.ShapeDtypeStruct((2, 16, 128), F32),
+        ],
+        in_specs=[
+            whole(3, HEAD, pixels), whole(2, HEAD, 128),
+            pl.BlockSpec((KBLOCK, pixels), lambda i: (i, 0)),
+            whole(16, pixels), whole(HEAD, pixels), whole(8, pixels), whole(HEAD, pixels),
+        ],
+        out_specs=[whole(3, HEAD, pixels), whole(2, 16, 128)],
+        scratch_shapes=[
+            pltpu.VMEM((pixels, 128), BF), pltpu.VMEM((16, 128), BF),
+            pltpu.VMEM((128, pixels), BF), pltpu.VMEM((pixels, 128), BF),
+            pltpu.VMEM((pixels, 128), BF), pltpu.VMEM((HEAD, pixels), F32),
+        ],
+        compiler_params=pltpu.CompilerParams(vmem_limit_bytes=VMEM_LIMIT),
+    )(qkv, ctx, p, pc, o, linv, dot_)
+
+
+TAPS = 22
+GROUP_TAPS = ((0, 1), (1, 3), (4, 3), (7, 3), (10, 3), (13, 3), (16, 3), (19, 3))
+
+
+class Reduce:
+    def __init__(self, me, part, from_core, from_chan, plane, from_plane, total, sems):
+        self.me = me
+        self.part, self.from_core, self.from_chan = part, from_core, from_chan
+        self.plane, self.from_plane, self.total = plane, from_plane, total
+        self.sems = sems
+        self.copies = {}
+
+    def advance(self, group):
+        stage = self.copies.get(group, (0, []))[0]
+        for copy in self.copies.get(group, (0, []))[1]:
+            copy.wait()
+        step = (self.core_send, self.chan_send, self.plane_send, self.plane_gather,
+                self.core_gather, lambda group, taps: [])[stage]
+        start, count = GROUP_TAPS[group]
+        self.copies[group] = (stage + 1, step(group, pl.ds(start, count)))
+
+    def core_send(self, group, taps):
+        me = self.me
+        s, r = self.sems[0], self.sems[1]
+        return [
+            send(self.part.at[taps, :, 1 - me.k], self.from_core.at[taps], s.at[group],
+                 r.at[group], (me.r + 1 - 2 * me.k, me.c))
+        ]
+
+    def chan_send(self, group, taps):
+        me = self.me
+        start, count = GROUP_TAPS[group]
+
+        @pl.loop(start, start + count)
+        def _(tap):
+            own = self.part[tap, :, me.k].astype(F32) + self.from_core[tap].astype(F32)
+            self.part[tap, :, me.k] = own.astype(BF)
+
+        s, r = self.sems[2], self.sems[3]
+        out = []
+        for t in range(1, 4):
+            chan = lax.rem(me.c + t, 4)
+            out.append(
+                send(self.part.at[taps, chan, me.k], self.from_chan.at[t - 1, taps],
+                     s.at[group, t], r.at[group, t], (me.r, chan))
+            )
+        return out
+
+    def plane_send(self, group, taps):
+        me = self.me
+        start, count = GROUP_TAPS[group]
+
+        @pl.loop(start, start + count)
+        def _(tap):
+            value = self.part[tap, me.c, me.k].astype(F32)
+            for t in range(3):
+                value = value + self.from_chan[t, tap].astype(F32)
+            self.plane[tap] = value.astype(BF)
+
+        s, r = self.sems[4], self.sems[5]
+        out = []
+        for t in range(1, 4):
+            z = lax.rem(me.z + t, 4)
+            rows = pl.ds(pl.multiple_of(z * 16, 16), 16)
+            out.append(
+                send(self.plane.at[taps, rows, :], self.from_plane.at[t - 1, taps],
+                     s.at[group, t], r.at[group, t], (2 * z + me.k, me.c))
+            )
+        return out
+
+    def plane_gather(self, group, taps):
+        me = self.me
+        start, count = GROUP_TAPS[group]
+        rows = pl.ds(pl.multiple_of(me.z * 16, 16), 16)
+
+        @pl.loop(start, start + count)
+        def _(tap):
+            value = self.plane[tap, rows, :].astype(F32)
+            for t in range(3):
+                value = value + self.from_plane[t, tap].astype(F32)
+            self.total[tap, me.k, me.z] = value.astype(BF)
+
+        s, r = self.sems[6], self.sems[7]
+        out = []
+        for t in range(1, 4):
+            z = lax.rem(me.z + t, 4)
+            piece = self.total.at[taps, me.k, me.z]
+            out.append(send(piece, piece, s.at[group, t], r.at[group, t], (2 * z + me.k, me.c)))
+        return out
+
+    def core_gather(self, group, taps):
+        me = self.me
+        s, r = self.sems[8], self.sems[9]
+        piece = self.total.at[taps, me.k]
+        return [send(piece, piece, s.at[group], r.at[group], (me.r + 1 - 2 * me.k, me.c))]
+
+
+def back_kernel(
+    dqkv, vec, st, x, a1, hid, a2, res, nrm, cot, w1, w2, wq, gwo, gob,
+    gimg_o, zv_o, fin_o,
+    dt_v, x_v, a1_v, hid_v, a2_v, res_v, nrm_v, drs_v, w1_v, w2_v, wq_v,
+    cat, turned, acc, groups, slots, halo, keep, img_b, back, zsl,
+    part, from_core, from_chan, plane, from_plane, total,
+    as_, ar, ss, sr, hs, hr, bs, br, zs, zr, c1s, c1r, c2s, c2r, p1s, p1r, p2s, p2r, c3s, c3r,
+    lsem, osem,
+):
+    me = Place()
+    barrier = pltpu.get_barrier_semaphore()
+    greet_plane(me, barrier)
+    others = greet_back(me, barrier)
+    for t in range(1, 4):
+        pl.semaphore_signal(
+            barrier, inc=1, device_id=(2 * lax.rem(me.z + t, 4) + me.k, me.c),
+            device_id_type=MESH_ID,
+        )
+    loads = [local(a, b, lsem.at[j]) for j, (a, b) in enumerate((
+        (gwo, part.at[0]), (nrm, nrm_v), (wq, wq_v), (res, res_v), (cot, drs_v), (a2, a2_v),
+        (w2, w2_v), (hid, hid_v), (a1, a1_v), (w1, w1_v), (x, x_v)))]
+    pl.semaphore_wait(barrier, 10 + others)
+    reduce = Reduce(me, part, from_core, from_chan, plane, from_plane, total,
+                    (c1s, c1r, c2s, c2r, p1s, p1r, p2s, p2r, c3s, c3r))
+    mine = pl.ds(pl.multiple_of(me.d * HEAD, HEAD), HEAD)
+
+    def band_cols(band):
+        return pl.ds(pl.multiple_of(band * PIX, PIX), PIX)
+
+    own = local(dqkv.at[:, :, band_cols(me.band)], dt_v.at[:, mine, :], lsem.at[11])
+    copies = []
+    for step in range(1, 8):
+        band = lax.rem(me.band + step, 8)
+        copies.append(
+            send(dqkv.at[:, :, band_cols(band)], dt_v.at[:, mine, :], as_.at[step], ar.at[me.d],
+                 me.band_device(band))
+        )
+    group_matrix(groups)
+    zero8 = jnp.zeros((8, C), F32)
+    members = 1.0 / (H * W * 16)
+    loads[0].wait()
+    reduce.advance(0)
+    loads[1].wait()
+    loads[2].wait()
+    own.wait()
+    for copy in copies:
+        copy.wait_send()
+    for step in range(1, 8):
+        head = lax.rem(me.d + step, 8)
+        pltpu.make_async_copy(
+            dqkv.at[:, :, band_cols(0)],
+            dt_v.at[:, pl.ds(pl.multiple_of(head * HEAD, HEAD), HEAD), :],
+            ar.at[head],
+        ).wait()
+
+    @pl.loop(0, 3)
+    def _(j):
+        part[1 + j] = mm(dt_v[j], nrm_v[...]).astype(BF).reshape(4, 2, 64, C)
+
+    reduce.advance(1)
+    reduce.advance(0)
+    for j in range(3):
+        rows = jnp.transpose(dt_v[j].astype(F32))
+        if j != 1:
+            keep[j : j + 1, :] = as_row(rows)
+        value = mm(rows.astype(BF), wq_v[j])
+        if j == 0:
+            acc[...] = value
+        else:
+            acc[...] += value
+    loads[3].wait()
+
+    def sums(scaled_of, upstream_of):
+        def add(i, carry):
+            upstream = upstream_of(i)
+            return (carry[0] + fold(upstream), carry[1] + fold(upstream * scaled_of(i)))
+
+        first, cross = lax.fori_loop(0, CHUNKS, add, (zero8, zero8))
+        return [as_row(first), as_row(cross)]
+
+    def scaled(ref, number):
+        return lambda i: (ref[chunk_of(i), :].astype(F32) - st[2 * number : 2 * number + 1, :]) * st[
+            2 * number + 1 : 2 * number + 2, :]
+
+    def exchange(number, rows):
+        store_rows(slots.at[number], me.d, rows)
+        return plane_exchange(me, slots.at[number], ss.at[number], sr.at[number])
+
+    scaled3, scaled2, scaled1 = scaled(res_v, 2), scaled(hid_v, 1), scaled(x_v, 0)
+    copies = exchange(0, sums(scaled3, lambda i: acc[chunk_of(i), :]))
+    reduce.advance(1)
+    for load in loads[4:]:
+        load.wait()
+    for copy in copies:
+        copy.wait()
+
+    def group_means(total_rows, factor):
+        return group_total(total_rows * factor, groups) * members
+
+    total3 = slots_total(slots.at[0])
+    gain = vec[2:3, :]
+    means = group_means(total3, gain)
+    keep[8:16, :] = total3
+    inverse = st[5:6, :]
+
+    def resid_grad(i, carry):
+        where = chunk_of(i)
+        value = drs_v[where, :] + inverse * (
+            acc[where, :] * gain - means[0:1] - scaled3(i) * means[1:2])
+        drs_v[where, :] = value
+        put_shifted(cat, 64 + i * 64, value)
+        return carry + fold(value.astype(BF).astype(F32))
+
+    keep[3:4, :] = as_row(lax.fori_loop(0, CHUNKS, resid_grad, zero8))
+    halo_send(me, cat, halo.at[0], hs.at[0], hr.at[0])
+    reduce.advance(0)
+    turned[...] = jnp.transpose(drs_v[...]).astype(BF)
+
+    def weight_grads(group, source):
+        start = GROUP_TAPS[group][0]
+        row = (group - 2) % 3
+
+        @pl.loop(0, 3)
+        def _(col):
+            part[start + col] = mm(turned[...], source[col, row * 64 : row * 64 + PIX, :]).astype(
+                BF).reshape(4, 2, 64, C)
+
+        reduce.advance(group)
+
+    weight_grads(2, a2_v)
+    reduce.advance(1)
+    weight_grads(3, a2_v)
+    reduce.advance(2)
+    weight_grads(4, a2_v)
+    reduce.advance(0)
+    reduce.advance(3)
+    acc[...] = jnp.zeros((PIX, C), F32)
+    conv_taps(acc, cat, w2_v, (1,), True, NN)
+    halo_wait(me, cat, halo.at[0], hs.at[0], hr.at[0])
+    reduce.advance(1)
+    reduce.advance(4)
+    conv_taps(acc, cat, w2_v, (0, 2), True, NN)
+    reduce.advance(2)
+    gain2, bias2 = vec[1:2, :], vec[4:5, :]
+    scale, shift = 1.0 + vec[11:12, :], vec[12:13, :]
+
+    def mod_grad(i):
+        where = chunk_of(i)
+        mod = (scaled2(i) * gain2 + bias2) * scale + shift
+        value = acc[where, :] * swish_slope(mod)
+        acc[where, :] = value
+        return value
+
+    copies = exchange(1, sums(scaled2, mod_grad))
+    reduce.advance(0)
+    reduce.advance(3)
+    for copy in copies:
+        copy.wait()
+    total2 = slots_total(slots.at[1])
+    means2 = group_means(total2, gain2 * scale)
+    keep[16:24, :] = total2
+    inverse2 = st[3:4, :]
+
+    def hidden_grad(i, carry):
+        where = chunk_of(i)
+        value = inverse2 * (
+            acc[where, :] * (gain2 * scale) - means2[0:1] - scaled2(i) * means2[1:2])
+        acc[where, :] = value
+        put_shifted(cat, 64 + i * 64, value)
+        return carry + fold(value.astype(BF).astype(F32))
+
+    keep[1:2, :] = as_row(lax.fori_loop(0, CHUNKS, hidden_grad, zero8))
+    halo_send(me, cat, halo.at[1], hs.at[1], hr.at[1])
+    turned[...] = jnp.transpose(acc[...]).astype(BF)
+    reduce.advance(1)
+    weight_grads(5, a1_v)
+    reduce.advance(4)
+    reduce.advance(2)
+    weight_grads(6, a1_v)
+    reduce.advance(5)
+    reduce.advance(3)
+    weight_grads(7, a1_v)
+    reduce.advance(6)
+    reduce.advance(1)
+    acc[...] = jnp.zeros((PIX, C), F32)
+    conv_taps(acc, cat, w1_v, (1,), True, NN)
+    halo_wait(me, cat, halo.at[1], hs.at[1], hr.at[1])
+    reduce.advance(7)
+    conv_taps(acc, cat, w1_v, (0, 2), True, NN)
+    gain1, bias1 = vec[0:1, :], vec[3:4, :]
+
+    def pre_grad(i):
+        where = chunk_of(i)
+        value = acc[where, :] * swish_slope(scaled1(i) * gain1 + bias1)
+        acc[where, :] = value
+        return value
+
+    first, cross = sums(scaled1, pre_grad)
+    copies = exchange(2, [first, cross, keep[1:2, :], keep[3:4, :], keep[0:1, :], keep[2:3, :],
+                          gob[0:1, :]])
+    reduce.advance(4)
+    reduce.advance(2)
+    reduce.advance(5)
+    for copy in copies:
+        copy.wait()
+    total1 = slots_total(slots.at[2])
+    means1 = group_means(total1, gain1)
+    inverse1 = st[1:2, :]
+
+    @pl.loop(0, CHUNKS)
+    def _(i):
+        where = chunk_of(i)
+        value = drs_v[where, :] + inverse1 * (
+            acc[where, :] * gain1 - means1[0:1] - scaled1(i) * means1[1:2])
+        img_b[where, :] = value.astype(BF)
+
+    band_back_send(me, img_b, back, bs, br)
+    u2, v2 = keep[16:17, :], keep[17:18, :]
+    keep[24:40, :] = jnp.concatenate(
+        [total1[1:2], total1[0:1], scale * v2, scale * u2, keep[9:10, :], keep[8:9, :],
+         total1[2:7], gain2 * v2 + bias2 * u2, u2, jnp.zeros((3, C), F32)], axis=0)
+    own_cols = pl.ds(pl.multiple_of(me.c * 128, 128), 128)
+    zsl[me.z] = keep[24:40, own_cols]
+    zcopies = [
+        send(zsl.at[me.z], zsl.at[me.z], zs.at[t], zr.at[t],
+             (2 * lax.rem(me.z + t, 4) + me.k, me.c))
+        for t in range(1, 4)
+    ]
+    for group in (3, 6, 7, 4, 2, 5, 3, 6, 7, 4, 2, 5, 3, 6, 7, 4, 5, 6, 7, 5, 6, 7, 6, 7):
+        if reduce.copies[group][0] < 6:
+            reduce.advance(group)
+    band_back_wait(me, img_b, back, bs, br)
+    gimg_o[...] = back[...].astype(F32)
+    for copy in zcopies:
+        copy.wait()
+    zv_o[...] = zsl[...]
+    for group in range(8):
+        while reduce.copies[group][0] < 6:
+            reduce.advance(group)
+    local(total, fin_o, osem.at[0]).wait()
+
+
+def back(*args):
+    shared = [
+        ((3, C, PIX), BF), ((PIX, C), BF), ((3, PAD, C), BF), ((PIX, C), F32), ((3, PAD, C), BF),
+        ((PIX, C), F32), ((PIX, C), BF), ((PIX, C), F32), ((9, C, C), BF), ((9, C, C), BF),
+        ((3, C, C), BF), ((3, PAD, C), BF), ((C, PIX), BF), ((PIX, C), F32), ((C, C), BF),
+        ((3, 8, 8, C), F32), ((2, 2, 64, C), BF), ((40, C), F32), ((PIX, C), BF),
+        ((4, PIX, 128), BF), ((4, 16, 128), F32),
+        ((TAPS, 4, 2, 64, C), BF), ((TAPS, 4, 64, C), BF), ((3, TAPS, 64, C), BF),
+        ((TAPS, 64, C), BF), ((3, TAPS, 16, C), BF), ((TAPS, 2, 4, 16, C), BF),
+    ]
+    return pl.pallas_call(
+        back_kernel,
+        name="back",
+        out_shape=[
+            jax.ShapeDtypeStruct((4, PIX, 128), F32),
+            jax.ShapeDtypeStruct((4, 16, 128), F32),
+            jax.ShapeDtypeStruct((TAPS, 2, 4, 16, C), BF),
+        ],
+        in_specs=[ANY, VMEM, VMEM] + [ANY] * 11 + [VMEM],
+        out_specs=[VMEM, VMEM, ANY],
+        scratch_shapes=[pltpu.VMEM(*one) for one in shared]
+        + [
+            DMA((8,)), DMA((8,)), DMA((3, 8)), DMA((3, 8)), DMA((2, 2)), DMA((2, 2)),
+            DMA((4,)), DMA((4,)), DMA((4,)), DMA((4,)), DMA((8,)), DMA((8,)), DMA((8, 4)),
+            DMA((8, 4)), DMA((8, 4)), DMA((8, 4)), DMA((8, 4)), DMA((8, 4)), DMA((8,)),
+            DMA((8,)), DMA((12,)), DMA((1,)),
+        ],
+        compiler_params=pltpu.CompilerParams(
+            collective_id=3, has_side_effects=True, vmem_limit_bytes=VMEM_LIMIT
+        ),
+    )(*args)
+
+
+def plane_body(
+    image, target, time_index, loss_weight, clip_embed, clip_tokens, norm_gain, norm_bias,
+    conv1_w, conv2_w, conv_bias, emb_w, emb_b, qkv_w, qv_bias, ctx_w, ctx_b, out_w, out_b,
+):
+    row = lax.axis_index("row")
+    z, k = row // 2, row % 2
+    feat = swish(time_features(time_index, EMB) + clip_embed.astype(F32)).astype(BF)
+    cond = jnp.einsum("ne,jde->njd", feat, emb_w, preferred_element_type=F32) + emb_b
+    weight_row = jnp.broadcast_to(lax.dynamic_slice_in_dim(loss_weight, z, 1), (1, 128))
+    vec = jnp.concatenate([
+        norm_gain, norm_bias, conv_bias, qv_bias, out_b[None],
+        lax.dynamic_index_in_dim(cond, z, 0, False), weight_row, jnp.zeros((2, 128), F32)])
+    tokens = lax.dynamic_index_in_dim(clip_tokens, z, 0, False)
+    ctx = jnp.einsum("jde,te->jdt", ctx_w, tokens, preferred_element_type=F32) + ctx_b[:, :, None]
+    ctx = lax.dynamic_slice_in_dim(ctx, k * HEAD, HEAD, 1).astype(BF)
+    ctx = jnp.pad(ctx, ((0, 0), (0, 0), (0, 128 - CTX)))
+    x, tgt, vec_all, st, a1, hid, a2, res, nrm, w1, w2, wq, wo, qkv = front(
+        image.reshape(4, PIX, 128), target.reshape(4, PIX, 128), vec,
+        conv1_w.reshape(9, 128, C), conv2_w.reshape(9, 128, C), qkv_w, out_w[None])
+    p, pc, o, ot, linv = attend(qkv, ctx)
+    result, cot, gwo, gob, dot_ = middle(ot, res, tgt, wo, vec_all)
+    dqkv, dctx = attend_back(qkv, ctx, p, pc, o, linv, dot_)
+    dctx = lax.all_gather(dctx[:, :CTX, :HEAD], "row", axis=0, tiled=False)
+    gimg, zv, fin = back(dqkv, vec_all, st, x, a1, hid, a2, res, nrm, cot, w1, w2, wq,
+                         gwo.reshape(4, 2, 64, C), gob)
+    dctx = dctx.reshape(4, 2, 2, CTX, HEAD)
+    dctx = jnp.transpose(dctx, (0, 3, 2, 1, 4)).reshape(4, CTX, 2, 128)
+    grad_ctx_w = jnp.einsum("nte,ntjd->jde", clip_tokens.astype(F32), dctx, precision=HIGH)
+    sums = jnp.sum(zv, axis=0)
+    dcond = zv[:, 11:13]
+    grad_emb_w = jnp.einsum("ne,njd->jde", feat.astype(F32), dcond, precision=HIGH)
+    fin = fin.reshape(TAPS, 128, C).astype(F32)
+    return (
+        result.reshape(image.shape),
+        gimg.reshape(image.shape),
+        jnp.stack([sums[0], sums[2], sums[4]]),
+        jnp.stack([sums[1], sums[3], sums[5]]),
+        fin[13:22].reshape(3, 3, 128, C),
+        fin[4:13].reshape(3, 3, 128, C),
+        sums[6:8],
+        grad_emb_w,
+        jnp.sum(dcond, axis=0),
+        fin[1:4],
+        sums[8:10],
+        grad_ctx_w,
+        jnp.sum(dctx, axis=(0, 1)),
+        fin[0],
+        sums[10],
+    )
+
+
 def solution(mesh):
+    sizes = dict(mesh.shape)
+    planes = sizes["row"] == 8 and sizes["chan"] == 4
     return jax.shard_map(
-        body,
+        plane_body if planes else general_body,
         mesh=mesh,
         in_specs=(
-            P(None, "row", None, "chan"),
-            P(None, "row", None, "chan"),
-            P(),
-            P(),
-            P(),
-            P(),
-            P(None, "chan"),
-            P(None, "chan"),
-            P(None, None, "chan", None),
-            P(None, None, "chan", None),
-            P(None, "chan"),
-            P(None, "chan", None),
-            P(None, "chan"),
-            P(None, "chan", None),
-            P(None, "chan"),
-            P(None, "chan", None),
-            P(None, "chan"),
-            P("chan", None),
-            P("chan"),
+            P(None, "row", None, "chan"), P(None, "row", None, "chan"), P(), P(), P(), P(),
+            P(None, "chan"), P(None, "chan"), P(None, None, "chan", None),
+            P(None, None, "chan", None), P(None, "chan"), P(None, "chan", None),
+            P(None, "chan"), P(None, "chan", None), P(None, "chan"), P(None, "chan", None),
+            P(None, "chan"), P("chan", None), P("chan"),
         ),
         out_specs=(
-            P(None, "row", None, "chan"),
-            P(None, "row", None, "chan"),
-            P(None, "chan"),
-            P(None, "chan"),
-            P(None, None, "chan", None),
-            P(None, None, "chan", None),
-            P(None, "chan"),
-            P(None, "chan", None),
-            P(None, "chan"),
-            P(None, "chan", None),
-            P(None, "chan"),
-            P(None, "chan", None),
-            P(None, "chan"),
-            P("chan", None),
-            P("chan"),
+            P(None, "row", None, "chan"), P(None, "row", None, "chan"), P(None, "chan"),
+            P(None, "chan"), P(None, None, "chan", None), P(None, None, "chan", None),
+            P(None, "chan"), P(None, "chan", None), P(None, "chan"), P(None, "chan", None),
+            P(None, "chan"), P(None, "chan", None), P(None, "chan"), P("chan", None), P("chan"),
         ),
         check_vma=False,
     )

time: 1380 us -> 438 us (0.32)
  waiting for transfers between devices: 532 us -> 0 us
  Pallas kernels: 0 us -> 392 us
  matrix products: 287 us -> 7.47 us
  blocking collectives: 183 us -> 13.9 us
  other arithmetic: 160 us -> 4.33 us
  local copies, waits for them, and re-layouts: 133 us -> 18.5 us
  starting transfers between devices: 58.2 us -> 0 us
  between operations: 15.9 us -> 0.77 us
    pallas_call x0 -> x5, Pallas kernels: none -> 392 us  [the longest x1 162 us: back(): pl.pallas_call(back_kernel, name='back', out_shape=[jax.ShapeDtypeStruct(...]
    dot_general x152 -> x4, matrix products: 287 us -> 7.47 us  [the longest x1 2.37 us: plane_body(): jnp.einsum('ne,njd->jde', feat.astype(F32), dcond, precision=HIGH)]
    all_gather x12 -> x0, waiting for transfers between devices: 255 us -> none  [the longest x8 204 us: all_channels(): return lax.all_gather(source, 'chan', axis=3, tiled=True)]
    psum x13 -> x0, blocking collectives: 183 us -> none  [the longest x6 84.6 us: norm_forward(): first_sum, square_sum = lax.psum((first_sum, square_sum), 'row')]
    while x32 -> x0, waiting for transfers between devices: 150 us -> none
    psum x1 -> x0, waiting for transfers between devices: 92.4 us -> none  [body(): lax.psum(sum_conv_one.astype(jnp.bfloat16), 'row').astype(jnp.float32)]
    convert_element_type x40 -> x1, other arithmetic: 86.8 us -> 0.08 us  [plane_body(): ctx = lax.dynamic_slice_in_dim(ctx, k * HEAD, HEAD, 1).astype(BF)]
    while x508 -> x0, local copies, waits for them, and re-layouts: 79.6 us -> none
  transfers between devices with their start and end apart: 41 -> 0, of which waited for: 29 -> 0; matrix products, arithmetic and copies ran while one was open for 22% -> 0% of each run, Pallas kernels for 0% -> 0%
where the time goes in v1:
time: 438 us; the launch traced here: 437 us
  Pallas kernels  392 us (89%)
  local copies, waits for them, and re-layouts  18.5 us (4%)
  blocking collectives  13.9 us (3%)
  matrix products  7.47 us (2%)
    pallas_call x1, Pallas kernels, back(): pl.pallas_call(back_kernel, name='back', out_shape=[jax.ShapeDtypeStruct(...  162 us
    pallas_call x1, Pallas kernels, front(): pl.pallas_call(front_kernel, name='front', out_shape=[jax.ShapeDtypeStruc...  120 us
    pallas_call x1, Pallas kernels, attend(): pl.pallas_call(attend_kernel, name='attend', grid=(pixels // QBLOCK,), ou...  41.3 us
    pallas_call x1, Pallas kernels, attend_back(): pl.pallas_call(attend_back_kernel, name='attend_back', grid=(pixels // KB...  39.7 us
    pallas_call x1, Pallas kernels, middle(): pl.pallas_call(middle_kernel, name='middle', out_shape=[jax.ShapeDtypeStr...  28.8 us
    all_gather x1, blocking collectives, plane_body(): dctx = lax.all_gather(dctx[:, :CTX, :HEAD], 'row', axis=0, tiled=False)  13.9 us

profile of v1, /device:TPU:7, one launch (start us, length us, event | category | flops | bytes accessed | tf_op | source)
XLA Modules:
  0.0 436.8 jit_solution(5684484172341142355)
XLA Ops:
  0.7 1.3 dynamic_slice.17
  2.0 0.6 broadcast_in_dim.9
  2.7 0.7 convert_element_type.23
  3.3 0.7 constant_dynamic-slice_fusion
  4.3 1.1 fusion.8
  5.4 0.7 dynamic-slice_add_fusion.1
  6.1 2.6 concatenate.7.vec
  8.7 1.6 fusion.4
  11.1 119.6 %front.1 = (bf16[512,512]{1,0:T(8,128)(2,1)}, bf16[512,512]{1,0:T(8,128)(2,1)}, f32[16,512]{1,0:T(8,128)}, f32[8,512]{1,0:T(8,128)}, bf16[3,640,512]{2,1,0:T(8,1...) custom-call(bf16[4,512,128]{2,1,0:T(8,128)(2,1)} %bitcast.49, ...), custom_call_target="tpu_custom_call" | custom-call | tf_op jit(solution)/shard_map/front/pallas_call | solution.py:892
  130.7 41.3 %attend.1 = (bf16[4096,4096]{1,0:T(8,128)(2,1)}, bf16[16,4096]{1,0:T(8,128)(2,1)}, f32[64,4096]{1,0:T(8,128)}, bf16[64,4096]{1,0:T(8,128)(2,1)}, f32[8,4096]{1,0:T(8,128)}) custom-call(bf16[3,64,4096]{2,1,0:T(8,128)(2,1)} %get-tuple-element.44.qkv, bf16[2,64,128]{2,1,0:T(8,128)(2,1)} %pad.4.ctx), custom_call_target="tpu_custom_call" | custom-call | tf_op jit(solution)/shard_map/attend/pallas_call | solution.py:962
  172.0 28.8 %middle.1 = (f32[4,512,128]{2,1,0:T(8,128)}, f32[512,512]{1,0:T(8,128)}, bf16[512,512]{1,0:T(8,128)(2,1)}, f32[8,512]{1,0:T(8,128)}, bf16[64,4096]{1,0:T(8,128)(2,1)}) custom-call(bf16[64,4096]{1,0:T(8,128)(2,1)} %get-tuple-element.45.ot, f32[512,512]{1,0:T(8,128)} %get-tuple-element.46.res, bf16[512,512]{1,0:T(8,128)(2,1)} %get-tuple-element.47.tgt, ...), custom_call_target="tpu_custom_call" | custom-call | tf_op jit(solution)/shard_map/middle/pallas_call | solution.py:1098
  200.9 39.7 %attend_back.1 = (bf16[3,64,4096]{2,1,0:T(8,128)(2,1)}, f32[2,16,128]{2,1,0:T(8,128)}) custom-call(bf16[3,64,4096]{2,1,0:T(8,128)(2,1)} %get-tuple-element.44.qkv, bf16[2,64,128]{2,1,0:T(8,128)(2,1)} %pad.4.ctx, bf16[4096,4096]{1,0:T(8,128)(2,1)} %get-tuple-element.51.p, bf16[16,4096]{1,0:T(8,128)(2,1)} %get-tuple-element.52.pc, ...), custom_call_target="tpu_custom_call" | custom-call | tf_op jit(solution)/shard_map/attend_back/pallas_call | solution.py:1180
  240.6 162.2 %back.1 = (f32[4,512,128]{2,1,0:T(8,128)}, f32[4,16,128]{2,1,0:T(8,128)}, bf16[22,2,4,16,512]{4,3,2,1,0:T(8,128)(2,1)}) custom-call(bf16[3,64,4096]{2,1,0:T(8,128)(2,1)} %get-tuple-element.56.dqkv, f32[16,512]{1,0:T(8,128)} %get-tuple-element.49.vec, f32[8,512]{1,0:T(8,128)} %get-tuple-element.57.st, bf16[512,512]{1,0:T(8,128)(2,1)} %get-tuple-element.58.x, ...), custom_call_target="tpu_custom_call" | custom-call | tf_op jit(solution)/shard_map/back/pallas_call | solution.py:1552
  402.8 0.7 slice.64
  403.5 1.3 slice_reduce_fusion
  404.8 0.8 reduce_sum.29
  407.3 13.9 %all-gather = f32[16,4,64]{2,1,0:T(4,128)S(1)} all-gather(f32[2,4,64]{2,1,0:T(4,128)S(1)} %slice.64), channel_id=2, replica_groups=mesh['row'=8,'chan'=4] {'row'}, dimensions={0}, use_global_device_ids=true | all-gather | bytes 18432 | tf_op jit(solution)/shard_map/all_gather | solution.py:1597
  422.0 1.6 slice.78
  423.6 2.0 slice.76
  425.6 4.5 %fusion.15 = (f32[9,2,4,16,512]{4,3,2,1,0:T(8,128)}, f32[9,2,4,16,512]{4,3,2,1,0:T(8,128)}) fusion(bf16[22,2,4,16,512]{4,3,2,1,0:T(8,128)(2,1)} %get-tuple-element.71), kind=kLoop, calls=%fused_computation.26 | loop fusion | bytes 9437184 | tf_op jit(solution)/shard_map/slice | solution.py:1613
  430.1 2.4 fusion.6
  432.5 2.4 convolution_bitcast_fusion
  434.8 1.0 copy.50
  435.8 1.0 copy.51
  (25 shorter events, 3.4 us)
Async XLA Ops:
  0.6 3.7 copy-start
  425.6 4.5 %copy-start.4 = (bf16[4,2048]{1,0:T(4,128)(2,1)S(1)}, bf16[4,2048]{1,0:T(4,128)(2,1)}, u32[]{:S(2)}) copy-start(bf16[4,2048]{1,0:T(4,128)(2,1)} %param.23) | copy-start | bytes 49156
  430.1 2.4 copy-start.5
  430.1 4.7 %copy-start.2 = (f32[4,512,128]{2,1,0:T(8,128)S(1)}, f32[4,512,128]{2,1,0:T(8,128)}, u32[]{:S(2)}) copy-start(f32[4,512,128]{2,1,0:T(8,128)} %get-tuple-element.50) | copy-start | bytes 3145732
  432.5 3.3 copy-start.3
  432.5 4.3 copy-start.1

commit v2 on v1

--- a/solution.py
+++ b/solution.py
@@ -669,21 +669,112 @@
         acc[...] += mm(cat[col, pl.ds(start, PIX), :], weight[tap], dims)
 
 
+LOG2E = 1.4426950408889634
+VROWS = 80
+SUB = 256
+KEYS = 512
+
+
 def image_targets(me):
     return [(n, (2 * n + me.k, lax.rem(me.z + n, 4))) for n in range(4)]
 
 
+class Gather:
+    def __init__(self, me, index, src, dst, sems):
+        self.me, self.src, self.dst = me, src, dst
+        third = src.shape[0] // 3
+        odd = lax.rem(me.z, 2)
+        self.plane_taps = pl.ds(third * odd, 2 * third)
+        self.give_taps = pl.ds(2 * third * odd, third)
+        self.take_taps = pl.ds(2 * third * (1 - odd), third)
+        self.x = me.c + 1 - 2 * lax.rem(me.c, 2)
+        self.y = lax.rem(me.c + 2, 4)
+        self.far = lax.rem(self.x + 2, 4)
+        self.core = (me.r + 1 - 2 * me.k, me.c)
+        self.over = (2 * (me.z + 1 - 2 * odd) + me.k, me.c)
+        (self.own, self.first_s, self.first_r, self.relay_s, self.relay_r, self.give_s,
+         self.give_r, self.core_s, self.core_r) = [sem.at[index] for sem in sems]
+        self.started = []
+        self.core_plane = []
+        self.core_take = []
+        self.gives = []
+
+    def rows(self, chan, start=0, size=64):
+        return pl.ds(pl.multiple_of(chan * 128 + self.me.k * 64 + start, size), size)
+
+    def move(self, taps, rows, s, r, device):
+        piece = self.dst.at[taps, rows, :]
+        return send(piece, piece, s, r, device)
+
+    def start(self):
+        me = self.me
+        half = pl.ds(pl.multiple_of(me.k * 64, 64), 64)
+        quarter = pl.ds(pl.multiple_of(me.c * 128, 128), 128)
+        for j, chan in enumerate((self.x, self.y)):
+            self.started.append(
+                send(self.src.at[self.plane_taps, half, :],
+                     self.dst.at[self.plane_taps, self.rows(me.c), :],
+                     self.first_s.at[j], self.first_r.at[j], (me.r, chan)))
+        self.kept = local(self.src, self.dst.at[:, quarter, :], self.own.at[0])
+
+    def spread(self, slot, chan):
+        self.core_plane.append(
+            self.move(self.plane_taps, self.rows(chan), self.core_s.at[slot], self.core_r.at[slot],
+                      self.core))
+        self.gives.append(
+            self.move(self.give_taps, self.rows(chan), self.give_s.at[slot], self.give_r.at[slot],
+                      self.over))
+
+    def relay(self):
+        self.relays = []
+        for j, (chan, onward) in enumerate(((self.x, self.y), (self.y, self.x))):
+            self.started[j].wait_recv()
+            self.relays.append(
+                self.move(self.plane_taps, self.rows(chan, 32 * j, 32), self.relay_s.at[j],
+                          self.relay_r.at[j], (self.me.r, onward)))
+            self.spread(j, chan)
+
+    def relayed(self):
+        for copy in self.relays:
+            copy.wait_recv()
+        self.spread(2, self.far)
+
+    def plane_done(self):
+        self.kept.wait()
+        for copy in self.core_plane:
+            copy.wait_recv()
+
+    def take(self):
+        for slot, chan in enumerate((self.x, self.y, self.far)):
+            self.gives[slot].wait_recv()
+            self.core_take.append(
+                self.move(self.take_taps, self.rows(chan), self.core_s.at[3 + slot],
+                          self.core_r.at[3 + slot], self.core))
+
+    def take_done(self):
+        for copy in self.core_take:
+            copy.wait_recv()
+
+    def drain(self):
+        for copy in self.started + self.relays + self.gives + self.core_plane + self.core_take:
+            copy.wait_send()
+
+
 def front_kernel(
-    img, tgt, vec, w1, w2, wq, wo,
+    img, tgt, vec, feat, tokens, emb_w, emb_b, ctx_w, ctx_b, w1, w2, wq, wo,
     x_o, t_o, vec_o, st_o, a1_o, hid_o, a2_o, res_o, nrm_o, w1_o, w2_o, wq_o, wo_o, qkv_o,
+    attn_o, p_o, ctx_o, pc_o, o_o, linv_o,
     x_v, t_v, vec_v, st_v, a1_v, hid_v, a2_v, res_v, nrm_v, w1_v, w2_v, wq_v, wo_v, qkv_v,
-    msg, groups, slots, halo,
-    vs, vr, ims, imr, tgs, tgr, ws, wr, fs, fr, wl, sts, str_, hs, hr, qs, qr, lsem, osem,
+    attn_v,
+    msg, groups, slots, halo, vsrc, cond, keys, ckeys, qs, vext, cvext, sbuf, mbuf, cbuf, pb, ob,
+    vs, vr, ims, imr, tgs, tgr, own_sem, first_s, first_r, relay_s, relay_r, give_s, give_r,
+    core_s, core_r, wos, wor, wofs, wofr, wol, sts, str_, hs, hr, qs_s, qs_r, lsem, osem, psem,
+    as_, ar,
 ):
     me = Place()
     barrier = pltpu.get_barrier_semaphore()
     greet_plane(me, barrier)
-    own_block = jnp.logical_and(me.c == lax.rem(2 * me.z, 4), True)
+    own_block = me.c == lax.rem(2 * me.z, 4)
     for chan in range(4):
         itself = jnp.logical_and(me.pair == me.z, me.c == chan)
 
@@ -693,14 +784,37 @@
                 barrier, inc=1, device_id=(2 * me.pair + me.k, chan), device_id_type=MESH_ID
             )
 
-    pl.semaphore_wait(barrier, 7 + 4 - jnp.where(own_block, 1, 0))
+    odd = lax.rem(me.z, 2)
+    pl.semaphore_signal(
+        barrier, inc=1, device_id=(2 * (me.z + 1 - 2 * odd) + me.k, me.c), device_id_type=MESH_ID
+    )
+    for j in range(2):
+        cond[j] = mm(feat[...], emb_w[j], NT) + emb_b[j : j + 1, :]
+    vsrc[0:11, :] = vec[0:11, :]
+    vsrc[11:12, :] = cond[0, pl.ds(me.z, 1), :]
+    vsrc[12:13, :] = cond[1, pl.ds(me.z, 1), :]
+    vsrc[13:16, :] = vec[13:16, :]
+    lane = lax.broadcasted_iota(jnp.int32, (16, 128), 1)
+    for j in range(2):
+        value = mm(tokens[...], ctx_w[j], NT) + ctx_b[j : j + 1, :]
+        turned = pltpu.roll(value, HEAD, 1)
+        first = lax.div(lane, HEAD) == me.k
+        both = jnp.where(first, value, turned)
+        ctx_o[j] = both.astype(BF)
+        if j == 0:
+            ckeys[...] = both.astype(BF)
+        else:
+            wide = jnp.concatenate([both, jnp.zeros((112, 128), F32)], axis=0)
+            cvext[0:HEAD, :] = jnp.transpose(wide)[0:HEAD].astype(BF)
+    row = lax.broadcasted_iota(jnp.int32, (16, H * W), 0)
+    vext[HEAD:, :] = jnp.where(row == 0, 1.0, 0.0).astype(BF)
+    cvext[HEAD:, :] = jnp.where(row[:, 0:128] == 0, 1.0, 0.0).astype(BF)
+    pl.semaphore_wait(barrier, 8 + 4 - jnp.where(own_block, 1, 0))
     own_cols = pl.ds(pl.multiple_of(me.c * 128, 128), 128)
-    half = pl.ds(pl.multiple_of(me.c * 128 + me.k * 64, 64), 64)
-    my_half = pl.ds(pl.multiple_of(me.k * 64, 64), 64)
-
-    vec_v[:, own_cols] = vec[...]
+
+    vec_v[:, own_cols] = vsrc[...]
     vec_copies = [
-        send(vec, vec_v.at[:, own_cols], vs.at[t], vr.at[t], (me.r, lax.rem(me.c + t, 4)))
+        send(vsrc, vec_v.at[:, own_cols], vs.at[t], vr.at[t], (me.r, lax.rem(me.c + t, 4)))
         for t in range(1, 4)
     ]
 
@@ -733,47 +847,21 @@
                     recv_sem=rsem.at[me.c], device_id=device, device_id_type=MESH_ID,
                 ).wait_send()
 
-    def weight_send(index, src, dst):
-        local(src, dst.at[:, own_cols, :], wl.at[index])
-        return [
-            send(src.at[:, my_half, :], dst.at[:, half, :], ws.at[index, t], wr.at[index, t],
-                 (me.r, lax.rem(me.c + t, 4)))
-            for t in range(1, 4)
-        ]
-
-    def weight_forward(index, dst, copies):
-        out = []
-        for t in range(1, 4):
-            copies[t - 1].wait_recv()
-            origin = lax.rem(me.c - t + 4, 4)
-            rows = pl.ds(pl.multiple_of(origin * 128 + me.k * 64, 64), 64)
-            out.append(
-                send(dst.at[:, rows, :], dst.at[:, rows, :], fs.at[index, t], fr.at[index, t],
-                     (me.r + 1 - 2 * me.k, me.c))
-            )
-        return out
-
-    def weight_wait(index, src, dst, copies, forwards):
-        for copy in copies:
-            copy.wait_send()
-        for copy in forwards:
-            copy.wait()
-        pltpu.make_async_copy(src, dst.at[:, own_cols, :], wl.at[index]).wait()
+    gather_sems = (own_sem, first_s, first_r, relay_s, relay_r, give_s, give_r, core_s, core_r)
+    gather1 = Gather(me, 0, w1, w1_v, gather_sems)
+    gather2 = Gather(me, 1, w2, w2_v, gather_sems)
+    gather3 = Gather(me, 2, wq, wq_v, gather_sems)
 
     image_send(img, x_v, ims, imr)
-    w1_copies = weight_send(0, w1, w1_v)
+    gather1.start()
     group_matrix(groups)
     col_zero = jnp.zeros((8, C), F32)
     for copy in vec_copies:
         copy.wait()
-    image_wait(img, x_v, ims, imr)
     outs = []
 
     def save(index, src, dst):
         outs.append(local(src, dst, osem.at[index]))
-
-    save(0, x_v, x_o)
-    save(2, vec_v, vec_o)
 
     def statistics(number, ref):
         def add(i, carry):
@@ -794,8 +882,11 @@
         st_v[2 * number + 1 : 2 * number + 2, :] = inverse
         return center, inverse
 
+    image_wait(img, x_v, ims, imr)
     copies = statistics(0, x_v)
-    w2_copies = weight_send(1, w2, w2_v)
+    save(0, x_v, x_o)
+    save(2, vec_v, vec_o)
+    gather1.relay()
     center, inverse = finish_statistics(0, copies)
     gain, bias = vec_v[0:1, :], vec_v[3:4, :]
 
@@ -805,19 +896,21 @@
         put_shifted(a1_v, 64 + i * 64, swish(value * gain + bias))
 
     halo_send(me, a1_v, halo.at[0], hs.at[0], hr.at[0])
+    gather1.relayed()
+    gather2.start()
     hid_v[...] = jnp.broadcast_to(vec_v[6:7, :], (PIX, C))
-    w1_forward = weight_forward(0, w1_v, w1_copies)
-    weight_wait(0, w1, w1_v, w1_copies, w1_forward)
-    save(9, w1_v, w1_o)
-    wq_copies = weight_send(2, wq, wq_v)
+    gather1.plane_done()
     conv_taps(hid_v, a1_v, w1_v, (1,), False, NT)
     halo_wait(me, a1_v, halo.at[0], hs.at[0], hr.at[0])
     save(4, a1_v, a1_o)
-    conv_taps(hid_v, a1_v, w1_v, (0, 2), False, NT)
+    gather1.take()
+    conv_taps(hid_v, a1_v, w1_v, (2 * odd,), False, NT)
+    gather1.take_done()
+    conv_taps(hid_v, a1_v, w1_v, (2 - 2 * odd,), False, NT)
+    copies = statistics(1, hid_v)
+    save(9, w1_v, w1_o)
     save(5, hid_v, hid_o)
-    copies = statistics(1, hid_v)
-    wo_copies = weight_send(3, wo, wo_v)
-    image_send(tgt, t_v, tgs, tgr)
+    gather2.relay()
     center, inverse = finish_statistics(1, copies)
     gain, bias = vec_v[1:2, :], vec_v[4:5, :]
     scale, shift = 1.0 + vec_v[11:12, :], vec_v[12:13, :]
@@ -828,157 +921,218 @@
         put_shifted(a2_v, 64 + i * 64, swish((value * gain + bias) * scale + shift))
 
     halo_send(me, a2_v, halo.at[1], hs.at[1], hr.at[1])
+    gather2.relayed()
+    gather3.start()
     res_v[...] = x_v[...].astype(F32) + vec_v[7:8, :]
-    w2_forward = weight_forward(1, w2_v, w2_copies)
-    weight_wait(1, w2, w2_v, w2_copies, w2_forward)
-    save(10, w2_v, w2_o)
+    gather2.plane_done()
     conv_taps(res_v, a2_v, w2_v, (1,), False, NT)
     halo_wait(me, a2_v, halo.at[1], hs.at[1], hr.at[1])
     save(6, a2_v, a2_o)
-    conv_taps(res_v, a2_v, w2_v, (0, 2), False, NT)
+    gather2.take()
+    gather3.relay()
+    conv_taps(res_v, a2_v, w2_v, (2 * odd,), False, NT)
+    gather2.take_done()
+    gather3.relayed()
+    conv_taps(res_v, a2_v, w2_v, (2 - 2 * odd,), False, NT)
+    copies = statistics(2, res_v)
+    save(10, w2_v, w2_o)
     save(7, res_v, res_o)
-    copies = statistics(2, res_v)
-    wq_forward = weight_forward(2, wq_v, wq_copies)
-    wo_forward = weight_forward(3, wo_v, wo_copies)
-    weight_wait(2, wq, wq_v, wq_copies, wq_forward)
-    save(11, wq_v, wq_o)
+    gather3.take()
     center, inverse = finish_statistics(2, copies)
     gain, bias = vec_v[2:3, :], vec_v[5:6, :]
-    normed = ((res_v[...] - center) * inverse * gain + bias)
+    normed = (res_v[...] - center) * inverse * gain + bias
     nrm_v[...] = normed.astype(BF)
+    st_v[6:8, :] = jnp.zeros((2, C), F32)
     save(8, nrm_v, nrm_o)
     save(3, st_v, st_o)
     turned = jnp.transpose(normed).astype(BF)
-    for j, row in ((0, 8), (1, None), (2, 9)):
+    gather3.plane_done()
+    gather3.take_done()
+    save(11, wq_v, wq_o)
+    band_cols = pl.ds(pl.multiple_of(me.band * PIX, PIX), PIX)
+
+    def head_rows(head):
+        return pl.ds(pl.multiple_of(head * HEAD, HEAD), HEAD)
+
+    owns = []
+    qkv_copies = {}
+    for j, bias_row in ((1, None), (0, 8), (2, 9)):
         value = mm(wq_v[j], turned)
-        if row is not None:
-            wide = jnp.transpose(jnp.broadcast_to(vec_v[row : row + 1, :], (128, C)))
+        if bias_row is not None:
+            wide = jnp.transpose(jnp.broadcast_to(vec_v[bias_row : bias_row + 1, :], (128, C)))
             value = value + jnp.concatenate([wide] * 4, axis=1)
         msg[j] = value.astype(BF)
-
-    band_cols = pl.ds(pl.multiple_of(me.band * PIX, PIX), PIX)
-
-    def head_rows(head):
-        return pl.ds(pl.multiple_of(head * HEAD, HEAD), HEAD)
-
-    own = local(msg.at[:, head_rows(me.d), :], qkv_v.at[:, :, band_cols], lsem.at[0])
-    copies = []
-    for step in range(1, 8):
-        head = lax.rem(me.d + step, 8)
-        copies.append(
-            send(msg.at[:, head_rows(head), :], qkv_v.at[:, :, band_cols], qs.at[step],
-                 qr.at[step], me.head_device(head))
-        )
-    weight_wait(3, wo, wo_v, wo_copies, wo_forward)
-    save(12, wo_v, wo_o)
+        owns.append(local(msg.at[j, head_rows(me.d), :], qkv_v.at[j, :, band_cols], lsem.at[j]))
+        qkv_copies[j] = []
+        for step in range(1, 8):
+            head = lax.rem(me.d + step, 8)
+            qkv_copies[j].append(
+                send(msg.at[j, head_rows(head), :], qkv_v.at[j, :, band_cols], qs_s.at[j, step],
+                     qs_r.at[j, step], me.head_device(head)))
+
+    for own in owns:
+        own.wait()
+    for copy in qkv_copies[1]:
+        copy.wait()
+    both = jnp.concatenate([qkv_v[1], qkv_v[1]], axis=0).astype(F32)
+    keys[...] = jnp.transpose(both).astype(BF)
+    for copy in qkv_copies[0]:
+        copy.wait()
+    scaled = qkv_v[0].astype(F32) * (HEAD ** (-0.5) * LOG2E)
+    top = scaled.astype(BF)
+    qs[0:HEAD, :] = top
+    qs[HEAD:, :] = (scaled - top.astype(F32)).astype(BF)
+    token = lax.broadcasted_iota(jnp.int32, (16, SUB), 0)
+    valid = lax.div(token, CTX) == me.z
+    chunks = H * W // KEYS
+
+    def begin(slot, block):
+        query = qs[:, pl.ds(pl.multiple_of(block * SUB, SUB), SUB)]
+        score = jnp.where(valid, mm(ckeys[...], query), -1e30)
+        cbuf[slot] = score
+        return query, jnp.maximum(score[0:8], score[8:16])
+
+    def score_chunk(slot, query, highest, chunk):
+        value = mm(keys[chunk * KEYS : (chunk + 1) * KEYS, :], query)
+        sbuf[slot, chunk * KEYS : (chunk + 1) * KEYS, :] = value
+        return jnp.maximum(highest, jnp.max(value.reshape(KEYS // 8, 8, SUB), axis=0))
+
+    query, highest = begin(0, 0)
+    for chunk in range(chunks):
+        highest = score_chunk(0, query, highest, chunk)
+    mbuf[0] = highest
+    for copy in qkv_copies[2]:
+        copy.wait()
+    vext[0:HEAD, :] = qkv_v[2]
+    save(13, qkv_v, qkv_o)
+    image_send(tgt, t_v, tgs, tgr)
+    half = pl.ds(pl.multiple_of(me.c * 128 + me.k * 64, 64), 64)
+    my_half = pl.ds(pl.multiple_of(me.k * 64, 64), 64)
+    wo_own = local(wo, wo_v.at[:, own_cols, :], wol.at[0])
+    wo_copies = [
+        send(wo.at[:, my_half, :], wo_v.at[:, half, :], wos.at[t], wor.at[t],
+             (me.r, lax.rem(me.c + t, 4)))
+        for t in range(1, 4)
+    ]
+    attn_rows = head_rows(me.d)
+
+    def p_copy(block, slot):
+        return pltpu.make_async_copy(
+            pb.at[slot], p_o.at[:, pl.ds(pl.multiple_of(block * PIX, PIX), PIX)], psem.at[slot])
+
+    @pl.loop(0, 8)
+    def _(block):
+        slot = lax.rem(block, 2)
+
+        @pl.when(block >= 2)
+        def _():
+            p_copy(block - 2, slot).wait()
+
+        for sub in range(2):
+            cols = pl.ds(sub * SUB, SUB)
+            wide = pl.ds(pl.multiple_of(block * PIX + sub * SUB, SUB), SUB)
+            following = jnp.minimum(2 * block + sub + 1, H * W // SUB - 1)
+            top = jnp.max(mbuf[sub], axis=0, keepdims=True)
+            pc = jnp.exp2(cbuf[sub] - top).astype(BF)
+            pc_o[:, wide] = pc
+            out = mm(cvext[:, 0:16], pc)
+            query, highest = begin(1 - sub, following)
+            for chunk in range(chunks):
+                highest = score_chunk(1 - sub, query, highest, chunk)
+                rows = slice(chunk * KEYS, (chunk + 1) * KEYS)
+                probs = jnp.exp2(sbuf[sub, rows, :] - top).astype(BF)
+                pb[slot, rows, cols] = probs
+                out = out + mm(vext[:, rows], probs)
+            mbuf[1 - sub] = highest
+            linv = 1.0 / out[HEAD : HEAD + 1]
+            out = out[0:HEAD] * linv
+            o_o[:, wide] = out
+            ob[block, :, cols] = out.astype(BF)
+            linv_o[:, wide] = jnp.broadcast_to(linv, (8, SUB))
+        p_copy(block, slot).start()
+
+        @pl.when(block != me.band)
+        def _():
+            send(ob.at[block], attn_v.at[attn_rows, :], as_.at[block], ar.at[me.d],
+                 me.band_device(block))
+
+        @pl.when(block == me.band)
+        def _():
+            local(ob.at[block], attn_v.at[attn_rows, :], ar.at[me.d])
+
+    wo_forward = []
+    for t in range(1, 4):
+        wo_copies[t - 1].wait()
+        origin = lax.rem(me.c - t + 4, 4)
+        rows = pl.ds(pl.multiple_of(origin * 128 + me.k * 64, 64), 64)
+        wo_forward.append(
+            send(wo_v.at[:, rows, :], wo_v.at[:, rows, :], wofs.at[t], wofr.at[t],
+                 (me.r + 1 - 2 * me.k, me.c)))
     image_wait(tgt, t_v, tgs, tgr)
     save(1, t_v, t_o)
+    for gather in (gather1, gather2, gather3):
+        gather.drain()
     image_drain(img, x_v, ims, imr)
     image_drain(tgt, t_v, tgs, tgr)
-    own.wait()
-    for copy in copies:
+    wo_own.wait()
+    for copy in wo_forward:
         copy.wait()
-    save(13, qkv_v, qkv_o)
+    save(12, wo_v, wo_o)
+    for block in range(8):
+
+        @pl.when(block != me.band)
+        def _():
+            pltpu.make_async_remote_copy(
+                src_ref=ob.at[block], dst_ref=attn_v.at[attn_rows, :], send_sem=as_.at[block],
+                recv_sem=ar.at[me.d], device_id=me.band_device(block), device_id_type=MESH_ID,
+            ).wait_send()
+
+        pltpu.make_async_copy(
+            ob.at[0], attn_v.at[pl.ds(block * HEAD, HEAD), :], ar.at[block]).wait()
+    save(14, attn_v, attn_o)
+    p_copy(6, 0).wait()
+    p_copy(7, 1).wait()
     for copy in outs:
         copy.wait()
 
 
-def front(img, tgt, vec, w1, w2, wq, wo):
+def front(*args):
+    pixels = H * W
     saved = [
         ((PIX, C), BF), ((PIX, C), BF), ((16, C), F32), ((8, C), F32), ((3, PAD, C), BF),
         ((PIX, C), F32), ((3, PAD, C), BF), ((PIX, C), F32), ((PIX, C), BF), ((9, C, C), BF),
-        ((9, C, C), BF), ((3, C, C), BF), ((1, C, C), BF), ((3, HEAD, H * W), BF),
+        ((9, C, C), BF), ((3, C, C), BF), ((1, C, C), BF), ((3, HEAD, pixels), BF), ((C, PIX), BF),
+    ]
+    more = [
+        ((pixels, pixels), BF), ((2, 16, 128), BF), ((16, pixels), BF), ((HEAD, pixels), F32),
+        ((8, pixels), F32),
     ]
     return pl.pallas_call(
         front_kernel,
         name="front",
-        out_shape=[jax.ShapeDtypeStruct(*one) for one in saved],
-        in_specs=[ANY, ANY, VMEM, ANY, ANY, ANY, ANY],
-        out_specs=[ANY] * len(saved),
+        out_shape=[jax.ShapeDtypeStruct(*one) for one in saved + more],
+        in_specs=[ANY, ANY] + [VMEM] * 7 + [ANY] * 4,
+        out_specs=[ANY] * (len(saved) + 1) + [VMEM] * 4,
         scratch_shapes=[pltpu.VMEM(*one) for one in saved]
         + [
             pltpu.VMEM((3, C, C), BF), pltpu.VMEM((C, C), BF), pltpu.VMEM((3, 8, 8, C), F32),
-            pltpu.VMEM((2, 2, 64, C), BF),
+            pltpu.VMEM((2, 2, 64, C), BF), pltpu.VMEM((16, 128), F32),
+            pltpu.VMEM((2, 16, 128), F32), pltpu.VMEM((pixels, 128), BF),
+            pltpu.VMEM((16, 128), BF), pltpu.VMEM((128, pixels), BF),
+            pltpu.VMEM((VROWS, pixels), BF), pltpu.VMEM((VROWS, 128), BF),
+            pltpu.VMEM((2, pixels, SUB), F32), pltpu.VMEM((2, 8, SUB), F32),
+            pltpu.VMEM((2, 16, SUB), F32), pltpu.VMEM((2, pixels, PIX), BF),
+            pltpu.VMEM((8, HEAD, PIX), BF),
             DMA((4,)), DMA((4,)), DMA((4,)), DMA((4,)), DMA((4,)), DMA((4,)),
-            DMA((4, 4)), DMA((4, 4)), DMA((4, 4)), DMA((4, 4)), DMA((4,)),
-            DMA((3, 8)), DMA((3, 8)), DMA((2, 2)), DMA((2, 2)), DMA((8,)), DMA((8,)),
-            DMA((1,)), DMA((14,)),
+            DMA((3, 1)), DMA((3, 2)), DMA((3, 2)), DMA((3, 2)), DMA((3, 2)), DMA((3, 3)),
+            DMA((3, 3)), DMA((3, 6)), DMA((3, 6)), DMA((4,)), DMA((4,)), DMA((4,)), DMA((4,)),
+            DMA((1,)), DMA((3, 8)), DMA((3, 8)), DMA((2, 2)), DMA((2, 2)), DMA((3, 8)),
+            DMA((3, 8)), DMA((3,)), DMA((15,)), DMA((2,)), DMA((8,)), DMA((8,)),
         ],
         compiler_params=pltpu.CompilerParams(
             collective_id=1, has_side_effects=True, vmem_limit_bytes=VMEM_LIMIT
         ),
-    )(img, tgt, vec, w1, w2, wq, wo)
-
-
-LOG2E = 1.4426950408889634
-QBLOCK = 256
-VROWS = 80
-
-
-def attend_kernel(qkv, ctx, p_o, pc_o, o_o, ot_o, linv_o, keys, ckeys, qs, vext, cvext):
-    pixels = H * W
-    i = pl.program_id(0)
-
-    @pl.when(i == 0)
-    def _():
-        both = jnp.concatenate([qkv[1], qkv[1]], axis=0).astype(F32)
-        keys[...] = jnp.transpose(both).astype(BF)
-        cboth = jnp.concatenate([ctx[0], ctx[0]], axis=0).astype(F32)
-        ckeys[...] = jnp.transpose(cboth)[0:16].astype(BF)
-        scaled = qkv[0].astype(F32) * (HEAD ** (-0.5) * LOG2E)
-        top = scaled.astype(BF)
-        qs[0:HEAD, :] = top
-        qs[HEAD:, :] = (scaled - top.astype(F32)).astype(BF)
-        row = lax.broadcasted_iota(jnp.int32, (16, pixels), 0)
-        vext[0:HEAD, :] = qkv[2]
-        vext[HEAD:, :] = jnp.where(row == 0, 1.0, 0.0).astype(BF)
-        cvext[0:HEAD, :] = ctx[1]
-        cvext[HEAD:, :] = jnp.where(row[:, 0:128] == 0, 1.0, 0.0).astype(BF)
-
-    cols = pl.ds(pl.multiple_of(i * QBLOCK, QBLOCK), QBLOCK)
-    query = qs[:, cols]
-    score = mm(keys[...], query)
-    cscore = mm(ckeys[...], query)
-    token = lax.broadcasted_iota(jnp.int32, (16, QBLOCK), 0)
-    cscore = jnp.where(token < CTX, cscore, -1e30)
-    top = jnp.maximum(
-        jnp.max(score, axis=0, keepdims=True), jnp.max(cscore, axis=0, keepdims=True)
-    )
-    p_o[...] = jnp.exp2(score - top).astype(BF)
-    pc = jnp.exp2(cscore - top).astype(BF)
-    pc_o[...] = pc
-    out = mm(vext[...], p_o[...]) + mm(cvext[:, 0:16], pc)
-    linv = 1.0 / out[HEAD : HEAD + 1]
-    out = out[0:HEAD] * linv
-    o_o[...] = out
-    ot_o[...] = out.astype(BF)
-    linv_o[...] = jnp.broadcast_to(linv, (8, QBLOCK))
-
-
-def attend(qkv, ctx):
-    pixels = H * W
-    whole = lambda *shape: pl.BlockSpec(shape, lambda i: (0,) * len(shape))
-    cols = lambda rows: pl.BlockSpec((rows, QBLOCK), lambda i: (0, i))
-    return pl.pallas_call(
-        attend_kernel,
-        name="attend",
-        grid=(pixels // QBLOCK,),
-        out_shape=[
-            jax.ShapeDtypeStruct((pixels, pixels), BF),
-            jax.ShapeDtypeStruct((16, pixels), BF),
-            jax.ShapeDtypeStruct((HEAD, pixels), F32),
-            jax.ShapeDtypeStruct((HEAD, pixels), BF),
-            jax.ShapeDtypeStruct((8, pixels), F32),
-        ],
-        in_specs=[whole(3, HEAD, pixels), whole(2, HEAD, 128)],
-        out_specs=[cols(pixels), cols(16), cols(HEAD), cols(HEAD), cols(8)],
-        scratch_shapes=[
-            pltpu.VMEM((pixels, 128), BF), pltpu.VMEM((16, 128), BF),
-            pltpu.VMEM((128, pixels), BF), pltpu.VMEM((VROWS, pixels), BF),
-            pltpu.VMEM((VROWS, 128), BF),
-        ],
-        compiler_params=pltpu.CompilerParams(vmem_limit_bytes=VMEM_LIMIT),
-    )(qkv, ctx)
+    )(*args)
 
 
 def band_back_send(me, src, dst, ssem, rsem):
@@ -1026,75 +1180,172 @@
 
 
 def middle_kernel(
-    ot, res, tgt, wo, vec,
-    out_o, cot_o, gwo_o, gob_o, dot_o,
-    attn_t, res_v, tgt_v, wo_v, out_b, back, cot_v, dat, dot_v,
-    as_, ar, bs, br, ds_, dr, lsem, osem,
+    attn, res, tgt, wo, vec, qkv, ctx, p, pc, o, linv, tokens,
+    out_o, cot_o, gwo_o, gob_o, dt_o, gcw_o, gcb_o,
+    attn_v, res_v, tgt_v, wo_v, out_b, back, cot_v, dat, dot_v, qkv_v, o_v,
+    vext, cvext, dos, dor, qrow, dq, pb, dkv, dqb, dt_v, dctx, cslots,
+    bs, br, ds_, dr, cs, cr, ks, kr, q_s, q_r, lsem, osem, psem,
 ):
     me = Place()
+    scaling = HEAD ** (-0.5)
     barrier = pltpu.get_barrier_semaphore()
     greet_plane(me, barrier)
     others = greet_back(me, barrier)
+    for step in range(1, 8):
+        pl.semaphore_signal(
+            barrier, inc=1, device_id=(lax.rem(me.r + step, 8), me.c), device_id_type=MESH_ID
+        )
     loads = [local(a, b, lsem.at[j]) for j, (a, b) in enumerate(
-        ((res, res_v), (tgt, tgt_v), (wo.at[0], wo_v)))]
-    pl.semaphore_wait(barrier, 7 + others)
-    mine = pl.ds(pl.multiple_of(me.d * HEAD, HEAD), HEAD)
+        ((attn, attn_v), (wo.at[0], wo_v), (res, res_v), (tgt, tgt_v), (qkv, qkv_v), (o, o_v)))]
+
+    def p_copy(block, slot):
+        return pltpu.make_async_copy(
+            p.at[pl.ds(pl.multiple_of(block * PIX, PIX), PIX), :], pb.at[slot], psem.at[slot])
+
+    p_copy(0, 0).start()
 
     def band_cols(band):
         return pl.ds(pl.multiple_of(band * PIX, PIX), PIX)
 
-    own = local(ot.at[:, band_cols(me.band)], attn_t.at[mine, :], lsem.at[3])
+    def head_rows(head):
+        return pl.ds(pl.multiple_of(head * HEAD, HEAD), HEAD)
+
+    for load in loads[0:4]:
+        load.wait()
+    rows = jnp.transpose(attn_v[...].astype(F32)).astype(BF)
+    result = res_v[...] + mm(rows, wo_v[...], NT) + vec[10:11, :]
+    out_b[...] = result.astype(BF)
+    cot = vec[13:14, :] * (result - tgt_v[...].astype(F32))
+    cot_v[...] = cot
+    low = cot.astype(BF)
+    dat[...] = jnp.transpose(mm(low, wo_v[...])).astype(BF)
+    pl.semaphore_wait(barrier, 14 + others)
+    own = local(dat.at[head_rows(me.d), :], dot_v.at[:, band_cols(me.band)], lsem.at[6])
+    copies = []
+    for step in range(1, 8):
+        head = lax.rem(me.d + step, 8)
+        copies.append(
+            send(dat.at[head_rows(head), :], dot_v.at[:, band_cols(me.band)], ds_.at[step],
+                 dr.at[step], me.head_device(head)))
+    saves = [local(cot_v, cot_o, osem.at[0])]
+    lowf = low.astype(F32)
+    gwo_o[...] = mm(jnp.transpose(lowf).astype(BF), rows).astype(BF)
+    gob_o[...] = jnp.broadcast_to(as_row(lowf), (8, C))
+    for load in loads[4:]:
+        load.wait()
+    row = lax.broadcasted_iota(jnp.int32, (HEAD, H * W), 0)
+    ones = jnp.where(row < 3, 1.0, 0.0)
+    vext[...] = jnp.transpose(jnp.concatenate([qkv_v[2].astype(F32), ones], axis=0)).astype(BF)
+    lane = lax.broadcasted_iota(jnp.int32, (16, 128), 1)
+    cvext[...] = jnp.where(
+        lane < HEAD, ctx[1].astype(F32), jnp.where(lane < HEAD + 3, 1.0, 0.0)).astype(BF)
+    queries = qkv_v[0].astype(F32) * scaling
+    qrow[...] = jnp.transpose(
+        jnp.concatenate([queries, jnp.zeros_like(queries)], axis=0)).astype(BF)
+    own.wait()
+    for copy in copies:
+        copy.wait()
+    band_back_send(me, out_b, back, bs, br)
+    grad = (dot_v[...].astype(F32) * linv[0:1, :]).astype(BF)
+    gradf = grad.astype(F32)
+    delta = -jnp.sum(gradf * o_v[...], axis=0, keepdims=True)
+    top = delta.astype(BF).astype(F32)
+    mid = (delta - top).astype(BF).astype(F32)
+    last = delta - top - mid
+    dos[0:HEAD, :] = grad
+    dos[HEAD:, :] = jnp.where(
+        row == 0, top, jnp.where(row == 1, mid, jnp.where(row == 2, last, 0.0))).astype(BF)
+    dor[...] = jnp.transpose(jnp.concatenate([gradf, jnp.zeros_like(gradf)], axis=0)).astype(BF)
+
+    def score_grads(values, probs):
+        return (probs.astype(F32) * mm(values, dos[...])).astype(BF)
+
+    dsc = score_grads(cvext[...], pc[...])
+    for j, (left, right) in enumerate(((dsc, qrow), (pc[...], dor))):
+        value = mm(left, right[...])
+        dctx[j] = jnp.where(me.k == 0, value, pltpu.roll(value, HEAD, 1))
+    cslots[me.r] = dctx[...]
+    ctx_copies = [
+        send(cslots.at[me.r], cslots.at[me.r], cs.at[step], cr.at[step],
+             (lax.rem(me.r + step, 8), me.c))
+        for step in range(1, 8)
+    ]
+    wide = jnp.concatenate([ctx[0].astype(F32), jnp.zeros((112, 128), F32)], axis=0)
+    dq[...] = mm(jnp.transpose(wide)[0:HEAD, 0:16].astype(BF), dsc)
+    mine = head_rows(me.d)
+
+    @pl.loop(0, 8)
+    def _(block):
+        slot = lax.rem(block, 2)
+
+        @pl.when(block < 7)
+        def _():
+            p_copy(block + 1, 1 - slot).start()
+
+        p_copy(block, slot).wait()
+        grads = []
+        for sub in range(2):
+            part = pl.ds(pl.multiple_of(block * PIX + sub * SUB, SUB), SUB)
+            probs = pb[slot, sub * SUB : (sub + 1) * SUB, :]
+            grads.append(score_grads(vext[part, :], probs))
+            dkv[block, 1, :, sub * SUB : (sub + 1) * SUB] = jnp.transpose(
+                mm(probs, dor[...]))[0:HEAD].astype(BF)
+        for sub in range(2):
+            part = pl.ds(pl.multiple_of(block * PIX + sub * SUB, SUB), SUB)
+            dkv[block, 0, :, sub * SUB : (sub + 1) * SUB] = jnp.transpose(
+                mm(grads[sub], qrow[...]))[0:HEAD].astype(BF)
+            dq[...] += mm(qkv_v[1, :, part], grads[sub])
+
+        @pl.when(block != me.band)
+        def _():
+            send(dkv.at[block], dt_v.at[1:3, mine, :], ks.at[block], kr.at[me.d],
+                 me.band_device(block))
+
+        @pl.when(block == me.band)
+        def _():
+            local(dkv.at[block], dt_v.at[1:3, mine, :], kr.at[me.d])
+
+    dqb[...] = (dq[...] * scaling).astype(BF)
+    own = local(dqb.at[:, band_cols(me.band)], dt_v.at[0, mine, :], q_r.at[me.d])
     copies = []
     for step in range(1, 8):
         band = lax.rem(me.band + step, 8)
         copies.append(
-            send(ot.at[:, band_cols(band)], attn_t.at[mine, :], as_.at[step], ar.at[me.d],
-                 me.band_device(band))
-        )
-    for load in loads:
-        load.wait()
-    own.wait()
+            send(dqb.at[:, band_cols(band)], dt_v.at[0, mine, :], q_s.at[step], q_r.at[me.d],
+                 me.band_device(band)))
+    for copy in ctx_copies:
+        copy.wait()
+    for j in range(2):
+        total = cslots[0, j]
+        for slot in range(1, 8):
+            total = total + cslots[slot, j]
+        gcb_o[j : j + 1, :] = as_row(total)
+        gcw_o[j] = sum(mm(term, tokens[...]) for term in split_rows(total))
+    band_back_wait(me, out_b, back, bs, br)
+    out_o[...] = back[...].astype(F32)
     for copy in copies:
         copy.wait_send()
-    for step in range(1, 8):
-        head = lax.rem(me.d + step, 8)
+    for block in range(8):
+
+        @pl.when(block != me.band)
+        def _():
+            pltpu.make_async_remote_copy(
+                src_ref=dkv.at[block], dst_ref=dt_v.at[1:3, mine, :], send_sem=ks.at[block],
+                recv_sem=kr.at[me.d], device_id=me.band_device(block), device_id_type=MESH_ID,
+            ).wait_send()
+
         pltpu.make_async_copy(
-            ot.at[:, band_cols(0)],
-            attn_t.at[pl.ds(pl.multiple_of(head * HEAD, HEAD), HEAD), :],
-            ar.at[head],
+            dkv.at[0], dt_v.at[1:3, pl.ds(block * HEAD, HEAD), :], kr.at[block]).wait()
+        pltpu.make_async_copy(
+            dqb.at[:, pl.ds(0, PIX)], dt_v.at[0, pl.ds(block * HEAD, HEAD), :], q_r.at[block]
         ).wait()
-    attn = jnp.transpose(attn_t[...].astype(F32)).astype(BF)
-    result = res_v[...] + mm(attn, wo_v[...], NT) + vec[10:11, :]
-    out_b[...] = result.astype(BF)
-    band_back_send(me, out_b, back, bs, br)
-    cot = vec[13:14, :] * (result - tgt_v[...].astype(F32))
-    cot_v[...] = cot
-    saves = [local(cot_v, cot_o, osem.at[0])]
-    low = cot.astype(BF)
-    dat[...] = jnp.transpose(mm(low, wo_v[...])).astype(BF)
-    own = local(dat.at[mine, :], dot_v.at[:, band_cols(me.band)], lsem.at[4])
-    copies = []
-    for step in range(1, 8):
-        head = lax.rem(me.d + step, 8)
-        rows = pl.ds(pl.multiple_of(head * HEAD, HEAD), HEAD)
-        copies.append(
-            send(dat.at[rows, :], dot_v.at[:, band_cols(me.band)], ds_.at[step], dr.at[step],
-                 me.head_device(head))
-        )
-    lowf = low.astype(F32)
-    gwo_o[...] = mm(jnp.transpose(lowf).astype(BF), attn).astype(BF)
-    gob_o[...] = jnp.broadcast_to(as_row(lowf), (8, C))
-    band_back_wait(me, out_b, back, bs, br)
-    out_o[...] = back[...].astype(F32)
-    own.wait()
-    for copy in copies:
-        copy.wait()
-    saves.append(local(dot_v, dot_o, osem.at[1]))
+    saves.append(local(dt_v, dt_o, osem.at[1]))
     for copy in saves:
         copy.wait()
 
 
-def middle(ot, res, tgt, wo, vec):
+def middle(*args):
+    pixels = H * W
     return pl.pallas_call(
         middle_kernel,
         name="middle",
@@ -1103,101 +1354,30 @@
             jax.ShapeDtypeStruct((PIX, C), F32),
             jax.ShapeDtypeStruct((C, C), BF),
             jax.ShapeDtypeStruct((8, C), F32),
-            jax.ShapeDtypeStruct((HEAD, H * W), BF),
+            jax.ShapeDtypeStruct((3, C, PIX), BF),
+            jax.ShapeDtypeStruct((2, 128, CTXW), F32),
+            jax.ShapeDtypeStruct((2, 128), F32),
         ],
-        in_specs=[ANY, ANY, ANY, ANY, VMEM],
-        out_specs=[VMEM, ANY, VMEM, VMEM, ANY],
+        in_specs=[ANY] * 4 + [VMEM, ANY, VMEM, ANY, VMEM, ANY, VMEM, VMEM],
+        out_specs=[VMEM, ANY, VMEM, VMEM, ANY, VMEM, VMEM],
         scratch_shapes=[
             pltpu.VMEM((C, PIX), BF), pltpu.VMEM((PIX, C), F32), pltpu.VMEM((PIX, C), BF),
             pltpu.VMEM((C, C), BF), pltpu.VMEM((PIX, C), BF), pltpu.VMEM((4, PIX, 128), BF),
-            pltpu.VMEM((PIX, C), F32), pltpu.VMEM((C, PIX), BF), pltpu.VMEM((HEAD, H * W), BF),
-            DMA((8,)), DMA((8,)), DMA((4,)), DMA((4,)), DMA((8,)), DMA((8,)), DMA((5,)),
-            DMA((2,)),
+            pltpu.VMEM((PIX, C), F32), pltpu.VMEM((C, PIX), BF), pltpu.VMEM((HEAD, pixels), BF),
+            pltpu.VMEM((3, HEAD, pixels), BF), pltpu.VMEM((HEAD, pixels), F32),
+            pltpu.VMEM((pixels, 128), BF), pltpu.VMEM((16, 128), BF),
+            pltpu.VMEM((128, pixels), BF), pltpu.VMEM((pixels, 128), BF),
+            pltpu.VMEM((pixels, 128), BF), pltpu.VMEM((HEAD, pixels), F32),
+            pltpu.VMEM((2, PIX, pixels), BF), pltpu.VMEM((8, 2, HEAD, PIX), BF),
+            pltpu.VMEM((HEAD, pixels), BF), pltpu.VMEM((3, C, PIX), BF),
+            pltpu.VMEM((2, 16, 128), F32), pltpu.VMEM((8, 2, 16, 128), F32),
+            DMA((4,)), DMA((4,)), DMA((8,)), DMA((8,)), DMA((8,)), DMA((8,)), DMA((8,)),
+            DMA((8,)), DMA((8,)), DMA((8,)), DMA((7,)), DMA((2,)), DMA((2,)),
         ],
         compiler_params=pltpu.CompilerParams(
             collective_id=2, has_side_effects=True, vmem_limit_bytes=VMEM_LIMIT
         ),
-    )(ot, res, tgt, wo, vec)
-
-
-KBLOCK = 256
-
-
-def attend_back_kernel(
-    qkv, ctx, p, pc, o, linv, dot_, dqkv_o, dctx_o, vext, cvext, dos, dor, qrow, dq
-):
-    pixels = H * W
-    i = pl.program_id(0)
-    scaling = HEAD ** (-0.5)
-
-    def score_grads(values, probs):
-        return (probs.astype(F32) * mm(values, dos[...])).astype(BF)
-
-    @pl.when(i == 0)
-    def _():
-        row = lax.broadcasted_iota(jnp.int32, (HEAD, pixels), 0)
-        ones = jnp.where(row < 3, 1.0, 0.0)
-        vext[...] = jnp.transpose(
-            jnp.concatenate([qkv[2].astype(F32), ones], axis=0)
-        ).astype(BF)
-        cvext[...] = jnp.transpose(
-            jnp.concatenate([ctx[1].astype(F32), ones[:, 0:128]], axis=0)
-        )[0:16].astype(BF)
-        grad = (dot_[...].astype(F32) * linv[0:1, :]).astype(BF)
-        gradf = grad.astype(F32)
-        delta = -jnp.sum(gradf * o[...], axis=0, keepdims=True)
-        top = delta.astype(BF).astype(F32)
-        mid = (delta - top).astype(BF).astype(F32)
-        low = delta - top - mid
-        dos[0:HEAD, :] = grad
-        dos[HEAD:, :] = jnp.where(
-            row == 0, top, jnp.where(row == 1, mid, jnp.where(row == 2, low, 0.0))
-        ).astype(BF)
-        dor[...] = jnp.transpose(jnp.concatenate([gradf, jnp.zeros_like(gradf)], axis=0)).astype(BF)
-        qf = qkv[0].astype(F32) * scaling
-        qrow[...] = jnp.transpose(jnp.concatenate([qf, jnp.zeros_like(qf)], axis=0)).astype(BF)
-        probs = pc[...]
-        dsc = score_grads(cvext[...], probs)
-        dctx_o[0] = mm(dsc, qrow[...])
-        dctx_o[1] = mm(probs, dor[...])
-        dq[...] = mm(ctx[0][:, 0:16], dsc)
-
-    cols = pl.ds(pl.multiple_of(i * KBLOCK, KBLOCK), KBLOCK)
-    probs = p[...]
-    ds = score_grads(vext[cols, :], probs)
-    dqkv_o[2, :, cols] = jnp.transpose(mm(probs, dor[...]))[0:HEAD].astype(BF)
-    dqkv_o[1, :, cols] = jnp.transpose(mm(ds, qrow[...]))[0:HEAD].astype(BF)
-    dq[...] += mm(qkv[1, :, cols], ds)
-
-    @pl.when(i == pixels // KBLOCK - 1)
-    def _():
-        dqkv_o[0] = (dq[...] * scaling).astype(BF)
-
-
-def attend_back(qkv, ctx, p, pc, o, linv, dot_):
-    pixels = H * W
-    whole = lambda *shape: pl.BlockSpec(shape, lambda i: (0,) * len(shape))
-    return pl.pallas_call(
-        attend_back_kernel,
-        name="attend_back",
-        grid=(pixels // KBLOCK,),
-        out_shape=[
-            jax.ShapeDtypeStruct((3, HEAD, pixels), BF),
-            jax.ShapeDtypeStruct((2, 16, 128), F32),
-        ],
-        in_specs=[
-            whole(3, HEAD, pixels), whole(2, HEAD, 128),
-            pl.BlockSpec((KBLOCK, pixels), lambda i: (i, 0)),
-            whole(16, pixels), whole(HEAD, pixels), whole(8, pixels), whole(HEAD, pixels),
-        ],
-        out_specs=[whole(3, HEAD, pixels), whole(2, 16, 128)],
-        scratch_shapes=[
-            pltpu.VMEM((pixels, 128), BF), pltpu.VMEM((16, 128), BF),
-            pltpu.VMEM((128, pixels), BF), pltpu.VMEM((pixels, 128), BF),
-            pltpu.VMEM((pixels, 128), BF), pltpu.VMEM((HEAD, pixels), F32),
-        ],
-        compiler_params=pltpu.CompilerParams(vmem_limit_bytes=VMEM_LIMIT),
-    )(qkv, ctx, p, pc, o, linv, dot_)
+    )(*args)
 
 
 TAPS = 22
@@ -1297,13 +1477,22 @@
         return [send(piece, piece, s.at[group], r.at[group], (me.r + 1 - 2 * me.k, me.c))]
 
 
+def split_rows(rows):
+    first = rows.astype(BF).astype(F32)
+    second = (rows - first).astype(BF).astype(F32)
+    stacked = jnp.concatenate([first, second, rows - first - second, jnp.zeros((80, 128), F32)],
+                              axis=0)
+    left = jnp.transpose(stacked).astype(BF)
+    return left[:, 0:16], left[:, 16:32], left[:, 32:48]
+
+
 def back_kernel(
-    dqkv, vec, st, x, a1, hid, a2, res, nrm, cot, w1, w2, wq, gwo, gob,
-    gimg_o, zv_o, fin_o,
+    dt, vec, st, x, a1, hid, a2, res, nrm, cot, w1, w2, wq, gwo, gob, feat,
+    gimg_o, zv_o, fin_o, gemb_o,
     dt_v, x_v, a1_v, hid_v, a2_v, res_v, nrm_v, drs_v, w1_v, w2_v, wq_v,
     cat, turned, acc, groups, slots, halo, keep, img_b, back, zsl,
     part, from_core, from_chan, plane, from_plane, total,
-    as_, ar, ss, sr, hs, hr, bs, br, zs, zr, c1s, c1r, c2s, c2r, p1s, p1r, p2s, p2r, c3s, c3r,
+    ss, sr, hs, hr, bs, br, zs, zr, c1s, c1r, c2s, c2r, p1s, p1r, p2s, p2r, c3s, c3r,
     lsem, osem,
 ):
     me = Place()
@@ -1316,48 +1505,15 @@
             device_id_type=MESH_ID,
         )
     loads = [local(a, b, lsem.at[j]) for j, (a, b) in enumerate((
-        (gwo, part.at[0]), (nrm, nrm_v), (wq, wq_v), (res, res_v), (cot, drs_v), (a2, a2_v),
-        (w2, w2_v), (hid, hid_v), (a1, a1_v), (w1, w1_v), (x, x_v)))]
-    pl.semaphore_wait(barrier, 10 + others)
+        (dt, dt_v), (wq, wq_v), (res, res_v), (gwo, part.at[0]), (nrm, nrm_v), (cot, drs_v),
+        (a2, a2_v), (w2, w2_v), (hid, hid_v), (a1, a1_v), (w1, w1_v), (x, x_v)))]
     reduce = Reduce(me, part, from_core, from_chan, plane, from_plane, total,
                     (c1s, c1r, c2s, c2r, p1s, p1r, p2s, p2r, c3s, c3r))
-    mine = pl.ds(pl.multiple_of(me.d * HEAD, HEAD), HEAD)
-
-    def band_cols(band):
-        return pl.ds(pl.multiple_of(band * PIX, PIX), PIX)
-
-    own = local(dqkv.at[:, :, band_cols(me.band)], dt_v.at[:, mine, :], lsem.at[11])
-    copies = []
-    for step in range(1, 8):
-        band = lax.rem(me.band + step, 8)
-        copies.append(
-            send(dqkv.at[:, :, band_cols(band)], dt_v.at[:, mine, :], as_.at[step], ar.at[me.d],
-                 me.band_device(band))
-        )
     group_matrix(groups)
     zero8 = jnp.zeros((8, C), F32)
     members = 1.0 / (H * W * 16)
     loads[0].wait()
-    reduce.advance(0)
     loads[1].wait()
-    loads[2].wait()
-    own.wait()
-    for copy in copies:
-        copy.wait_send()
-    for step in range(1, 8):
-        head = lax.rem(me.d + step, 8)
-        pltpu.make_async_copy(
-            dqkv.at[:, :, band_cols(0)],
-            dt_v.at[:, pl.ds(pl.multiple_of(head * HEAD, HEAD), HEAD), :],
-            ar.at[head],
-        ).wait()
-
-    @pl.loop(0, 3)
-    def _(j):
-        part[1 + j] = mm(dt_v[j], nrm_v[...]).astype(BF).reshape(4, 2, 64, C)
-
-    reduce.advance(1)
-    reduce.advance(0)
     for j in range(3):
         rows = jnp.transpose(dt_v[j].astype(F32))
         if j != 1:
@@ -1367,7 +1523,7 @@
             acc[...] = value
         else:
             acc[...] += value
-    loads[3].wait()
+    loads[2].wait()
 
     def sums(scaled_of, upstream_of):
         def add(i, carry):
@@ -1386,9 +1542,20 @@
         return plane_exchange(me, slots.at[number], ss.at[number], sr.at[number])
 
     scaled3, scaled2, scaled1 = scaled(res_v, 2), scaled(hid_v, 1), scaled(x_v, 0)
-    copies = exchange(0, sums(scaled3, lambda i: acc[chunk_of(i), :]))
+    rows3 = sums(scaled3, lambda i: acc[chunk_of(i), :])
+    pl.semaphore_wait(barrier, 10 + others)
+    copies = exchange(0, rows3)
+    loads[3].wait()
+    reduce.advance(0)
+    loads[4].wait()
+
+    @pl.loop(0, 3)
+    def _(j):
+        part[1 + j] = mm(dt_v[j], nrm_v[...]).astype(BF).reshape(4, 2, 64, C)
+
     reduce.advance(1)
-    for load in loads[4:]:
+    reduce.advance(0)
+    for load in loads[5:]:
         load.wait()
     for copy in copies:
         copy.wait()
@@ -1412,7 +1579,7 @@
 
     keep[3:4, :] = as_row(lax.fori_loop(0, CHUNKS, resid_grad, zero8))
     halo_send(me, cat, halo.at[0], hs.at[0], hr.at[0])
-    reduce.advance(0)
+    reduce.advance(1)
     turned[...] = jnp.transpose(drs_v[...]).astype(BF)
 
     def weight_grads(group, source):
@@ -1427,19 +1594,14 @@
         reduce.advance(group)
 
     weight_grads(2, a2_v)
-    reduce.advance(1)
     weight_grads(3, a2_v)
-    reduce.advance(2)
     weight_grads(4, a2_v)
     reduce.advance(0)
-    reduce.advance(3)
     acc[...] = jnp.zeros((PIX, C), F32)
     conv_taps(acc, cat, w2_v, (1,), True, NN)
     halo_wait(me, cat, halo.at[0], hs.at[0], hr.at[0])
-    reduce.advance(1)
-    reduce.advance(4)
+    reduce.advance(2)
     conv_taps(acc, cat, w2_v, (0, 2), True, NN)
-    reduce.advance(2)
     gain2, bias2 = vec[1:2, :], vec[4:5, :]
     scale, shift = 1.0 + vec[11:12, :], vec[12:13, :]
 
@@ -1451,8 +1613,8 @@
         return value
 
     copies = exchange(1, sums(scaled2, mod_grad))
+    reduce.advance(1)
     reduce.advance(0)
-    reduce.advance(3)
     for copy in copies:
         copy.wait()
     total2 = slots_total(slots.at[1])
@@ -1470,21 +1632,18 @@
 
     keep[1:2, :] = as_row(lax.fori_loop(0, CHUNKS, hidden_grad, zero8))
     halo_send(me, cat, halo.at[1], hs.at[1], hr.at[1])
+    reduce.advance(3)
     turned[...] = jnp.transpose(acc[...]).astype(BF)
-    reduce.advance(1)
     weight_grads(5, a1_v)
-    reduce.advance(4)
     reduce.advance(2)
     weight_grads(6, a1_v)
-    reduce.advance(5)
-    reduce.advance(3)
+    reduce.advance(1)
     weight_grads(7, a1_v)
-    reduce.advance(6)
-    reduce.advance(1)
+    reduce.advance(0)
+    reduce.advance(4)
     acc[...] = jnp.zeros((PIX, C), F32)
     conv_taps(acc, cat, w1_v, (1,), True, NN)
     halo_wait(me, cat, halo.at[1], hs.at[1], hr.at[1])
-    reduce.advance(7)
     conv_taps(acc, cat, w1_v, (0, 2), True, NN)
     gain1, bias1 = vec[0:1, :], vec[3:4, :]
 
@@ -1497,9 +1656,10 @@
     first, cross = sums(scaled1, pre_grad)
     copies = exchange(2, [first, cross, keep[1:2, :], keep[3:4, :], keep[0:1, :], keep[2:3, :],
                           gob[0:1, :]])
-    reduce.advance(4)
+    reduce.advance(5)
+    reduce.advance(3)
     reduce.advance(2)
-    reduce.advance(5)
+    reduce.advance(1)
     for copy in copies:
         copy.wait()
     total1 = slots_total(slots.at[2])
@@ -1525,14 +1685,22 @@
              (2 * lax.rem(me.z + t, 4) + me.k, me.c))
         for t in range(1, 4)
     ]
-    for group in (3, 6, 7, 4, 2, 5, 3, 6, 7, 4, 2, 5, 3, 6, 7, 4, 5, 6, 7, 5, 6, 7, 6, 7):
-        if reduce.copies[group][0] < 6:
-            reduce.advance(group)
-    band_back_wait(me, img_b, back, bs, br)
-    gimg_o[...] = back[...].astype(F32)
+    for group in (6, 4, 7, 3, 2, 5, 4, 3):
+        reduce.advance(group)
     for copy in zcopies:
         copy.wait()
     zv_o[...] = zsl[...]
+    for j in range(2):
+        rows = jnp.concatenate([zsl[n, 11 + j : 12 + j, :] for n in range(4)]
+                               + [jnp.zeros((12, 128), F32)], axis=0)
+        terms = split_rows(rows)
+        gemb_o[j] = sum(mm(term, feat[...]) for term in terms)
+    for group in (6, 5, 4):
+        reduce.advance(group)
+    band_back_wait(me, img_b, back, bs, br)
+    gimg_o[...] = back[...].astype(F32)
+    for group in (7, 6, 5, 7, 6, 7):
+        reduce.advance(group)
     for group in range(8):
         while reduce.copies[group][0] < 6:
             reduce.advance(group)
@@ -1556,12 +1724,13 @@
             jax.ShapeDtypeStruct((4, PIX, 128), F32),
             jax.ShapeDtypeStruct((4, 16, 128), F32),
             jax.ShapeDtypeStruct((TAPS, 2, 4, 16, C), BF),
+            jax.ShapeDtypeStruct((2, 128, EMB), F32),
         ],
-        in_specs=[ANY, VMEM, VMEM] + [ANY] * 11 + [VMEM],
-        out_specs=[VMEM, VMEM, ANY],
+        in_specs=[ANY, VMEM, VMEM] + [ANY] * 11 + [VMEM, VMEM],
+        out_specs=[VMEM, VMEM, ANY, VMEM],
         scratch_shapes=[pltpu.VMEM(*one) for one in shared]
         + [
-            DMA((8,)), DMA((8,)), DMA((3, 8)), DMA((3, 8)), DMA((2, 2)), DMA((2, 2)),
+            DMA((3, 8)), DMA((3, 8)), DMA((2, 2)), DMA((2, 2)),
             DMA((4,)), DMA((4,)), DMA((4,)), DMA((4,)), DMA((8,)), DMA((8,)), DMA((8, 4)),
             DMA((8, 4)), DMA((8, 4)), DMA((8, 4)), DMA((8, 4)), DMA((8, 4)), DMA((8,)),
             DMA((8,)), DMA((12,)), DMA((1,)),
@@ -1576,33 +1745,24 @@
     image, target, time_index, loss_weight, clip_embed, clip_tokens, norm_gain, norm_bias,
     conv1_w, conv2_w, conv_bias, emb_w, emb_b, qkv_w, qv_bias, ctx_w, ctx_b, out_w, out_b,
 ):
-    row = lax.axis_index("row")
-    z, k = row // 2, row % 2
+    z = lax.axis_index("row") // 2
     feat = swish(time_features(time_index, EMB) + clip_embed.astype(F32)).astype(BF)
-    cond = jnp.einsum("ne,jde->njd", feat, emb_w, preferred_element_type=F32) + emb_b
+    feat = jnp.pad(feat, ((0, 12), (0, 0)))
+    tokens = clip_tokens.reshape(4 * CTX, CTXW)
     weight_row = jnp.broadcast_to(lax.dynamic_slice_in_dim(loss_weight, z, 1), (1, 128))
     vec = jnp.concatenate([
-        norm_gain, norm_bias, conv_bias, qv_bias, out_b[None],
-        lax.dynamic_index_in_dim(cond, z, 0, False), weight_row, jnp.zeros((2, 128), F32)])
-    tokens = lax.dynamic_index_in_dim(clip_tokens, z, 0, False)
-    ctx = jnp.einsum("jde,te->jdt", ctx_w, tokens, preferred_element_type=F32) + ctx_b[:, :, None]
-    ctx = lax.dynamic_slice_in_dim(ctx, k * HEAD, HEAD, 1).astype(BF)
-    ctx = jnp.pad(ctx, ((0, 0), (0, 0), (0, 128 - CTX)))
-    x, tgt, vec_all, st, a1, hid, a2, res, nrm, w1, w2, wq, wo, qkv = front(
-        image.reshape(4, PIX, 128), target.reshape(4, PIX, 128), vec,
-        conv1_w.reshape(9, 128, C), conv2_w.reshape(9, 128, C), qkv_w, out_w[None])
-    p, pc, o, ot, linv = attend(qkv, ctx)
-    result, cot, gwo, gob, dot_ = middle(ot, res, tgt, wo, vec_all)
-    dqkv, dctx = attend_back(qkv, ctx, p, pc, o, linv, dot_)
-    dctx = lax.all_gather(dctx[:, :CTX, :HEAD], "row", axis=0, tiled=False)
-    gimg, zv, fin = back(dqkv, vec_all, st, x, a1, hid, a2, res, nrm, cot, w1, w2, wq,
-                         gwo.reshape(4, 2, 64, C), gob)
-    dctx = dctx.reshape(4, 2, 2, CTX, HEAD)
-    dctx = jnp.transpose(dctx, (0, 3, 2, 1, 4)).reshape(4, CTX, 2, 128)
-    grad_ctx_w = jnp.einsum("nte,ntjd->jde", clip_tokens.astype(F32), dctx, precision=HIGH)
+        norm_gain, norm_bias, conv_bias, qv_bias, out_b[None], jnp.zeros((2, 128), F32),
+        weight_row, jnp.zeros((2, 128), F32)])
+    (x, tgt, vec_all, st, a1, hid, a2, res, nrm, w1, w2, wq, wo, qkv, attn, p, ctx, pc, o,
+     linv) = front(
+        image.reshape(4, PIX, 128), target.reshape(4, PIX, 128), vec, feat, tokens, emb_w, emb_b,
+        ctx_w, ctx_b, conv1_w.reshape(9, 128, C), conv2_w.reshape(9, 128, C), qkv_w, out_w[None])
+    result, cot, gwo, gob, dt, grad_ctx_w, grad_ctx_b = middle(
+        attn, res, tgt, wo, vec_all, qkv, ctx, p, pc, o, linv, tokens)
+    gimg, zv, fin, grad_emb_w = back(
+        dt, vec_all, st, x, a1, hid, a2, res, nrm, cot, w1, w2, wq, gwo.reshape(4, 2, 64, C), gob,
+        feat)
     sums = jnp.sum(zv, axis=0)
-    dcond = zv[:, 11:13]
-    grad_emb_w = jnp.einsum("ne,njd->jde", feat.astype(F32), dcond, precision=HIGH)
     fin = fin.reshape(TAPS, 128, C).astype(F32)
     return (
         result.reshape(image.shape),
@@ -1613,11 +1773,11 @@
         fin[4:13].reshape(3, 3, 128, C),
         sums[6:8],
         grad_emb_w,
-        jnp.sum(dcond, axis=0),
+        sums[11:13],
         fin[1:4],
         sums[8:10],
         grad_ctx_w,
-        jnp.sum(dctx, axis=(0, 1)),
+        grad_ctx_b,
         fin[0],
         sums[10],
     )

time: 438 us -> 324 us (0.74)
  Pallas kernels: 392 us -> 297 us
  blocking collectives: 13.9 us -> 0 us
  matrix products: 7.47 us -> 0 us
    pallas_call x2 -> x0, Pallas kernels: 81.1 us -> none  [the longest x1 41.3 us: attend(): pl.pallas_call(attend_kernel, name='attend', grid=(pixels // QBLOCK,), ou...]
    pallas_call x1, Pallas kernels: 162 us -> 124 us  [back(): pl.pallas_call(back_kernel, name='back', out_shape=[jax.ShapeDtypeStruct(...]
    pallas_call x1, Pallas kernels: 28.8 us -> 62.9 us  [middle(): pl.pallas_call(middle_kernel, name='middle', out_shape=[jax.ShapeDtypeStr...]
    all_gather x1 -> x0, blocking collectives: 13.9 us -> none  [plane_body(): dctx = lax.all_gather(dctx[:, :CTX, :HEAD], 'row', axis=0, tiled=False)]
    pallas_call x1, Pallas kernels: 120 us -> 110 us  [front(): pl.pallas_call(front_kernel, name='front', out_shape=[jax.ShapeDtypeStruc...]
    dot_general x4 -> x0, matrix products: 7.47 us -> none  [the longest x1 2.37 us: plane_body(): jnp.einsum('ne,njd->jde', feat.astype(F32), dcond, precision=HIGH)]
    unnamed x14 -> x15, local copies, waits for them, and re-layouts: 1.97 us -> 6.8 us
where the time goes in v2:
time: 324 us; the launch traced here: 323 us
  Pallas kernels  297 us (92%)
  local copies, waits for them, and re-layouts  22.7 us (7%)
    pallas_call x1, Pallas kernels, back(): pl.pallas_call(back_kernel, name='back', out_shape=[jax.ShapeDtypeStruct(...  124 us
    pallas_call x1, Pallas kernels, front(): pl.pallas_call(front_kernel, name='front', out_shape=[jax.ShapeDtypeStruc...  110 us
    pallas_call x1, Pallas kernels, middle(): pl.pallas_call(middle_kernel, name='middle', out_shape=[jax.ShapeDtypeStr...  62.9 us
    unnamed x15, local copies, waits for them, and re-layouts  6.8 us

profile of v2, /device:TPU:7, one launch (start us, length us, event | category | flops | bytes accessed | tf_op | source)
XLA Modules:
  0.0 323.3 jit_solution(10267244455644180174)
XLA Ops:
  0.7 1.2 dynamic_slice.5
  1.9 0.6 broadcast_in_dim.14
  2.6 0.7 convert_element_type.15
  3.2 2.6 concatenate.6.vec
  6.0 0.8 fusion
  6.8 0.6 pad.4.feat
  7.4 1.5 reshape.80.tokens
  8.9 110.3 %front.1 = (bf16[512,512]{1,0:T(8,128)(2,1)}, bf16[512,512]{1,0:T(8,128)(2,1)}, f32[16,512]{1,0:T(8,128)}, f32[8,512]{1,0:T(8,128)}, bf16[3,640,512]{2,1,0:T(8,1...) custom-call(bf16[4,512,128]{2,1,0:T(8,128)(2,1)} %bitcast.23, ...), custom_call_target="tpu_custom_call" | custom-call | tf_op jit(solution)/shard_map/front/pallas_call | solution.py:1110
  119.2 62.9 %middle.1 = (f32[4,512,128]{2,1,0:T(8,128)}, f32[512,512]{1,0:T(8,128)}, bf16[512,512]{1,0:T(8,128)(2,1)}, f32[8,512]{1,0:T(8,128)}, bf16[3,512,512]{2,1,0:T(8,1...) custom-call(bf16[512,512]{1,0:T(8,128)(2,1)} %get-tuple-element.46.attn, f32[512,512]{1,0:T(8,128)} %get-tuple-element.47.res, ...), custom_call_target="tpu_custom_call" | custom-call | tf_op jit(solution)/shard_map/middle/pallas_call | solution.py:1349
  182.2 123.7 %back.1 = (f32[4,512,128]{2,1,0:T(8,128)}, f32[4,16,128]{2,1,0:T(8,128)}, bf16[22,2,4,16,512]{4,3,2,1,0:T(8,128)(2,1)}, f32[2,128,2048]{2,1,0:T(8,128)}) custom-call(bf16[3,512,512]{2,1,0:T(8,128)(2,1)} %get-tuple-element.58.dt, f32[16,512]{1,0:T(8,128)} %get-tuple-element.50.vec, f32[8,512]{1,0:T(8,128)} %get-tuple-element.59.st, ...), custom_call_target="tpu_custom_call" | custom-call | tf_op jit(solution)/shard_map/back/pallas_call | solution.py:1720
  305.9 0.8 reduce_sum.9
  306.7 0.6 fusion.2
  307.2 0.5 slice_bitcast_fusion
  307.8 0.6 pad_maximum_fusion
  308.4 1.6 slice.75
  310.0 2.0 slice.73
  312.0 4.6 %fusion.1 = (f32[9,2,4,16,512]{4,3,2,1,0:T(8,128)}, f32[9,2,4,16,512]{4,3,2,1,0:T(8,128)}) fusion(bf16[22,2,4,16,512]{4,3,2,1,0:T(8,128)(2,1)} %get-tuple-element.73), kind=kLoop, calls=%fused_computation.9 | loop fusion | bytes 9437184 | tf_op jit(solution)/shard_map/slice | solution.py:1773
  316.5 1.0 copy.39
  317.5 0.6 copy-done.3
  318.1 1.0 copy.40
  319.1 1.3 copy.41
  320.4 1.0 copy-done
  321.4 1.3 copy.42
  322.8 0.6 copy.43
  (11 shorter events, 0.2 us)
Async XLA Ops:
  312.0 4.6 %copy-start.2 = (f32[4,512,128]{2,1,0:T(8,128)S(1)}, f32[4,512,128]{2,1,0:T(8,128)}, u32[]{:S(2)}) copy-start(f32[4,512,128]{2,1,0:T(8,128)} %get-tuple-element.57) | copy-start | bytes 3145732
  316.5 1.6 copy-start.3
  316.5 2.6 copy-start.1
  319.1 2.3 copy-start
  321.4 1.3 copy-start.4

commit v3 on v2

--- a/solution.py
+++ b/solution.py
@@ -494,6 +494,7 @@
 NT = (((1,), (1,)), ((), ()))
 ANY = pl.BlockSpec(memory_space=pl.ANY)
 VMEM = pl.BlockSpec(memory_space=pltpu.VMEM)
+SMEM = pl.BlockSpec(memory_space=pltpu.SMEM)
 PIX = 512
 PAD = 640
 CHUNKS = 8
@@ -503,6 +504,11 @@
 
 def mm(left, right, dims=NN):
     return lax.dot_general(left, right, dims, preferred_element_type=F32)
+
+
+def mixed(chan, z):
+    low = lax.rem(chan + lax.div(z, 2), 2)
+    return low + 2 * lax.rem(lax.div(chan, 2) + lax.rem(z, 2), 2)
 
 
 class Place:
@@ -512,14 +518,14 @@
         self.z = lax.div(self.r, 2)
         self.k = lax.rem(self.r, 2)
         self.d = 2 * self.c + self.k
-        self.pair = lax.rem(self.c - self.z + 4, 4)
+        self.pair = mixed(self.c, self.z)
         self.band = 2 * self.pair + self.k
 
     def head_device(self, head):
         return (2 * self.z + lax.rem(head, 2), lax.div(head, 2))
 
     def band_device(self, band):
-        return (2 * self.z + lax.rem(band, 2), lax.rem(lax.div(band, 2) + self.z, 4))
+        return (2 * self.z + lax.rem(band, 2), mixed(lax.div(band, 2), self.z))
 
 
 def send(src, dst, send_sem, recv_sem, device):
@@ -676,7 +682,7 @@
 
 
 def image_targets(me):
-    return [(n, (2 * n + me.k, lax.rem(me.z + n, 4))) for n in range(4)]
+    return [(n, (2 * n + me.k, mixed(me.z, jnp.int32(n)))) for n in range(4)]
 
 
 class Gather:
@@ -761,12 +767,13 @@
 
 
 def front_kernel(
-    img, tgt, vec, feat, tokens, emb_w, emb_b, ctx_w, ctx_b, w1, w2, wq, wo,
+    img, tgt, steps, loss, embed, words, norm_gain, norm_bias, conv_bias, qv_bias, out_b,
+    emb_w, emb_b, ctx_w, ctx_b, w1, w2, wq, wo,
     x_o, t_o, vec_o, st_o, a1_o, hid_o, a2_o, res_o, nrm_o, w1_o, w2_o, wq_o, wo_o, qkv_o,
-    attn_o, p_o, ctx_o, pc_o, o_o, linv_o,
+    attn_o, p_o, ctx_o, pc_o, o_o, linv_o, feat, tokens,
     x_v, t_v, vec_v, st_v, a1_v, hid_v, a2_v, res_v, nrm_v, w1_v, w2_v, wq_v, wo_v, qkv_v,
     attn_v,
-    msg, groups, slots, halo, vsrc, cond, keys, ckeys, qs, vext, cvext, sbuf, mbuf, cbuf, pb, ob,
+    msg, groups, slots, halo, vsrc, wide, cond, keys, ckeys, qs, vext, cvext, sbuf, mbuf, cbuf, pb, ob,
     vs, vr, ims, imr, tgs, tgr, own_sem, first_s, first_r, relay_s, relay_r, give_s, give_r,
     core_s, core_r, wos, wor, wofs, wofr, wol, sts, str_, hs, hr, qs_s, qs_r, lsem, osem, psem,
     as_, ar,
@@ -774,7 +781,7 @@
     me = Place()
     barrier = pltpu.get_barrier_semaphore()
     greet_plane(me, barrier)
-    own_block = me.c == lax.rem(2 * me.z, 4)
+    own_block = me.pair == me.z
     for chan in range(4):
         itself = jnp.logical_and(me.pair == me.z, me.c == chan)
 
@@ -788,12 +795,31 @@
     pl.semaphore_signal(
         barrier, inc=1, device_id=(2 * (me.z + 1 - 2 * odd) + me.k, me.c), device_id_type=MESH_ID
     )
+    wide[...] = jnp.zeros((16, EMB), F32)
+    wide[0:4, :] = embed[...].astype(F32)
+    row = lax.broadcasted_iota(jnp.int32, (16, EMB // 2), 0)
+    column = lax.broadcasted_iota(jnp.int32, (16, EMB // 2), 1).astype(F32)
+    frequency = jnp.exp(-math.log(10000.0) * column / (EMB // 2))
+    angle = jnp.zeros((16, EMB // 2), F32)
+    for n in range(4):
+        angle = jnp.where(row == n, steps[n].astype(F32) * frequency, angle)
+    for start, wave in ((0, jnp.cos), (EMB // 2, jnp.sin)):
+        value = wave(angle) + wide[:, start : start + EMB // 2]
+        feat[:, start : start + EMB // 2] = jnp.where(row < 4, swish(value), 0.0).astype(BF)
+    for n in range(4):
+        wide[4 * n : 4 * n + 4, :] = words[n].astype(F32)
+    tokens[...] = wide[...].astype(BF)
     for j in range(2):
         cond[j] = mm(feat[...], emb_w[j], NT) + emb_b[j : j + 1, :]
-    vsrc[0:11, :] = vec[0:11, :]
+    vsrc[0:3, :] = norm_gain[...]
+    vsrc[3:6, :] = norm_bias[...]
+    vsrc[6:8, :] = conv_bias[...]
+    vsrc[8:10, :] = qv_bias[...]
+    vsrc[10:11, :] = out_b[...]
     vsrc[11:12, :] = cond[0, pl.ds(me.z, 1), :]
     vsrc[12:13, :] = cond[1, pl.ds(me.z, 1), :]
-    vsrc[13:16, :] = vec[13:16, :]
+    vsrc[13:14, :] = jnp.full((1, 128), loss[me.z], F32)
+    vsrc[14:16, :] = jnp.zeros((2, 128), F32)
     lane = lax.broadcasted_iota(jnp.int32, (16, 128), 1)
     for j in range(2):
         value = mm(tokens[...], ctx_w[j], NT) + ctx_b[j : j + 1, :]
@@ -804,8 +830,8 @@
         if j == 0:
             ckeys[...] = both.astype(BF)
         else:
-            wide = jnp.concatenate([both, jnp.zeros((112, 128), F32)], axis=0)
-            cvext[0:HEAD, :] = jnp.transpose(wide)[0:HEAD].astype(BF)
+            tall = jnp.concatenate([both, jnp.zeros((112, 128), F32)], axis=0)
+            cvext[0:HEAD, :] = jnp.transpose(tall)[0:HEAD].astype(BF)
     row = lax.broadcasted_iota(jnp.int32, (16, H * W), 0)
     vext[HEAD:, :] = jnp.where(row == 0, 1.0, 0.0).astype(BF)
     cvext[HEAD:, :] = jnp.where(row[:, 0:128] == 0, 1.0, 0.0).astype(BF)
@@ -956,11 +982,11 @@
 
     owns = []
     qkv_copies = {}
-    for j, bias_row in ((1, None), (0, 8), (2, 9)):
+    for j, bias_row in ((1, None), (2, 9), (0, 8)):
         value = mm(wq_v[j], turned)
         if bias_row is not None:
-            wide = jnp.transpose(jnp.broadcast_to(vec_v[bias_row : bias_row + 1, :], (128, C)))
-            value = value + jnp.concatenate([wide] * 4, axis=1)
+            tall = jnp.transpose(jnp.broadcast_to(vec_v[bias_row : bias_row + 1, :], (128, C)))
+            value = value + jnp.concatenate([tall] * 4, axis=1)
         msg[j] = value.astype(BF)
         owns.append(local(msg.at[j, head_rows(me.d), :], qkv_v.at[j, :, band_cols], lsem.at[j]))
         qkv_copies[j] = []
@@ -976,12 +1002,14 @@
         copy.wait()
     both = jnp.concatenate([qkv_v[1], qkv_v[1]], axis=0).astype(F32)
     keys[...] = jnp.transpose(both).astype(BF)
-    for copy in qkv_copies[0]:
-        copy.wait()
-    scaled = qkv_v[0].astype(F32) * (HEAD ** (-0.5) * LOG2E)
-    top = scaled.astype(BF)
-    qs[0:HEAD, :] = top
-    qs[HEAD:, :] = (scaled - top.astype(F32)).astype(BF)
+
+    def scale_queries(where):
+        scaled = qkv_v[0, :, where].astype(F32) * (HEAD ** (-0.5) * LOG2E)
+        top = scaled.astype(BF)
+        qs[0:HEAD, where] = top
+        qs[HEAD:, where] = (scaled - top.astype(F32)).astype(BF)
+
+    scale_queries(band_cols)
     token = lax.broadcasted_iota(jnp.int32, (16, SUB), 0)
     valid = lax.div(token, CTX) == me.z
     chunks = H * W // KEYS
@@ -997,13 +1025,16 @@
         sbuf[slot, chunk * KEYS : (chunk + 1) * KEYS, :] = value
         return jnp.maximum(highest, jnp.max(value.reshape(KEYS // 8, 8, SUB), axis=0))
 
-    query, highest = begin(0, 0)
+    query, highest = begin(0, 2 * me.band)
     for chunk in range(chunks):
         highest = score_chunk(0, query, highest, chunk)
     mbuf[0] = highest
     for copy in qkv_copies[2]:
         copy.wait()
     vext[0:HEAD, :] = qkv_v[2]
+    for copy in qkv_copies[0]:
+        copy.wait()
+    scale_queries(pl.ds(0, H * W))
     save(13, qkv_v, qkv_o)
     image_send(tgt, t_v, tgs, tgr)
     half = pl.ds(pl.multiple_of(me.c * 128 + me.k * 64, 64), 64)
@@ -1021,20 +1052,21 @@
             pb.at[slot], p_o.at[:, pl.ds(pl.multiple_of(block * PIX, PIX), PIX)], psem.at[slot])
 
     @pl.loop(0, 8)
-    def _(block):
-        slot = lax.rem(block, 2)
-
-        @pl.when(block >= 2)
+    def _(turn):
+        block = lax.rem(me.band + turn, 8)
+        slot = lax.rem(turn, 2)
+
+        @pl.when(turn >= 2)
         def _():
-            p_copy(block - 2, slot).wait()
+            p_copy(block, slot).wait()
 
         for sub in range(2):
             cols = pl.ds(sub * SUB, SUB)
-            wide = pl.ds(pl.multiple_of(block * PIX + sub * SUB, SUB), SUB)
-            following = jnp.minimum(2 * block + sub + 1, H * W // SUB - 1)
+            place = pl.ds(pl.multiple_of(block * PIX + sub * SUB, SUB), SUB)
+            following = lax.rem(2 * block + sub + 1, H * W // SUB)
             top = jnp.max(mbuf[sub], axis=0, keepdims=True)
             pc = jnp.exp2(cbuf[sub] - top).astype(BF)
-            pc_o[:, wide] = pc
+            pc_o[:, place] = pc
             out = mm(cvext[:, 0:16], pc)
             query, highest = begin(1 - sub, following)
             for chunk in range(chunks):
@@ -1046,9 +1078,9 @@
             mbuf[1 - sub] = highest
             linv = 1.0 / out[HEAD : HEAD + 1]
             out = out[0:HEAD] * linv
-            o_o[:, wide] = out
+            o_o[:, place] = out
             ob[block, :, cols] = out.astype(BF)
-            linv_o[:, wide] = jnp.broadcast_to(linv, (8, SUB))
+            linv_o[:, place] = jnp.broadcast_to(linv, (8, SUB))
         p_copy(block, slot).start()
 
         @pl.when(block != me.band)
@@ -1090,8 +1122,8 @@
         pltpu.make_async_copy(
             ob.at[0], attn_v.at[pl.ds(block * HEAD, HEAD), :], ar.at[block]).wait()
     save(14, attn_v, attn_o)
-    p_copy(6, 0).wait()
-    p_copy(7, 1).wait()
+    p_copy(0, 0).wait()
+    p_copy(0, 1).wait()
     for copy in outs:
         copy.wait()
 
@@ -1105,18 +1137,19 @@
     ]
     more = [
         ((pixels, pixels), BF), ((2, 16, 128), BF), ((16, pixels), BF), ((HEAD, pixels), F32),
-        ((8, pixels), F32),
+        ((8, pixels), F32), ((16, EMB), BF), ((16, CTXW), BF),
     ]
     return pl.pallas_call(
         front_kernel,
         name="front",
         out_shape=[jax.ShapeDtypeStruct(*one) for one in saved + more],
-        in_specs=[ANY, ANY] + [VMEM] * 7 + [ANY] * 4,
-        out_specs=[ANY] * (len(saved) + 1) + [VMEM] * 4,
+        in_specs=[ANY, ANY] + [SMEM] * 2 + [VMEM] * 11 + [ANY] * 4,
+        out_specs=[ANY] * (len(saved) + 1) + [VMEM] * 6,
         scratch_shapes=[pltpu.VMEM(*one) for one in saved]
         + [
             pltpu.VMEM((3, C, C), BF), pltpu.VMEM((C, C), BF), pltpu.VMEM((3, 8, 8, C), F32),
             pltpu.VMEM((2, 2, 64, C), BF), pltpu.VMEM((16, 128), F32),
+            pltpu.VMEM((16, EMB), F32),
             pltpu.VMEM((2, 16, 128), F32), pltpu.VMEM((pixels, 128), BF),
             pltpu.VMEM((16, 128), BF), pltpu.VMEM((128, pixels), BF),
             pltpu.VMEM((VROWS, pixels), BF), pltpu.VMEM((VROWS, 128), BF),
@@ -1165,14 +1198,14 @@
 
 
 def greet_back(me, barrier):
-    own_block = me.c == lax.rem(2 * me.z, 4)
+    own_block = me.pair == me.z
     for n in range(4):
         itself = jnp.logical_and(own_block, me.z == n)
 
         @pl.when(jnp.logical_not(itself))
         def _():
             pl.semaphore_signal(
-                barrier, inc=1, device_id=(2 * n + me.k, lax.rem(me.z + n, 4)),
+                barrier, inc=1, device_id=(2 * n + me.k, mixed(me.z, jnp.int32(n))),
                 device_id_type=MESH_ID,
             )
 
@@ -1180,8 +1213,8 @@
 
 
 def middle_kernel(
-    attn, res, tgt, wo, vec, qkv, ctx, p, pc, o, linv, tokens,
-    out_o, cot_o, gwo_o, gob_o, dt_o, gcw_o, gcb_o,
+    attn, res, tgt, wo, vec, qkv, ctx, p, pc, o, linv,
+    out_o, cot_o, gwo_o, gob_o, dt_o, ctot_o,
     attn_v, res_v, tgt_v, wo_v, out_b, back, cot_v, dat, dot_v, qkv_v, o_v,
     vext, cvext, dos, dor, qrow, dq, pb, dkv, dqb, dt_v, dctx, cslots,
     bs, br, ds_, dr, cs, cr, ks, kr, q_s, q_r, lsem, osem, psem,
@@ -1202,7 +1235,7 @@
         return pltpu.make_async_copy(
             p.at[pl.ds(pl.multiple_of(block * PIX, PIX), PIX), :], pb.at[slot], psem.at[slot])
 
-    p_copy(0, 0).start()
+    p_copy(me.band, 0).start()
 
     def band_cols(band):
         return pl.ds(pl.multiple_of(band * PIX, PIX), PIX)
@@ -1275,12 +1308,13 @@
     mine = head_rows(me.d)
 
     @pl.loop(0, 8)
-    def _(block):
-        slot = lax.rem(block, 2)
-
-        @pl.when(block < 7)
+    def _(turn):
+        block = lax.rem(me.band + turn, 8)
+        slot = lax.rem(turn, 2)
+
+        @pl.when(turn < 7)
         def _():
-            p_copy(block + 1, 1 - slot).start()
+            p_copy(lax.rem(block + 1, 8), 1 - slot).start()
 
         p_copy(block, slot).wait()
         grads = []
@@ -1319,10 +1353,9 @@
         total = cslots[0, j]
         for slot in range(1, 8):
             total = total + cslots[slot, j]
-        gcb_o[j : j + 1, :] = as_row(total)
-        gcw_o[j] = sum(mm(term, tokens[...]) for term in split_rows(total))
+        ctot_o[j] = total
     band_back_wait(me, out_b, back, bs, br)
-    out_o[...] = back[...].astype(F32)
+    saves.append(local(back, out_o, osem.at[2]))
     for copy in copies:
         copy.wait_send()
     for block in range(8):
@@ -1350,16 +1383,15 @@
         middle_kernel,
         name="middle",
         out_shape=[
-            jax.ShapeDtypeStruct((4, PIX, 128), F32),
+            jax.ShapeDtypeStruct((4, PIX, 128), BF),
             jax.ShapeDtypeStruct((PIX, C), F32),
             jax.ShapeDtypeStruct((C, C), BF),
             jax.ShapeDtypeStruct((8, C), F32),
             jax.ShapeDtypeStruct((3, C, PIX), BF),
-            jax.ShapeDtypeStruct((2, 128, CTXW), F32),
-            jax.ShapeDtypeStruct((2, 128), F32),
+            jax.ShapeDtypeStruct((2, 16, 128), F32),
         ],
-        in_specs=[ANY] * 4 + [VMEM, ANY, VMEM, ANY, VMEM, ANY, VMEM, VMEM],
-        out_specs=[VMEM, ANY, VMEM, VMEM, ANY, VMEM, VMEM],
+        in_specs=[ANY] * 4 + [VMEM, ANY, VMEM, ANY, VMEM, ANY, VMEM],
+        out_specs=[ANY, ANY, VMEM, VMEM, ANY, VMEM],
         scratch_shapes=[
             pltpu.VMEM((C, PIX), BF), pltpu.VMEM((PIX, C), F32), pltpu.VMEM((PIX, C), BF),
             pltpu.VMEM((C, C), BF), pltpu.VMEM((PIX, C), BF), pltpu.VMEM((4, PIX, 128), BF),
@@ -1372,7 +1404,7 @@
             pltpu.VMEM((HEAD, pixels), BF), pltpu.VMEM((3, C, PIX), BF),
             pltpu.VMEM((2, 16, 128), F32), pltpu.VMEM((8, 2, 16, 128), F32),
             DMA((4,)), DMA((4,)), DMA((8,)), DMA((8,)), DMA((8,)), DMA((8,)), DMA((8,)),
-            DMA((8,)), DMA((8,)), DMA((8,)), DMA((7,)), DMA((2,)), DMA((2,)),
+            DMA((8,)), DMA((8,)), DMA((8,)), DMA((7,)), DMA((3,)), DMA((2,)),
         ],
         compiler_params=pltpu.CompilerParams(
             collective_id=2, has_side_effects=True, vmem_limit_bytes=VMEM_LIMIT
@@ -1381,119 +1413,141 @@
 
 
 TAPS = 22
-GROUP_TAPS = ((0, 1), (1, 3), (4, 3), (7, 3), (10, 3), (13, 3), (16, 3), (19, 3))
+GROUP_TAPS = ((0, 1), (1, 3), (4, 3), (7, 3), (10, 3), (13, 3), (16, 3), (19, 2), (21, 1))
+GROUPS_SENT = len(GROUP_TAPS)
+STAGES = 9
 
 
 class Reduce:
-    def __init__(self, me, part, from_core, from_chan, plane, from_plane, total, sems):
-        self.me = me
-        self.part, self.from_core, self.from_chan = part, from_core, from_chan
-        self.plane, self.from_plane, self.total = plane, from_plane, total
-        self.sems = sems
+    def __init__(self, me, part, bufs, total, sems):
+        self.me, self.part, self.total = me, part, total
+        (self.from_core, self.near_x, self.near_y, self.last_x, self.last_y, self.plane,
+         self.plane_two, self.plane_one) = bufs
+        self.s, self.r = sems
+        odd = lax.rem(me.z, 2)
+        self.x = me.c + 1 - 2 * lax.rem(me.c, 2)
+        self.y = lax.rem(me.c + 2, 4)
+        self.far = lax.rem(self.x + 2, 4)
+        self.core = (me.r + 1 - 2 * me.k, me.c)
+        self.z1 = me.z + 1 - 2 * odd
+        self.z2 = lax.rem(me.z + 2, 4)
+        self.z3 = lax.rem(self.z1 + 2, 4)
         self.copies = {}
 
+    def plane_device(self, z):
+        return (2 * z + self.me.k, self.me.c)
+
     def advance(self, group):
-        stage = self.copies.get(group, (0, []))[0]
-        for copy in self.copies.get(group, (0, []))[1]:
+        stage, waiting = self.copies.get(group, (0, []))
+        for copy in waiting:
             copy.wait()
-        step = (self.core_send, self.chan_send, self.plane_send, self.plane_gather,
-                self.core_gather, lambda group, taps: [])[stage]
         start, count = GROUP_TAPS[group]
-        self.copies[group] = (stage + 1, step(group, pl.ds(start, count)))
-
-    def core_send(self, group, taps):
+        step = (self.core_send, self.first_send, self.second_send, self.halve_send,
+                self.quarter_send, self.quarter_back, self.half_back, self.core_back,
+                lambda *_: [])[stage]
+        taps = pl.ds(start, count)
+        moves = step(taps, lambda body: pl.loop(start, start + count)(body))
+        copies = [
+            send(src, dst, self.s.at[group, stage, j], self.r.at[group, stage, j], device)
+            for j, (src, dst, device) in enumerate(moves)
+        ]
+        self.copies[group] = (stage + 1, copies)
+
+    def core_send(self, taps, each):
+        return [(self.part.at[taps, :, 1 - self.me.k], self.from_core.at[taps], self.core)]
+
+    def first_send(self, taps, each):
+        me, part = self.me, self.part
+
+        @each
+        def _(tap):
+            own = part[tap, :, me.k].astype(F32) + self.from_core[tap].astype(F32)
+            part[tap, :, me.k] = own.astype(BF)
+
+        low, high = pl.ds(0, 32), pl.ds(32, 32)
+        x, y = (me.r, self.x), (me.r, self.y)
+        return [
+            (part.at[taps, self.far, me.k, low, :], self.near_x.at[1, taps], x),
+            (part.at[taps, self.far, me.k, high, :], self.near_y.at[1, taps], y),
+            (part.at[taps, self.x, me.k, low, :], self.near_x.at[0, taps], x),
+            (part.at[taps, self.y, me.k, high, :], self.near_y.at[0, taps], y),
+        ]
+
+    def second_send(self, taps, each):
+        me, part = self.me, self.part
+        low, high = pl.ds(0, 32), pl.ds(32, 32)
+
+        @each
+        def _(tap):
+            for chan, rows, near in ((self.y, low, self.near_x), (self.x, high, self.near_y)):
+                value = part[tap, chan, me.k, rows, :].astype(F32) + near[1, tap].astype(F32)
+                part[tap, chan, me.k, rows, :] = value.astype(BF)
+
+        return [
+            (part.at[taps, self.y, me.k, low, :], self.last_y.at[taps], (me.r, self.y)),
+            (part.at[taps, self.x, me.k, high, :], self.last_x.at[taps], (me.r, self.x)),
+        ]
+
+    def rows(self, z):
+        return pl.ds(pl.multiple_of(z * 16, 16), 16)
+
+    def halve_send(self, taps, each):
+        me, part = self.me, self.part
+
+        @each
+        def _(tap):
+            for start, near, last in ((0, self.near_x, self.last_y), (32, self.near_y, self.last_x)):
+                rows = pl.ds(start, 32)
+                value = (part[tap, me.c, me.k, rows, :].astype(F32) + near[0, tap].astype(F32)
+                         + last[tap].astype(F32))
+                self.plane[tap, rows, :] = value.astype(BF)
+
+        device = self.plane_device(self.z1)
+        return [
+            (self.plane.at[taps, self.rows(self.z1), :], self.plane_two.at[0, taps], device),
+            (self.plane.at[taps, self.rows(self.z3), :], self.plane_two.at[1, taps], device),
+        ]
+
+    def quarter_send(self, taps, each):
+        @each
+        def _(tap):
+            for j, z in enumerate((self.me.z, self.z2)):
+                value = (self.plane[tap, self.rows(z), :].astype(F32)
+                         + self.plane_two[j, tap].astype(F32))
+                self.plane[tap, self.rows(z), :] = value.astype(BF)
+
+        return [(self.plane.at[taps, self.rows(self.z2), :], self.plane_one.at[taps],
+                 self.plane_device(self.z2))]
+
+    def quarter_back(self, taps, each):
         me = self.me
-        s, r = self.sems[0], self.sems[1]
-        return [
-            send(self.part.at[taps, :, 1 - me.k], self.from_core.at[taps], s.at[group],
-                 r.at[group], (me.r + 1 - 2 * me.k, me.c))
-        ]
-
-    def chan_send(self, group, taps):
-        me = self.me
-        start, count = GROUP_TAPS[group]
-
-        @pl.loop(start, start + count)
+
+        @each
         def _(tap):
-            own = self.part[tap, :, me.k].astype(F32) + self.from_core[tap].astype(F32)
-            self.part[tap, :, me.k] = own.astype(BF)
-
-        s, r = self.sems[2], self.sems[3]
-        out = []
-        for t in range(1, 4):
-            chan = lax.rem(me.c + t, 4)
-            out.append(
-                send(self.part.at[taps, chan, me.k], self.from_chan.at[t - 1, taps],
-                     s.at[group, t], r.at[group, t], (me.r, chan))
-            )
-        return out
-
-    def plane_send(self, group, taps):
-        me = self.me
-        start, count = GROUP_TAPS[group]
-
-        @pl.loop(start, start + count)
-        def _(tap):
-            value = self.part[tap, me.c, me.k].astype(F32)
-            for t in range(3):
-                value = value + self.from_chan[t, tap].astype(F32)
-            self.plane[tap] = value.astype(BF)
-
-        s, r = self.sems[4], self.sems[5]
-        out = []
-        for t in range(1, 4):
-            z = lax.rem(me.z + t, 4)
-            rows = pl.ds(pl.multiple_of(z * 16, 16), 16)
-            out.append(
-                send(self.plane.at[taps, rows, :], self.from_plane.at[t - 1, taps],
-                     s.at[group, t], r.at[group, t], (2 * z + me.k, me.c))
-            )
-        return out
-
-    def plane_gather(self, group, taps):
-        me = self.me
-        start, count = GROUP_TAPS[group]
-        rows = pl.ds(pl.multiple_of(me.z * 16, 16), 16)
-
-        @pl.loop(start, start + count)
-        def _(tap):
-            value = self.plane[tap, rows, :].astype(F32)
-            for t in range(3):
-                value = value + self.from_plane[t, tap].astype(F32)
+            value = (self.plane[tap, self.rows(me.z), :].astype(F32)
+                     + self.plane_one[tap].astype(F32))
             self.total[tap, me.k, me.z] = value.astype(BF)
 
-        s, r = self.sems[6], self.sems[7]
-        out = []
-        for t in range(1, 4):
-            z = lax.rem(me.z + t, 4)
-            piece = self.total.at[taps, me.k, me.z]
-            out.append(send(piece, piece, s.at[group, t], r.at[group, t], (2 * z + me.k, me.c)))
-        return out
-
-    def core_gather(self, group, taps):
-        me = self.me
-        s, r = self.sems[8], self.sems[9]
-        piece = self.total.at[taps, me.k]
-        return [send(piece, piece, s.at[group], r.at[group], (me.r + 1 - 2 * me.k, me.c))]
-
-
-def split_rows(rows):
-    first = rows.astype(BF).astype(F32)
-    second = (rows - first).astype(BF).astype(F32)
-    stacked = jnp.concatenate([first, second, rows - first - second, jnp.zeros((80, 128), F32)],
-                              axis=0)
-    left = jnp.transpose(stacked).astype(BF)
-    return left[:, 0:16], left[:, 16:32], left[:, 32:48]
+        piece = self.total.at[taps, me.k, me.z]
+        return [(piece, piece, self.plane_device(self.z2))]
+
+    def half_back(self, taps, each):
+        device = self.plane_device(self.z1)
+        pieces = [self.total.at[taps, self.me.k, z] for z in (self.me.z, self.z2)]
+        return [(piece, piece, device) for piece in pieces]
+
+    def core_back(self, taps, each):
+        piece = self.total.at[taps, self.me.k]
+        return [(piece, piece, self.core)]
 
 
 def back_kernel(
-    dt, vec, st, x, a1, hid, a2, res, nrm, cot, w1, w2, wq, gwo, gob, feat,
-    gimg_o, zv_o, fin_o, gemb_o,
+    dt, vec, st, x, a1, hid, a2, res, nrm, cot, w1, w2, wq, gwo, gob,
+    gimg_o, zs_o, gw1_o, gw2_o, gqkv_o, gwo_o,
     dt_v, x_v, a1_v, hid_v, a2_v, res_v, nrm_v, drs_v, w1_v, w2_v, wq_v,
     cat, turned, acc, groups, slots, halo, keep, img_b, back, zsl,
-    part, from_core, from_chan, plane, from_plane, total,
-    ss, sr, hs, hr, bs, br, zs, zr, c1s, c1r, c2s, c2r, p1s, p1r, p2s, p2r, c3s, c3r,
-    lsem, osem,
+    part, from_core, near_x, near_y, last_x, last_y, plane, plane_two, plane_one, total,
+    ss, sr, hs, hr, bs, br, zs, zr, red_s, red_r, lsem, osem,
 ):
     me = Place()
     barrier = pltpu.get_barrier_semaphore()
@@ -1507,8 +1561,14 @@
     loads = [local(a, b, lsem.at[j]) for j, (a, b) in enumerate((
         (dt, dt_v), (wq, wq_v), (res, res_v), (gwo, part.at[0]), (nrm, nrm_v), (cot, drs_v),
         (a2, a2_v), (w2, w2_v), (hid, hid_v), (a1, a1_v), (w1, w1_v), (x, x_v)))]
-    reduce = Reduce(me, part, from_core, from_chan, plane, from_plane, total,
-                    (c1s, c1r, c2s, c2r, p1s, p1r, p2s, p2r, c3s, c3r))
+    reduce = Reduce(
+        me, part, (from_core, near_x, near_y, last_x, last_y, plane, plane_two, plane_one), total,
+        (red_s, red_r))
+
+    def advance(*groups):
+        for group in groups:
+            reduce.advance(group)
+
     group_matrix(groups)
     zero8 = jnp.zeros((8, C), F32)
     members = 1.0 / (H * W * 16)
@@ -1546,17 +1606,15 @@
     pl.semaphore_wait(barrier, 10 + others)
     copies = exchange(0, rows3)
     loads[3].wait()
-    reduce.advance(0)
+    advance(0)
     loads[4].wait()
 
     @pl.loop(0, 3)
     def _(j):
         part[1 + j] = mm(dt_v[j], nrm_v[...]).astype(BF).reshape(4, 2, 64, C)
 
-    reduce.advance(1)
-    reduce.advance(0)
-    for load in loads[5:]:
-        load.wait()
+    advance(1)
+    loads[5].wait()
     for copy in copies:
         copy.wait()
 
@@ -1579,29 +1637,33 @@
 
     keep[3:4, :] = as_row(lax.fori_loop(0, CHUNKS, resid_grad, zero8))
     halo_send(me, cat, halo.at[0], hs.at[0], hr.at[0])
-    reduce.advance(1)
+    advance(0, 1)
     turned[...] = jnp.transpose(drs_v[...]).astype(BF)
 
-    def weight_grads(group, source):
-        start = GROUP_TAPS[group][0]
-        row = (group - 2) % 3
-
-        @pl.loop(0, 3)
-        def _(col):
-            part[start + col] = mm(turned[...], source[col, row * 64 : row * 64 + PIX, :]).astype(
+    def weight_grads(group, source, first):
+        start, count = GROUP_TAPS[group]
+
+        @pl.loop(0, count)
+        def _(i):
+            tap = start - first + i
+            rows = pl.ds(pl.multiple_of(lax.div(tap, 3) * 64, 64), PIX)
+            part[start + i] = mm(turned[...], source[lax.rem(tap, 3), rows, :]).astype(
                 BF).reshape(4, 2, 64, C)
 
-        reduce.advance(group)
-
-    weight_grads(2, a2_v)
-    weight_grads(3, a2_v)
-    weight_grads(4, a2_v)
-    reduce.advance(0)
+        advance(group)
+
+    loads[6].wait()
+    for group in (2, 3, 4):
+        weight_grads(group, a2_v, 4)
+    advance(0)
     acc[...] = jnp.zeros((PIX, C), F32)
+    loads[7].wait()
     conv_taps(acc, cat, w2_v, (1,), True, NN)
     halo_wait(me, cat, halo.at[0], hs.at[0], hr.at[0])
-    reduce.advance(2)
+    advance(2)
     conv_taps(acc, cat, w2_v, (0, 2), True, NN)
+    advance(1)
+    loads[8].wait()
     gain2, bias2 = vec[1:2, :], vec[4:5, :]
     scale, shift = 1.0 + vec[11:12, :], vec[12:13, :]
 
@@ -1613,8 +1675,7 @@
         return value
 
     copies = exchange(1, sums(scaled2, mod_grad))
-    reduce.advance(1)
-    reduce.advance(0)
+    advance(0, 2)
     for copy in copies:
         copy.wait()
     total2 = slots_total(slots.at[1])
@@ -1632,19 +1693,19 @@
 
     keep[1:2, :] = as_row(lax.fori_loop(0, CHUNKS, hidden_grad, zero8))
     halo_send(me, cat, halo.at[1], hs.at[1], hr.at[1])
-    reduce.advance(3)
+    advance(3, 1)
     turned[...] = jnp.transpose(acc[...]).astype(BF)
-    weight_grads(5, a1_v)
-    reduce.advance(2)
-    weight_grads(6, a1_v)
-    reduce.advance(1)
-    weight_grads(7, a1_v)
-    reduce.advance(0)
-    reduce.advance(4)
+    loads[9].wait()
+    for group in (5, 6, 7, 8):
+        weight_grads(group, a1_v, 13)
+    advance(0, 2)
     acc[...] = jnp.zeros((PIX, C), F32)
+    loads[10].wait()
     conv_taps(acc, cat, w1_v, (1,), True, NN)
     halo_wait(me, cat, halo.at[1], hs.at[1], hr.at[1])
+    advance(1, 3)
     conv_taps(acc, cat, w1_v, (0, 2), True, NN)
+    loads[11].wait()
     gain1, bias1 = vec[0:1, :], vec[3:4, :]
 
     def pre_grad(i):
@@ -1656,10 +1717,7 @@
     first, cross = sums(scaled1, pre_grad)
     copies = exchange(2, [first, cross, keep[1:2, :], keep[3:4, :], keep[0:1, :], keep[2:3, :],
                           gob[0:1, :]])
-    reduce.advance(5)
-    reduce.advance(3)
-    reduce.advance(2)
-    reduce.advance(1)
+    advance(4, 0, 2, 3, 1)
     for copy in copies:
         copy.wait()
     total1 = slots_total(slots.at[2])
@@ -1676,7 +1734,7 @@
     band_back_send(me, img_b, back, bs, br)
     u2, v2 = keep[16:17, :], keep[17:18, :]
     keep[24:40, :] = jnp.concatenate(
-        [total1[1:2], total1[0:1], scale * v2, scale * u2, keep[9:10, :], keep[8:9, :],
+        [total1[1:2], scale * v2, keep[9:10, :], total1[0:1], scale * u2, keep[8:9, :],
          total1[2:7], gain2 * v2 + bias2 * u2, u2, jnp.zeros((3, C), F32)], axis=0)
     own_cols = pl.ds(pl.multiple_of(me.c * 128, 128), 128)
     zsl[me.z] = keep[24:40, own_cols]
@@ -1685,26 +1743,22 @@
              (2 * lax.rem(me.z + t, 4) + me.k, me.c))
         for t in range(1, 4)
     ]
-    for group in (6, 4, 7, 3, 2, 5, 4, 3):
-        reduce.advance(group)
+    advance(4, 5, 2, 3, 1, 0, 6, 4, 5, 2, 3, 7, 1, 6, 4, 5, 8)
     for copy in zcopies:
         copy.wait()
-    zv_o[...] = zsl[...]
-    for j in range(2):
-        rows = jnp.concatenate([zsl[n, 11 + j : 12 + j, :] for n in range(4)]
-                               + [jnp.zeros((12, 128), F32)], axis=0)
-        terms = split_rows(rows)
-        gemb_o[j] = sum(mm(term, feat[...]) for term in terms)
-    for group in (6, 5, 4):
-        reduce.advance(group)
+    zs_o[...] = zsl[...]
+    advance(7, 3, 4, 6, 5, 8, 7)
     band_back_wait(me, img_b, back, bs, br)
-    gimg_o[...] = back[...].astype(F32)
-    for group in (7, 6, 5, 7, 6, 7):
-        reduce.advance(group)
-    for group in range(8):
-        while reduce.copies[group][0] < 6:
-            reduce.advance(group)
-    local(total, fin_o, osem.at[0]).wait()
+    saves = [local(back, gimg_o, osem.at[0])]
+    for _ in range(STAGES):
+        for group in range(GROUPS_SENT):
+            if reduce.copies[group][0] < STAGES:
+                reduce.advance(group)
+    for j, (dst, start, count) in enumerate(
+            ((gwo_o, 0, 1), (gqkv_o, 1, 3), (gw2_o, 4, 9), (gw1_o, 13, 9))):
+        saves.append(local(total.at[pl.ds(start, count)], dst, osem.at[j + 1]))
+    for copy in saves:
+        copy.wait()
 
 
 def back(*args):
@@ -1714,26 +1768,28 @@
         ((3, C, C), BF), ((3, PAD, C), BF), ((C, PIX), BF), ((PIX, C), F32), ((C, C), BF),
         ((3, 8, 8, C), F32), ((2, 2, 64, C), BF), ((40, C), F32), ((PIX, C), BF),
         ((4, PIX, 128), BF), ((4, 16, 128), F32),
-        ((TAPS, 4, 2, 64, C), BF), ((TAPS, 4, 64, C), BF), ((3, TAPS, 64, C), BF),
-        ((TAPS, 64, C), BF), ((3, TAPS, 16, C), BF), ((TAPS, 2, 4, 16, C), BF),
+        ((TAPS, 4, 2, 64, C), BF), ((TAPS, 4, 64, C), BF), ((2, TAPS, 32, C), BF),
+        ((2, TAPS, 32, C), BF), ((TAPS, 32, C), BF), ((TAPS, 32, C), BF), ((TAPS, 64, C), BF),
+        ((2, TAPS, 16, C), BF), ((TAPS, 16, C), BF), ((TAPS, 2, 4, 16, C), BF),
     ]
     return pl.pallas_call(
         back_kernel,
         name="back",
         out_shape=[
-            jax.ShapeDtypeStruct((4, PIX, 128), F32),
+            jax.ShapeDtypeStruct((4, PIX, 128), BF),
             jax.ShapeDtypeStruct((4, 16, 128), F32),
-            jax.ShapeDtypeStruct((TAPS, 2, 4, 16, C), BF),
-            jax.ShapeDtypeStruct((2, 128, EMB), F32),
+            jax.ShapeDtypeStruct((9, 2, 4, 16, C), BF),
+            jax.ShapeDtypeStruct((9, 2, 4, 16, C), BF),
+            jax.ShapeDtypeStruct((3, 2, 4, 16, C), BF),
+            jax.ShapeDtypeStruct((1, 2, 4, 16, C), BF),
         ],
-        in_specs=[ANY, VMEM, VMEM] + [ANY] * 11 + [VMEM, VMEM],
-        out_specs=[VMEM, VMEM, ANY, VMEM],
+        in_specs=[ANY, VMEM, VMEM] + [ANY] * 11 + [VMEM],
+        out_specs=[ANY, VMEM, ANY, ANY, ANY, ANY],
         scratch_shapes=[pltpu.VMEM(*one) for one in shared]
         + [
-            DMA((3, 8)), DMA((3, 8)), DMA((2, 2)), DMA((2, 2)),
-            DMA((4,)), DMA((4,)), DMA((4,)), DMA((4,)), DMA((8,)), DMA((8,)), DMA((8, 4)),
-            DMA((8, 4)), DMA((8, 4)), DMA((8, 4)), DMA((8, 4)), DMA((8, 4)), DMA((8,)),
-            DMA((8,)), DMA((12,)), DMA((1,)),
+            DMA((3, 8)), DMA((3, 8)), DMA((2, 2)), DMA((2, 2)), DMA((4,)), DMA((4,)), DMA((4,)),
+            DMA((4,)), DMA((GROUPS_SENT, STAGES, 4)), DMA((GROUPS_SENT, STAGES, 4)), DMA((12,)),
+            DMA((5,)),
         ],
         compiler_params=pltpu.CompilerParams(
             collective_id=3, has_side_effects=True, vmem_limit_bytes=VMEM_LIMIT
@@ -1741,46 +1797,94 @@
     )(*args)
 
 
+def split_rows(rows):
+    first = rows.astype(BF).astype(F32)
+    second = (rows - first).astype(BF).astype(F32)
+    stacked = jnp.concatenate([first, second, rows - first - second, jnp.zeros((80, 128), F32)],
+                              axis=0)
+    left = jnp.transpose(stacked).astype(BF)
+    return left[:, 0:16], left[:, 16:32], left[:, 32:48]
+
+
+def finish_kernel(
+    res, gimg, gw1, gw2, gqkv, gwo, zs, ctot, feat, tokens,
+    res_o, gimg_o, gain_o, bias_o, gw1_o, gw2_o, cb_o, gemb_o, gembb_o, gqkv_o, qvb_o, gctx_o,
+    gctxb_o, gwo_o, ob_o,
+    res_v, gimg_v, gw1_v, gw2_v, gqkv_v, gwo_v, res_f, gimg_f, gw1_f, gw2_f, gqkv_f, gwo_f,
+    gemb_f, gctx_f, lsem, osem,
+):
+    pairs = (
+        (gw1, gw1_v, gw1_f, gw1_o), (gw2, gw2_v, gw2_f, gw2_o), (res, res_v, res_f, res_o),
+        (gimg, gimg_v, gimg_f, gimg_o), (gqkv, gqkv_v, gqkv_f, gqkv_o), (gwo, gwo_v, gwo_f, gwo_o))
+    loads = [local(src, low, lsem.at[j]) for j, (src, low, _, _) in enumerate(pairs)]
+    saves = []
+    for j in range(2):
+        rows = jnp.concatenate([zs[n, 11 + j : 12 + j, :] for n in range(4)]
+                               + [jnp.zeros((12, 128), F32)], axis=0)
+        gemb_f[j] = sum(mm(term, feat[...]) for term in split_rows(rows))
+        saves.append(local(gemb_f.at[j], gemb_o.at[j], osem.at[6 + j]))
+        gctx_f[j] = sum(mm(term, tokens[...]) for term in split_rows(ctot[j]))
+        saves.append(local(gctx_f.at[j], gctx_o.at[j], osem.at[8 + j]))
+        gctxb_o[j : j + 1, :] = as_row(ctot[j])
+    total = (zs[0] + zs[1]) + (zs[2] + zs[3])
+    gain_o[...] = total[0:3]
+    bias_o[...] = total[3:6]
+    cb_o[...] = total[6:8]
+    qvb_o[...] = total[8:10]
+    ob_o[...] = total[10:11]
+    gembb_o[...] = total[11:13]
+    for j, (_, low, high, dst) in enumerate(pairs):
+        loads[j].wait()
+
+        @pl.loop(0, high.shape[0])
+        def _(i):
+            high[i] = low[i].astype(F32)
+
+        saves.append(local(high, dst, osem.at[j]))
+    for copy in saves:
+        copy.wait()
+
+
+def finish(*args):
+    wide = [((4, PIX, 128), F32)] * 2 + [((9, 128, C), F32)] * 2 + [((3, 128, C), F32),
+                                                                    ((1, 128, C), F32)]
+    res, gimg, gw1, gw2, gqkv, gwo = wide
+    emb, ctx = ((2, 128, EMB), F32), ((2, 128, CTXW), F32)
+    outs = [
+        res, gimg, ((3, 128), F32), ((3, 128), F32), gw1, gw2, ((2, 128), F32), emb,
+        ((2, 128), F32), gqkv, ((2, 128), F32), ctx, ((2, 128), F32), gwo, ((1, 128), F32)]
+    return pl.pallas_call(
+        finish_kernel,
+        name="finish",
+        out_shape=[jax.ShapeDtypeStruct(*one) for one in outs],
+        in_specs=[ANY] * 6 + [VMEM] * 4,
+        out_specs=[VMEM if len(one[0]) == 2 else ANY for one in outs],
+        scratch_shapes=[pltpu.VMEM(shape, BF) for shape, _ in wide]
+        + [pltpu.VMEM(*one) for one in wide + [emb, ctx]] + [DMA((6,)), DMA((10,))],
+        compiler_params=pltpu.CompilerParams(vmem_limit_bytes=VMEM_LIMIT),
+    )(*args)
+
+
 def plane_body(
     image, target, time_index, loss_weight, clip_embed, clip_tokens, norm_gain, norm_bias,
     conv1_w, conv2_w, conv_bias, emb_w, emb_b, qkv_w, qv_bias, ctx_w, ctx_b, out_w, out_b,
 ):
-    z = lax.axis_index("row") // 2
-    feat = swish(time_features(time_index, EMB) + clip_embed.astype(F32)).astype(BF)
-    feat = jnp.pad(feat, ((0, 12), (0, 0)))
-    tokens = clip_tokens.reshape(4 * CTX, CTXW)
-    weight_row = jnp.broadcast_to(lax.dynamic_slice_in_dim(loss_weight, z, 1), (1, 128))
-    vec = jnp.concatenate([
-        norm_gain, norm_bias, conv_bias, qv_bias, out_b[None], jnp.zeros((2, 128), F32),
-        weight_row, jnp.zeros((2, 128), F32)])
-    (x, tgt, vec_all, st, a1, hid, a2, res, nrm, w1, w2, wq, wo, qkv, attn, p, ctx, pc, o,
-     linv) = front(
-        image.reshape(4, PIX, 128), target.reshape(4, PIX, 128), vec, feat, tokens, emb_w, emb_b,
-        ctx_w, ctx_b, conv1_w.reshape(9, 128, C), conv2_w.reshape(9, 128, C), qkv_w, out_w[None])
-    result, cot, gwo, gob, dt, grad_ctx_w, grad_ctx_b = middle(
-        attn, res, tgt, wo, vec_all, qkv, ctx, p, pc, o, linv, tokens)
-    gimg, zv, fin, grad_emb_w = back(
-        dt, vec_all, st, x, a1, hid, a2, res, nrm, cot, w1, w2, wq, gwo.reshape(4, 2, 64, C), gob,
-        feat)
-    sums = jnp.sum(zv, axis=0)
-    fin = fin.reshape(TAPS, 128, C).astype(F32)
-    return (
-        result.reshape(image.shape),
-        gimg.reshape(image.shape),
-        jnp.stack([sums[0], sums[2], sums[4]]),
-        jnp.stack([sums[1], sums[3], sums[5]]),
-        fin[13:22].reshape(3, 3, 128, C),
-        fin[4:13].reshape(3, 3, 128, C),
-        sums[6:8],
-        grad_emb_w,
-        sums[11:13],
-        fin[1:4],
-        sums[8:10],
-        grad_ctx_w,
-        grad_ctx_b,
-        fin[0],
-        sums[10],
-    )
+    (x, tgt, vec, st, a1, hid, a2, res, nrm, w1, w2, wq, wo, qkv, attn, p, ctx, pc, o, linv, feat,
+     tokens) = front(
+        image.reshape(4, PIX, 128), target.reshape(4, PIX, 128), time_index, loss_weight,
+        clip_embed, clip_tokens, norm_gain, norm_bias, conv_bias, qv_bias, out_b[None], emb_w,
+        emb_b, ctx_w, ctx_b, conv1_w.reshape(9, 128, C), conv2_w.reshape(9, 128, C), qkv_w,
+        out_w[None])
+    result, cot, gwo, gob, dt, ctot = middle(
+        attn, res, tgt, wo, vec, qkv, ctx, p, pc, o, linv)
+    gimg, zs, gw1, gw2, gqkv, gwo = back(
+        dt, vec, st, x, a1, hid, a2, res, nrm, cot, w1, w2, wq, gwo.reshape(4, 2, 64, C), gob)
+    taps = lambda value: value.reshape(value.shape[0], 128, C)
+    outs = finish(result, gimg, taps(gw1), taps(gw2), taps(gqkv), taps(gwo), zs, ctot, feat, tokens)
+    shapes = (
+        image, image, norm_gain, norm_bias, conv1_w, conv2_w, conv_bias, emb_w, emb_b, qkv_w,
+        qv_bias, ctx_w, ctx_b, out_w, out_b)
+    return tuple(out.reshape(like.shape) for out, like in zip(outs, shapes))
 
 
 def solution(mesh):

time: 324 us -> 283 us (0.87)
  local copies, waits for them, and re-layouts: 22.7 us -> 0 us
  Pallas kernels: 297 us -> 281 us
    pallas_call x1, Pallas kernels: 124 us -> 108 us  [back(): pl.pallas_call(back_kernel, name='back', out_shape=[jax.ShapeDtypeStruct(...]
    slice x4 -> x0, local copies, waits for them, and re-layouts: 8.73 us -> none  [the longest x1 4.55 us: plane_body(): fin[4:13].reshape(3, 3, 128, C)]
    pallas_call x0 -> x1, Pallas kernels: none -> 6.9 us  [finish(): pl.pallas_call(finish_kernel, name='finish', out_shape=[jax.ShapeDtypeStr...]
    unnamed x15 -> x0, local copies, waits for them, and re-layouts: 6.8 us -> none
    pallas_call x1, Pallas kernels: 62.9 us -> 57.8 us  [middle(): pl.pallas_call(middle_kernel, name='middle', out_shape=[jax.ShapeDtypeStr...]
where the time goes in v3:
time: 283 us; the launch traced here: 282 us
  Pallas kernels  281 us (99%)
    pallas_call x1, Pallas kernels, front(): pl.pallas_call(front_kernel, name='front', out_shape=[jax.ShapeDtypeStruc...  109 us
    pallas_call x1, Pallas kernels, back(): pl.pallas_call(back_kernel, name='back', out_shape=[jax.ShapeDtypeStruct(...  108 us
    pallas_call x1, Pallas kernels, middle(): pl.pallas_call(middle_kernel, name='middle', out_shape=[jax.ShapeDtypeStr...  57.8 us
    pallas_call x1, Pallas kernels, finish(): pl.pallas_call(finish_kernel, name='finish', out_shape=[jax.ShapeDtypeStr...  6.9 us

profile of v3, /device:TPU:7, one launch (start us, length us, event | category | flops | bytes accessed | tf_op | source)
XLA Modules:
  0.0 282.3 jit_solution(11500671387154633680)
XLA Ops:
  0.7 108.5 %front.1 = (bf16[512,512]{1,0:T(8,128)(2,1)}, bf16[512,512]{1,0:T(8,128)(2,1)}, f32[16,512]{1,0:T(8,128)}, f32[8,512]{1,0:T(8,128)}, bf16[3,640,512]{2,1,0:T(8,1...) custom-call(bf16[4,512,128]{2,1,0:T(8,128)(2,1)} %bitcast.21, ...), custom_call_target="tpu_custom_call" | custom-call | tf_op jit(solution)/shard_map/front/pallas_call | solution.py:1142
  109.2 57.8 %middle.1 = (bf16[4,512,128]{2,1,0:T(8,128)(2,1)}, f32[512,512]{1,0:T(8,128)}, bf16[512,512]{1,0:T(8,128)(2,1)}, f32[8,512]{1,0:T(8,128)}, bf16[3,512,512]{2,1,0:T(8,128)(2,1)}, /*index=5*/f32[2,16,128]{2,1,0:T(8,128)}) custom-call(bf16[512,512]{1,0:T(8,128)(2,1)} %get-tuple-element.64.attn, f32[512,512]{1,0:T(8,128)} %get-tuple-element.65.res, ...), custom_call_target="tpu_custom_call" | custom-call | tf_op jit(solution)/shard_map/middle/pallas_call | solution.py:1382
  167.0 108.3 %back.1 = (bf16[4,512,128]{2,1,0:T(8,128)(2,1)}, f32[4,16,128]{2,1,0:T(8,128)}, bf16[9,2,4,16,512]{4,3,2,1,0:T(8,128)(2,1)}, bf16[9,2,4,16,512]{4,3,2,1,0:T(8,12...) custom-call(bf16[3,512,512]{2,1,0:T(8,128)(2,1)} %get-tuple-element.76.dt, ...), custom_call_target="tpu_custom_call" | custom-call | tf_op jit(solution)/shard_map/back/pallas_call | solution.py:1775
  275.3 6.9 %finish.1 = (f32[4,512,128]{2,1,0:T(8,128)}, f32[4,512,128]{2,1,0:T(8,128)}, f32[3,128]{1,0:T(4,128)}, f32[3,128]{1,0:T(4,128)}, f32[9,128,512]{2,1,0:T(8,128)},...) custom-call(bf16[4,512,128]{2,1,0:T(8,128)(2,1)} %get-tuple-element., ...), custom_call_target="tpu_custom_call" | custom-call | tf_op jit(solution)/shard_map/finish/pallas_call | solution.py:1856

commit v4 on v3

--- a/solution.py
+++ b/solution.py
@@ -675,6 +675,97 @@
         acc[...] += mm(cat[col, pl.ds(start, PIX), :], weight[tap], dims)
 
 
+HALF_ROWS = 34 * 64
+SPREAD = (1, 2, 3, 0)
+
+
+def half_place(me):
+    return lax.div(me.pair, 2), lax.rem(me.band, 4)
+
+
+def spread_rows(me, src_of, dst, place_rows, ssem, rsem, steps):
+    core, place = half_place(me)
+    for step in steps:
+        chan = lax.rem(me.c + step, 4)
+        args = (src_of(chan), dst.at[place_rows(place), :])
+        if step == 0:
+
+            @pl.when(core == me.k)
+            def _():
+                local(*args, rsem.at[place])
+
+            @pl.when(core != me.k)
+            def _():
+                send(*args, ssem.at[step], rsem.at[place], (2 * me.z + core, chan))
+
+        else:
+            send(*args, ssem.at[step], rsem.at[place], (2 * me.z + core, chan))
+
+
+def spread_sent(me, src_of, dst, place_rows, ssem, rsem):
+    core, place = half_place(me)
+    for step in range(4):
+        chan = lax.rem(me.c + step, 4)
+
+        def done():
+            pltpu.make_async_remote_copy(
+                src_ref=src_of(chan), dst_ref=dst.at[place_rows(place), :],
+                send_sem=ssem.at[step], recv_sem=rsem.at[place],
+                device_id=(2 * me.z + core, chan), device_id_type=MESH_ID).wait_send()
+
+        if step == 0:
+            pl.when(core != me.k)(done)
+        else:
+            done()
+
+
+def spread_received(src_of, dst, place_rows, rsem):
+    for place in range(4):
+        pltpu.make_async_copy(src_of(0), dst.at[place_rows(place), :], rsem.at[place]).wait()
+
+
+def act_rows(place):
+    return pl.ds(pl.multiple_of(64 + place * PIX, 64), PIX)
+
+
+def grad_rows(place):
+    return pl.ds(place * PIX, PIX)
+
+
+def spread_edges(me, act, dst, ssem, rsem, finish=False):
+    for band, core, start, to in ((3, 1, 512, 0), (4, 0, 64, HALF_ROWS - 64)):
+
+        @pl.when(me.band == band)
+        def _():
+            piece, there = act.at[pl.ds(start, 64), :], dst.at[pl.ds(to, 64), :]
+            for step in range(4):
+                chan = lax.rem(me.c + step, 4)
+                if step == 0:
+                    if not finish:
+                        local(piece, there, rsem.at[0])
+                else:
+                    copy = pltpu.make_async_remote_copy(
+                        src_ref=piece, dst_ref=there, send_sem=ssem.at[step], recv_sem=rsem.at[0],
+                        device_id=(2 * me.z + core, chan), device_id_type=MESH_ID)
+                    if finish:
+                        copy.wait_send()
+                    else:
+                        copy.start()
+
+    if finish:
+        pltpu.make_async_copy(act.at[pl.ds(0, 64), :], dst.at[pl.ds(0, 64), :], rsem.at[0]).wait()
+    else:
+        empty = jnp.zeros((64, C), BF)
+
+        @pl.when(me.k == 0)
+        def _():
+            dst[0:64, :] = empty
+
+        @pl.when(me.k == 1)
+        def _():
+            dst[HALF_ROWS - 64 :, :] = empty
+
+
 LOG2E = 1.4426950408889634
 VROWS = 80
 SUB = 256
@@ -953,7 +1044,7 @@
     gather2.plane_done()
     conv_taps(res_v, a2_v, w2_v, (1,), False, NT)
     halo_wait(me, a2_v, halo.at[1], hs.at[1], hr.at[1])
-    save(6, a2_v, a2_o)
+    save(6, a2_v.at[1], a2_o)
     gather2.take()
     gather3.relay()
     conv_taps(res_v, a2_v, w2_v, (2 * odd,), False, NT)
@@ -1142,7 +1233,9 @@
     return pl.pallas_call(
         front_kernel,
         name="front",
-        out_shape=[jax.ShapeDtypeStruct(*one) for one in saved + more],
+        out_shape=[
+            jax.ShapeDtypeStruct(shape[1:] if j == 6 else shape, kind)
+            for j, (shape, kind) in enumerate(saved + more)],
         in_specs=[ANY, ANY] + [SMEM] * 2 + [VMEM] * 11 + [ANY] * 4,
         out_specs=[ANY] * (len(saved) + 1) + [VMEM] * 6,
         scratch_shapes=[pltpu.VMEM(*one) for one in saved]
@@ -1213,11 +1306,11 @@
 
 
 def middle_kernel(
-    attn, res, tgt, wo, vec, qkv, ctx, p, pc, o, linv,
-    out_o, cot_o, gwo_o, gob_o, dt_o, ctot_o,
+    attn, res, tgt, wo, vec, qkv, ctx, p, pc, o, linv, a2,
+    out_o, cot_o, gwo_o, gob_o, dt_o, ctot_o, act_o,
     attn_v, res_v, tgt_v, wo_v, out_b, back, cot_v, dat, dot_v, qkv_v, o_v,
-    vext, cvext, dos, dor, qrow, dq, pb, dkv, dqb, dt_v, dctx, cslots,
-    bs, br, ds_, dr, cs, cr, ks, kr, q_s, q_r, lsem, osem, psem,
+    vext, cvext, dos, dor, qrow, dq, pb, dkv, dqb, dt_v, dctx, cslots, act_v,
+    bs, br, ds_, dr, cs, cr, ks, kr, q_s, q_r, lsem, osem, psem, acts, actr, es, er,
 ):
     me = Place()
     scaling = HEAD ** (-0.5)
@@ -1260,6 +1353,41 @@
         copies.append(
             send(dat.at[head_rows(head), :], dot_v.at[:, band_cols(me.band)], ds_.at[step],
                  dr.at[step], me.head_device(head)))
+    piece = a2.at[pl.ds(64, PIX), :]
+    x = me.c + 1 - 2 * lax.rem(me.c, 2)
+    y = lax.rem(me.c + 2, 4)
+    far = lax.rem(x + 2, 4)
+    half, place = half_place(me)
+    owner = half == me.k
+    direct = [
+        send(piece, act_v.at[act_rows(place), :], acts.at[j], actr.at[place],
+             (2 * me.z + half, chan))
+        for j, chan in enumerate((x, y))
+    ]
+    core_copy = pltpu.make_async_remote_copy(
+        src_ref=piece, dst_ref=act_v.at[act_rows(place), :], send_sem=acts.at[2],
+        recv_sem=actr.at[place], device_id=(2 * me.z + half, me.c), device_id_type=MESH_ID)
+    pl.when(owner)(lambda: local(piece, act_v.at[act_rows(place), :], actr.at[place]) and None)
+    pl.when(jnp.logical_not(owner))(lambda: core_copy.start())
+
+    def places_of(chan):
+        first = lax.rem(2 * mixed(chan, me.z), 4)
+        return first, first + 1
+
+    def act_wait(where):
+        pltpu.make_async_copy(piece, act_v.at[act_rows(where), :], actr.at[where]).wait()
+
+    def part_copy(slot, where, part, chan):
+        rows = act_v.at[pl.ds(pl.multiple_of(64 + where * PIX + part * 256, 64), 256), :]
+        return pltpu.make_async_remote_copy(
+            src_ref=rows, dst_ref=rows, send_sem=acts.at[3 + slot],
+            recv_sem=actr.at[4 + 4 * part + where], device_id=(2 * me.z + me.k, chan),
+            device_id_type=MESH_ID)
+
+    given = places_of(jnp.where(owner, x, y))
+    given_part = jnp.where(owner, 0, 1)
+    given_chan = jnp.where(owner, y, x)
+    spread_edges(me, a2, act_v, es, er)
     saves = [local(cot_v, cot_o, osem.at[0])]
     lowf = low.astype(F32)
     gwo_o[...] = mm(jnp.transpose(lowf).astype(BF), rows).astype(BF)
@@ -1317,6 +1445,13 @@
             p_copy(lax.rem(block + 1, 8), 1 - slot).start()
 
         p_copy(block, slot).wait()
+
+        @pl.when(turn == 3)
+        def _():
+            for j, where in enumerate(given):
+                act_wait(where)
+                part_copy(j, where, given_part, given_chan).start()
+
         grads = []
         for sub in range(2):
             part = pl.ds(pl.multiple_of(block * PIX + sub * SUB, SUB), SUB)
@@ -1373,6 +1508,25 @@
             dqb.at[:, pl.ds(0, PIX)], dt_v.at[0, pl.ds(block * HEAD, HEAD), :], q_r.at[block]
         ).wait()
     saves.append(local(dt_v, dt_o, osem.at[1]))
+    spread_edges(me, a2, act_v, es, er, finish=True)
+    for copy in direct:
+        copy.wait_send()
+    pl.when(jnp.logical_not(owner))(lambda: core_copy.wait_send())
+    for j, where in enumerate(given):
+        part_copy(j, where, given_part, given_chan).wait_send()
+
+    @pl.when(owner)
+    def _():
+        for where in places_of(me.c):
+            act_wait(where)
+
+    @pl.when(jnp.logical_not(owner))
+    def _():
+        for where in places_of(far):
+            for part in range(2):
+                part_copy(0, where, part, x).wait_recv()
+
+    saves.append(local(act_v, act_o, osem.at[3]))
     for copy in saves:
         copy.wait()
 
@@ -1389,9 +1543,10 @@
             jax.ShapeDtypeStruct((8, C), F32),
             jax.ShapeDtypeStruct((3, C, PIX), BF),
             jax.ShapeDtypeStruct((2, 16, 128), F32),
+            jax.ShapeDtypeStruct((HALF_ROWS, C), BF),
         ],
-        in_specs=[ANY] * 4 + [VMEM, ANY, VMEM, ANY, VMEM, ANY, VMEM],
-        out_specs=[ANY, ANY, VMEM, VMEM, ANY, VMEM],
+        in_specs=[ANY] * 4 + [VMEM, ANY, VMEM, ANY, VMEM, ANY, VMEM, ANY],
+        out_specs=[ANY, ANY, VMEM, VMEM, ANY, VMEM, ANY],
         scratch_shapes=[
             pltpu.VMEM((C, PIX), BF), pltpu.VMEM((PIX, C), F32), pltpu.VMEM((PIX, C), BF),
             pltpu.VMEM((C, C), BF), pltpu.VMEM((PIX, C), BF), pltpu.VMEM((4, PIX, 128), BF),
@@ -1403,8 +1558,10 @@
             pltpu.VMEM((2, PIX, pixels), BF), pltpu.VMEM((8, 2, HEAD, PIX), BF),
             pltpu.VMEM((HEAD, pixels), BF), pltpu.VMEM((3, C, PIX), BF),
             pltpu.VMEM((2, 16, 128), F32), pltpu.VMEM((8, 2, 16, 128), F32),
+            pltpu.VMEM((HALF_ROWS, C), BF),
             DMA((4,)), DMA((4,)), DMA((8,)), DMA((8,)), DMA((8,)), DMA((8,)), DMA((8,)),
-            DMA((8,)), DMA((8,)), DMA((8,)), DMA((7,)), DMA((3,)), DMA((2,)),
+            DMA((8,)), DMA((8,)), DMA((8,)), DMA((7,)), DMA((4,)), DMA((2,)),
+            DMA((5,)), DMA((12,)), DMA((4,)), DMA((1,)),
         ],
         compiler_params=pltpu.CompilerParams(
             collective_id=2, has_side_effects=True, vmem_limit_bytes=VMEM_LIMIT
@@ -1413,16 +1570,24 @@
 
 
 TAPS = 22
-GROUP_TAPS = ((0, 1), (1, 3), (4, 3), (7, 3), (10, 3), (13, 3), (16, 3), (19, 2), (21, 1))
+WHOLE = 13
+GROUP_TAPS = ((0, 1), (1, 3), (13, 3), (16, 3), (19, 3), (4, 3), (7, 3), (10, 3))
 GROUPS_SENT = len(GROUP_TAPS)
 STAGES = 9
 
 
+def only(condition, action):
+    if condition is None:
+        action()
+    else:
+        pl.when(condition)(lambda: action() and None)
+
+
 class Reduce:
-    def __init__(self, me, part, bufs, total, sems):
-        self.me, self.part, self.total = me, part, total
-        (self.from_core, self.near_x, self.near_y, self.last_x, self.last_y, self.plane,
-         self.plane_two, self.plane_one) = bufs
+    def __init__(self, me, part, quarter, bufs, total, sems):
+        self.me, self.part, self.quarter, self.total = me, part, quarter, total
+        (self.from_core, self.quarter_core, self.near_x, self.near_y, self.last_x, self.last_y, self.plane,
+         self.plane_in, self.half_in) = bufs
         self.s, self.r = sems
         odd = lax.rem(me.z, 2)
         self.x = me.c + 1 - 2 * lax.rem(me.c, 2)
@@ -1430,8 +1595,9 @@
         self.far = lax.rem(self.x + 2, 4)
         self.core = (me.r + 1 - 2 * me.k, me.c)
         self.z1 = me.z + 1 - 2 * odd
-        self.z2 = lax.rem(me.z + 2, 4)
-        self.z3 = lax.rem(self.z1 + 2, 4)
+        self.inner = jnp.logical_or(me.z == 1, me.z == 2)
+        self.outer = jnp.logical_not(self.inner)
+        self.half = lax.rem(me.z + 1, 2)
         self.copies = {}
 
     def plane_device(self, z):
@@ -1439,18 +1605,25 @@
 
     def advance(self, group):
         stage, waiting = self.copies.get(group, (0, []))
-        for copy in waiting:
-            copy.wait()
+        for copy, sends, takes in waiting:
+            only(sends, copy.wait_send)
+            only(takes, copy.wait_recv)
         start, count = GROUP_TAPS[group]
-        step = (self.core_send, self.first_send, self.second_send, self.halve_send,
-                self.quarter_send, self.quarter_back, self.half_back, self.core_back,
-                lambda *_: [])[stage]
+        first = ((self.core_send, self.first_send, self.second_send, self.inward)
+                 if start < WHOLE else (self.conv_core_send, self.conv_inward))
+        step = (first + (self.half_send, self.half_back, self.outward, self.core_back,
+                         lambda *_: []))[stage]
         taps = pl.ds(start, count)
+        self.conv = pl.ds(start - WHOLE, count)
         moves = step(taps, lambda body: pl.loop(start, start + count)(body))
-        copies = [
-            send(src, dst, self.s.at[group, stage, j], self.r.at[group, stage, j], device)
-            for j, (src, dst, device) in enumerate(moves)
-        ]
+        copies = []
+        for j, (src, dst, device, *when) in enumerate(moves):
+            copy = pltpu.make_async_remote_copy(
+                src_ref=src, dst_ref=dst, send_sem=self.s.at[group, stage, j],
+                recv_sem=self.r.at[group, stage, j], device_id=device, device_id_type=MESH_ID)
+            sends, takes = when if when else (None, None)
+            only(sends, copy.start)
+            copies.append((copy, sends, takes))
         self.copies[group] = (stage + 1, copies)
 
     def core_send(self, taps, each):
@@ -1473,6 +1646,18 @@
             (part.at[taps, self.y, me.k, high, :], self.near_y.at[0, taps], y),
         ]
 
+    def conv_core_send(self, taps, each):
+        return [(self.quarter.at[self.conv, 1 - self.me.k], self.quarter_core.at[self.conv], self.core)]
+
+    def conv_inward(self, taps, each):
+        @each
+        def _(tap):
+            value = (self.quarter[tap - WHOLE, self.me.k].astype(F32)
+                     + self.quarter_core[tap - WHOLE].astype(F32))
+            self.plane[tap] = value.astype(BF)
+
+        return self.to_inner(taps)
+
     def second_send(self, taps, each):
         me, part = self.me, self.part
         low, high = pl.ds(0, 32), pl.ds(32, 32)
@@ -1488,10 +1673,7 @@
             (part.at[taps, self.x, me.k, high, :], self.last_x.at[taps], (me.r, self.x)),
         ]
 
-    def rows(self, z):
-        return pl.ds(pl.multiple_of(z * 16, 16), 16)
-
-    def halve_send(self, taps, each):
+    def inward(self, taps, each):
         me, part = self.me, self.part
 
         @each
@@ -1502,39 +1684,43 @@
                          + last[tap].astype(F32))
                 self.plane[tap, rows, :] = value.astype(BF)
 
-        device = self.plane_device(self.z1)
-        return [
-            (self.plane.at[taps, self.rows(self.z1), :], self.plane_two.at[0, taps], device),
-            (self.plane.at[taps, self.rows(self.z3), :], self.plane_two.at[1, taps], device),
-        ]
-
-    def quarter_send(self, taps, each):
-        @each
-        def _(tap):
-            for j, z in enumerate((self.me.z, self.z2)):
-                value = (self.plane[tap, self.rows(z), :].astype(F32)
-                         + self.plane_two[j, tap].astype(F32))
-                self.plane[tap, self.rows(z), :] = value.astype(BF)
-
-        return [(self.plane.at[taps, self.rows(self.z2), :], self.plane_one.at[taps],
-                 self.plane_device(self.z2))]
-
-    def quarter_back(self, taps, each):
+        return self.to_inner(taps)
+
+    def to_inner(self, taps):
+        return [(self.plane.at[taps], self.plane_in.at[taps], self.plane_device(self.z1),
+                 self.outer, self.inner)]
+
+    def half_rows(self, half):
+        return pl.ds(pl.multiple_of(half * 32, 32), 32)
+
+    def half_send(self, taps, each):
+        @pl.when(self.inner)
+        def _():
+            @each
+            def _(tap):
+                value = self.plane[tap].astype(F32) + self.plane_in[tap].astype(F32)
+                self.plane[tap] = value.astype(BF)
+
+        return [(self.plane.at[taps, self.half_rows(1 - self.half), :], self.half_in.at[taps],
+                 self.plane_device(3 - self.me.z), self.inner, self.inner)]
+
+    def half_back(self, taps, each):
         me = self.me
 
-        @each
-        def _(tap):
-            value = (self.plane[tap, self.rows(me.z), :].astype(F32)
-                     + self.plane_one[tap].astype(F32))
-            self.total[tap, me.k, me.z] = value.astype(BF)
-
-        piece = self.total.at[taps, me.k, me.z]
-        return [(piece, piece, self.plane_device(self.z2))]
-
-    def half_back(self, taps, each):
-        device = self.plane_device(self.z1)
-        pieces = [self.total.at[taps, self.me.k, z] for z in (self.me.z, self.z2)]
-        return [(piece, piece, device) for piece in pieces]
+        @pl.when(self.inner)
+        def _():
+            @each
+            def _(tap):
+                value = (self.plane[tap, self.half_rows(self.half), :].astype(F32)
+                         + self.half_in[tap].astype(F32))
+                self.total[tap, me.k, self.half] = value.astype(BF)
+
+        piece = self.total.at[taps, me.k, self.half]
+        return [(piece, piece, self.plane_device(3 - me.z), self.inner, self.inner)]
+
+    def outward(self, taps, each):
+        piece = self.total.at[taps, self.me.k]
+        return [(piece, piece, self.plane_device(self.z1), self.inner, self.outer)]
 
     def core_back(self, taps, each):
         piece = self.total.at[taps, self.me.k]
@@ -1542,12 +1728,12 @@
 
 
 def back_kernel(
-    dt, vec, st, x, a1, hid, a2, res, nrm, cot, w1, w2, wq, gwo, gob,
+    dt, vec, st, x, a1, hid, act2, res, nrm, cot, w1, w2, wq, gwo, gob,
     gimg_o, zs_o, gw1_o, gw2_o, gqkv_o, gwo_o,
-    dt_v, x_v, a1_v, hid_v, a2_v, res_v, nrm_v, drs_v, w1_v, w2_v, wq_v,
-    cat, turned, acc, groups, slots, halo, keep, img_b, back, zsl,
-    part, from_core, near_x, near_y, last_x, last_y, plane, plane_two, plane_one, total,
-    ss, sr, hs, hr, bs, br, zs, zr, red_s, red_r, lsem, osem,
+    dt_v, x_v, a1_v, hid_v, act2_v, res_v, nrm_v, drs_v, w1_v, w2_v, wq_v,
+    cat, turned, turned1, acc, groups, slots, halo, keep, img_b, back, zsl, dquart,
+    part, quarter, from_core, quarter_core, near_x, near_y, last_x, last_y, plane, plane_in, half_in, total,
+    ss, sr, hs, hr, bs, br, zs, zr, red_s, red_r, lsem, osem, ds_, dr,
 ):
     me = Place()
     barrier = pltpu.get_barrier_semaphore()
@@ -1560,10 +1746,10 @@
         )
     loads = [local(a, b, lsem.at[j]) for j, (a, b) in enumerate((
         (dt, dt_v), (wq, wq_v), (res, res_v), (gwo, part.at[0]), (nrm, nrm_v), (cot, drs_v),
-        (a2, a2_v), (w2, w2_v), (hid, hid_v), (a1, a1_v), (w1, w1_v), (x, x_v)))]
+        (act2, act2_v), (w2, w2_v), (hid, hid_v), (a1, a1_v), (w1, w1_v), (x, x_v)))]
     reduce = Reduce(
-        me, part, (from_core, near_x, near_y, last_x, last_y, plane, plane_two, plane_one), total,
-        (red_s, red_r))
+        me, part, quarter, (from_core, quarter_core, near_x, near_y, last_x, last_y, plane, plane_in,
+                            half_in), total, (red_s, red_r))
 
     def advance(*groups):
         for group in groups:
@@ -1636,33 +1822,46 @@
         return carry + fold(value.astype(BF).astype(F32))
 
     keep[3:4, :] = as_row(lax.fori_loop(0, CHUNKS, resid_grad, zero8))
-    halo_send(me, cat, halo.at[0], hs.at[0], hr.at[0])
-    advance(0, 1)
-    turned[...] = jnp.transpose(drs_v[...]).astype(BF)
-
-    def weight_grads(group, source, first):
+    def grad_of(chan):
+        return cat.at[1, pl.ds(64, PIX), pl.ds(pl.multiple_of(chan * 128, 128), 128)]
+
+    grads_sems = (ds_, dr)
+
+    def half_weight_grads(act, groups_of):
+        spread_received(grad_of, dquart, grad_rows, dr)
+        value = dquart[...].astype(F32)
+        col = lax.rem(lax.broadcasted_iota(jnp.int32, (4 * PIX, 128), 0), 64)
+        moved = (jnp.where(col == 63, 0.0, pltpu.roll(value, 4 * PIX - 1, 0)), value,
+                 jnp.where(col == 0, 0.0, pltpu.roll(value, 1, 0)))
+        for j in range(3):
+            turned[j * 128 : (j + 1) * 128, :] = jnp.transpose(moved[j]).astype(BF)
+        for row, group in enumerate(groups_of):
+            start = GROUP_TAPS[group][0]
+            taps = mm(turned[...], act[row * 64 : row * 64 + 4 * PIX, :])
+            for j in range(3):
+                quarter[start - WHOLE + j] = taps[j * 128 : (j + 1) * 128].astype(BF).reshape(
+                    2, 64, C)
+            advance(group)
+
+    def weight_grads(group, source):
         start, count = GROUP_TAPS[group]
 
         @pl.loop(0, count)
         def _(i):
-            tap = start - first + i
+            tap = start - 4 + i
             rows = pl.ds(pl.multiple_of(lax.div(tap, 3) * 64, 64), PIX)
-            part[start + i] = mm(turned[...], source[lax.rem(tap, 3), rows, :]).astype(
+            part[start + i] = mm(turned1[...], source[lax.rem(tap, 3), rows, :]).astype(
                 BF).reshape(4, 2, 64, C)
 
         advance(group)
 
-    loads[6].wait()
-    for group in (2, 3, 4):
-        weight_grads(group, a2_v, 4)
-    advance(0)
+    halo_send(me, cat, halo.at[0], hs.at[0], hr.at[0])
+    spread_rows(me, grad_of, dquart, grad_rows, *grads_sems, SPREAD)
     acc[...] = jnp.zeros((PIX, C), F32)
     loads[7].wait()
     conv_taps(acc, cat, w2_v, (1,), True, NN)
     halo_wait(me, cat, halo.at[0], hs.at[0], hr.at[0])
-    advance(2)
     conv_taps(acc, cat, w2_v, (0, 2), True, NN)
-    advance(1)
     loads[8].wait()
     gain2, bias2 = vec[1:2, :], vec[4:5, :]
     scale, shift = 1.0 + vec[11:12, :], vec[12:13, :]
@@ -1675,7 +1874,10 @@
         return value
 
     copies = exchange(1, sums(scaled2, mod_grad))
-    advance(0, 2)
+    advance(0, 1)
+    loads[6].wait()
+    half_weight_grads(act2_v, (2, 3, 4))
+    spread_sent(me, grad_of, dquart, grad_rows, *grads_sems)
     for copy in copies:
         copy.wait()
     total2 = slots_total(slots.at[1])
@@ -1693,17 +1895,16 @@
 
     keep[1:2, :] = as_row(lax.fori_loop(0, CHUNKS, hidden_grad, zero8))
     halo_send(me, cat, halo.at[1], hs.at[1], hr.at[1])
-    advance(3, 1)
-    turned[...] = jnp.transpose(acc[...]).astype(BF)
+    advance(2, 3, 4)
+    turned1[...] = jnp.transpose(acc[...]).astype(BF)
     loads[9].wait()
-    for group in (5, 6, 7, 8):
-        weight_grads(group, a1_v, 13)
-    advance(0, 2)
+    for group in (5, 6, 7):
+        weight_grads(group, a1_v)
+    advance(0, 1, 5)
     acc[...] = jnp.zeros((PIX, C), F32)
     loads[10].wait()
     conv_taps(acc, cat, w1_v, (1,), True, NN)
     halo_wait(me, cat, halo.at[1], hs.at[1], hr.at[1])
-    advance(1, 3)
     conv_taps(acc, cat, w1_v, (0, 2), True, NN)
     loads[11].wait()
     gain1, bias1 = vec[0:1, :], vec[3:4, :]
@@ -1717,7 +1918,7 @@
     first, cross = sums(scaled1, pre_grad)
     copies = exchange(2, [first, cross, keep[1:2, :], keep[3:4, :], keep[0:1, :], keep[2:3, :],
                           gob[0:1, :]])
-    advance(4, 0, 2, 3, 1)
+    advance(6, 2, 3, 4)
     for copy in copies:
         copy.wait()
     total1 = slots_total(slots.at[2])
@@ -1743,19 +1944,19 @@
              (2 * lax.rem(me.z + t, 4) + me.k, me.c))
         for t in range(1, 4)
     ]
-    advance(4, 5, 2, 3, 1, 0, 6, 4, 5, 2, 3, 7, 1, 6, 4, 5, 8)
+    advance(7, 5, 6, 0, 1, 2, 3, 4, 7, 5, 6, 2, 3, 4, 0, 1, 7, 5, 6, 2, 3, 4, 0, 1, 7, 5, 6)
     for copy in zcopies:
         copy.wait()
     zs_o[...] = zsl[...]
-    advance(7, 3, 4, 6, 5, 8, 7)
+    advance(0, 1, 7, 5, 6, 7, 0, 1, 5, 6, 7)
     band_back_wait(me, img_b, back, bs, br)
     saves = [local(back, gimg_o, osem.at[0])]
     for _ in range(STAGES):
         for group in range(GROUPS_SENT):
-            if reduce.copies[group][0] < STAGES:
+            if reduce.copies[group][0] < (STAGES - 2 if 2 <= group < 5 else STAGES):
                 reduce.advance(group)
     for j, (dst, start, count) in enumerate(
-            ((gwo_o, 0, 1), (gqkv_o, 1, 3), (gw2_o, 4, 9), (gw1_o, 13, 9))):
+            ((gwo_o, 0, 1), (gqkv_o, 1, 3), (gw2_o, 13, 9), (gw1_o, 4, 9))):
         saves.append(local(total.at[pl.ds(start, count)], dst, osem.at[j + 1]))
     for copy in saves:
         copy.wait()
@@ -1763,14 +1964,15 @@
 
 def back(*args):
     shared = [
-        ((3, C, PIX), BF), ((PIX, C), BF), ((3, PAD, C), BF), ((PIX, C), F32), ((3, PAD, C), BF),
-        ((PIX, C), F32), ((PIX, C), BF), ((PIX, C), F32), ((9, C, C), BF), ((9, C, C), BF),
-        ((3, C, C), BF), ((3, PAD, C), BF), ((C, PIX), BF), ((PIX, C), F32), ((C, C), BF),
-        ((3, 8, 8, C), F32), ((2, 2, 64, C), BF), ((40, C), F32), ((PIX, C), BF),
-        ((4, PIX, 128), BF), ((4, 16, 128), F32),
-        ((TAPS, 4, 2, 64, C), BF), ((TAPS, 4, 64, C), BF), ((2, TAPS, 32, C), BF),
-        ((2, TAPS, 32, C), BF), ((TAPS, 32, C), BF), ((TAPS, 32, C), BF), ((TAPS, 64, C), BF),
-        ((2, TAPS, 16, C), BF), ((TAPS, 16, C), BF), ((TAPS, 2, 4, 16, C), BF),
+        ((3, C, PIX), BF), ((PIX, C), BF), ((3, PAD, C), BF), ((PIX, C), F32),
+        ((HALF_ROWS, C), BF), ((PIX, C), F32), ((PIX, C), BF), ((PIX, C), F32), ((9, C, C), BF),
+        ((9, C, C), BF), ((3, C, C), BF), ((3, PAD, C), BF), ((384, 4 * PIX), BF), ((C, PIX), BF), ((PIX, C), F32),
+        ((C, C), BF), ((3, 8, 8, C), F32), ((2, 2, 64, C), BF), ((40, C), F32), ((PIX, C), BF),
+        ((4, PIX, 128), BF), ((4, 16, 128), F32), ((4 * PIX, 128), BF),
+        ((WHOLE, 4, 2, 64, C), BF), ((TAPS - WHOLE, 2, 64, C), BF), ((WHOLE, 4, 64, C), BF),
+        ((TAPS - WHOLE, 64, C), BF), ((2, WHOLE, 32, C), BF), ((2, WHOLE, 32, C), BF),
+        ((WHOLE, 32, C), BF), ((WHOLE, 32, C), BF), ((TAPS, 64, C), BF), ((TAPS, 64, C), BF),
+        ((TAPS, 32, C), BF), ((TAPS, 2, 2, 32, C), BF),
     ]
     return pl.pallas_call(
         back_kernel,
@@ -1778,10 +1980,10 @@
         out_shape=[
             jax.ShapeDtypeStruct((4, PIX, 128), BF),
             jax.ShapeDtypeStruct((4, 16, 128), F32),
-            jax.ShapeDtypeStruct((9, 2, 4, 16, C), BF),
-            jax.ShapeDtypeStruct((9, 2, 4, 16, C), BF),
-            jax.ShapeDtypeStruct((3, 2, 4, 16, C), BF),
-            jax.ShapeDtypeStruct((1, 2, 4, 16, C), BF),
+            jax.ShapeDtypeStruct((9, 2, 2, 32, C), BF),
+            jax.ShapeDtypeStruct((9, 2, 2, 32, C), BF),
+            jax.ShapeDtypeStruct((3, 2, 2, 32, C), BF),
+            jax.ShapeDtypeStruct((1, 2, 2, 32, C), BF),
         ],
         in_specs=[ANY, VMEM, VMEM] + [ANY] * 11 + [VMEM],
         out_specs=[ANY, VMEM, ANY, ANY, ANY, ANY],
@@ -1789,7 +1991,7 @@
         + [
             DMA((3, 8)), DMA((3, 8)), DMA((2, 2)), DMA((2, 2)), DMA((4,)), DMA((4,)), DMA((4,)),
             DMA((4,)), DMA((GROUPS_SENT, STAGES, 4)), DMA((GROUPS_SENT, STAGES, 4)), DMA((12,)),
-            DMA((5,)),
+            DMA((5,)), DMA((4,)), DMA((4,)),
         ],
         compiler_params=pltpu.CompilerParams(
             collective_id=3, has_side_effects=True, vmem_limit_bytes=VMEM_LIMIT
@@ -1875,10 +2077,10 @@
         clip_embed, clip_tokens, norm_gain, norm_bias, conv_bias, qv_bias, out_b[None], emb_w,
         emb_b, ctx_w, ctx_b, conv1_w.reshape(9, 128, C), conv2_w.reshape(9, 128, C), qkv_w,
         out_w[None])
-    result, cot, gwo, gob, dt, ctot = middle(
-        attn, res, tgt, wo, vec, qkv, ctx, p, pc, o, linv)
+    result, cot, gwo, gob, dt, ctot, act2 = middle(
+        attn, res, tgt, wo, vec, qkv, ctx, p, pc, o, linv, a2)
     gimg, zs, gw1, gw2, gqkv, gwo = back(
-        dt, vec, st, x, a1, hid, a2, res, nrm, cot, w1, w2, wq, gwo.reshape(4, 2, 64, C), gob)
+        dt, vec, st, x, a1, hid, act2, res, nrm, cot, w1, w2, wq, gwo.reshape(4, 2, 64, C), gob)
     taps = lambda value: value.reshape(value.shape[0], 128, C)
     outs = finish(result, gimg, taps(gw1), taps(gw2), taps(gqkv), taps(gwo), zs, ctot, feat, tokens)
     shapes = (

time: 283 us -> 280 us (0.989)
    pallas_call x1, Pallas kernels: 108 us -> 101 us  [back(): pl.pallas_call(back_kernel, name='back', out_shape=[jax.ShapeDtypeStruct(...]
    pallas_call x1, Pallas kernels: 57.8 us -> 62.3 us  [middle(): pl.pallas_call(middle_kernel, name='middle', out_shape=[jax.ShapeDtypeStr...]
where the time goes in v4:
time: 280 us
  Pallas kernels  279 us (100%)
    pallas_call x1, Pallas kernels, front(): pl.pallas_call(front_kernel, name='front', out_shape=[jax.ShapeDtypeStruc...  109 us
    pallas_call x1, Pallas kernels, back(): pl.pallas_call(back_kernel, name='back', out_shape=[jax.ShapeDtypeStruct(...  101 us
    pallas_call x1, Pallas kernels, middle(): pl.pallas_call(middle_kernel, name='middle', out_shape=[jax.ShapeDtypeStr...  62.3 us
    pallas_call x1, Pallas kernels, finish(): pl.pallas_call(finish_kernel, name='finish', out_shape=[jax.ShapeDtypeStr...  6.9 us

profile of v4, /device:TPU:7, one launch (start us, length us, event | category | flops | bytes accessed | tf_op | source)
XLA Modules:
  0.0 279.8 jit_solution(5198124436503093510)
XLA Ops:
  0.7 108.5 %front.1 = (bf16[512,512]{1,0:T(8,128)(2,1)}, bf16[512,512]{1,0:T(8,128)(2,1)}, f32[16,512]{1,0:T(8,128)}, f32[8,512]{1,0:T(8,128)}, bf16[3,640,512]{2,1,0:T(8,1...) custom-call(bf16[4,512,128]{2,1,0:T(8,128)(2,1)} %bitcast.21, ...), custom_call_target="tpu_custom_call" | custom-call | tf_op jit(solution)/shard_map/front/pallas_call | solution.py:1233
  109.2 62.3 %middle.1 = (bf16[4,512,128]{2,1,0:T(8,128)(2,1)}, f32[512,512]{1,0:T(8,128)}, bf16[512,512]{1,0:T(8,128)(2,1)}, f32[8,512]{1,0:T(8,128)}, bf16[3,512,512]{2,1,0...) custom-call(bf16[512,512]{1,0:T(8,128)(2,1)} %get-tuple-element.65.attn, ...), custom_call_target="tpu_custom_call" | custom-call | tf_op jit(solution)/shard_map/middle/pallas_call | solution.py:1536
  171.5 101.2 %back.1 = (bf16[4,512,128]{2,1,0:T(8,128)(2,1)}, f32[4,16,128]{2,1,0:T(8,128)}, bf16[9,2,2,32,512]{4,3,2,1,0:T(8,128)(2,1)}, bf16[9,2,2,32,512]{4,3,2,1,0:T(8,12...) custom-call(bf16[3,512,512]{2,1,0:T(8,128)(2,1)} %get-tuple-element.78.dt, ...), custom_call_target="tpu_custom_call" | custom-call | tf_op jit(solution)/shard_map/back/pallas_call | solution.py:1977
  272.7 6.9 %finish.1 = (f32[4,512,128]{2,1,0:T(8,128)}, f32[4,512,128]{2,1,0:T(8,128)}, f32[3,128]{1,0:T(4,128)}, f32[3,128]{1,0:T(4,128)}, f32[9,128,512]{2,1,0:T(8,128)},...) custom-call(bf16[4,512,128]{2,1,0:T(8,128)(2,1)} %get-tuple-element., ...), custom_call_target="tpu_custom_call" | custom-call | tf_op jit(solution)/shard_map/finish/pallas_call | solution.py:2058

commit v5 on v4

--- a/solution.py
+++ b/solution.py
@@ -769,7 +769,7 @@
 LOG2E = 1.4426950408889634
 VROWS = 80
 SUB = 256
-KEYS = 512
+KEYS = 256
 
 
 def image_targets(me):

time: 280 us -> 280 us (level)
  no operation moved by 1% of the time
where the time goes in v5:
time: 280 us; the launch traced here: 279 us
  Pallas kernels  278 us (99%)
    pallas_call x1, Pallas kernels, front(): pl.pallas_call(front_kernel, name='front', out_shape=[jax.ShapeDtypeStruc...  108 us
    pallas_call x1, Pallas kernels, back(): pl.pallas_call(back_kernel, name='back', out_shape=[jax.ShapeDtypeStruct(...  101 us
    pallas_call x1, Pallas kernels, middle(): pl.pallas_call(middle_kernel, name='middle', out_shape=[jax.ShapeDtypeStr...  62.2 us
    pallas_call x1, Pallas kernels, finish(): pl.pallas_call(finish_kernel, name='finish', out_shape=[jax.ShapeDtypeStr...  6.9 us

profile of v5, /device:TPU:7, one launch (start us, length us, event | category | flops | bytes accessed | tf_op | source)
XLA Modules:
  0.0 279.1 jit_solution(6986480742886537538)
XLA Ops:
  0.7 107.8 %front.1 = (bf16[512,512]{1,0:T(8,128)(2,1)}, bf16[512,512]{1,0:T(8,128)(2,1)}, f32[16,512]{1,0:T(8,128)}, f32[8,512]{1,0:T(8,128)}, bf16[3,640,512]{2,1,0:T(8,1...) custom-call(bf16[4,512,128]{2,1,0:T(8,128)(2,1)} %bitcast.21, ...), custom_call_target="tpu_custom_call" | custom-call | tf_op jit(solution)/shard_map/front/pallas_call | solution.py:1233
  108.5 62.2 %middle.1 = (bf16[4,512,128]{2,1,0:T(8,128)(2,1)}, f32[512,512]{1,0:T(8,128)}, bf16[512,512]{1,0:T(8,128)(2,1)}, f32[8,512]{1,0:T(8,128)}, bf16[3,512,512]{2,1,0...) custom-call(bf16[512,512]{1,0:T(8,128)(2,1)} %get-tuple-element.65.attn, ...), custom_call_target="tpu_custom_call" | custom-call | tf_op jit(solution)/shard_map/middle/pallas_call | solution.py:1536
  170.6 101.4 %back.1 = (bf16[4,512,128]{2,1,0:T(8,128)(2,1)}, f32[4,16,128]{2,1,0:T(8,128)}, bf16[9,2,2,32,512]{4,3,2,1,0:T(8,128)(2,1)}, bf16[9,2,2,32,512]{4,3,2,1,0:T(8,12...) custom-call(bf16[3,512,512]{2,1,0:T(8,128)(2,1)} %get-tuple-element.78.dt, ...), custom_call_target="tpu_custom_call" | custom-call | tf_op jit(solution)/shard_map/back/pallas_call | solution.py:1977
  272.0 6.9 %finish.1 = (f32[4,512,128]{2,1,0:T(8,128)}, f32[4,512,128]{2,1,0:T(8,128)}, f32[3,128]{1,0:T(4,128)}, f32[3,128]{1,0:T(4,128)}, f32[9,128,512]{2,1,0:T(8,128)},...) custom-call(bf16[4,512,128]{2,1,0:T(8,128)(2,1)} %get-tuple-element., ...), custom_call_target="tpu_custom_call" | custom-call | tf_op jit(solution)/shard_map/finish/pallas_call | solution.py:2058
